TPU v7x, 32 devices: a whole 2x2x4 slice. The times are simulated.
32 devices in a mesh: req: 2 (over x), exp: 16 (over z, y, core).
Axes of the slice: x: 2, y: 2, z: 4, core: 2. Of those that a mesh axis runs over, the one named last changes fastest.
Arguments:
- attn_out: bfloat16 [4096, 2048], P(('req', 'exp')), may hold values from -6 to 6
- residual: bfloat16 [4096, 2048], P(('req', 'exp')), may hold values from -6 to 6
- out_weight: bfloat16 [2048, 2048], P('exp'), may hold values from -0.125 to 0.125
- norm_gain: float32 [2048], replicated, may hold values from 0.25 to 1.75
- expert_ids: int32 [4096, 6], P(('req', 'exp')), may hold values from 0 to 15, all different within a row; in each aligned block of 128 rows (0 to 127, 128 to 255, ...) at most 72 rows name the same one
- gate_weights: float32 [4096, 6], P(('req', 'exp')), may hold values from 0.05 to 0.5
- expert_gate: bfloat16 [16, 2048, 1408], P('exp'), may hold values from -0.125 to 0.125
- expert_up: bfloat16 [16, 2048, 1408], P('exp'), may hold values from -0.125 to 0.125
- expert_down: bfloat16 [16, 1408, 2048], P('exp'), may hold values from -0.15625 to 0.15625
- shared_gate: bfloat16 [2048, 1408], P(None, 'req'), may hold values from -0.125 to 0.125
- shared_up: bfloat16 [2048, 1408], P(None, 'req'), may hold values from -0.125 to 0.125
- shared_down: bfloat16 [2048, 1408], P(None, 'req'), may hold values from -0.15625 to 0.15625
Outputs:
- mixed: bfloat16 [4096, 2048], P(('req', 'exp'))
Inputs may be any that keep to these rules, and one draw needn't show every extreme that they name: `expert_ids`: within the rows of one device no expert is named by more than 72 rows, and each row names 6 different experts.
All inputs are finite; a program needn't handle non-finite values.
Results may differ from a plain program's by a relative error of at most 0.012.
Values may be sent and summed in bfloat16 or wider, within the bound.
No kernel may reach another device: no remote copies, remote signals or barrier semaphores. Data moves between devices by JAX's collectives and lax.ppermute only.
A program may use at most 192 MiB of HBM per device.

v0:
```python
import functools

import jax
import jax.numpy as jnp
from jax import lax
from jax.experimental import pallas as pl
from jax.experimental.pallas import tpu as pltpu
from jax.sharding import PartitionSpec as P

F32 = jnp.float32
BF16 = jnp.bfloat16
VMEM_BYTES = 12 * 1024 * 1024
TILE = 512
TABLE_ROWS = 16


def ring_order(chips):
    slow = 4
    fast = chips // slow
    order = [a * fast for a in range(slow)]
    for turn, a in enumerate(reversed(range(slow))):
        inner = range(1, fast) if turn % 2 == 0 else range(fast - 1, 0, -1)
        order += [a * fast + b for b in inner]
    return order


def mm(a, b):
    return jnp.dot(a, b, preferred_element_type=F32)


def vmem():
    return pl.BlockSpec(memory_space=pltpu.VMEM)


def smem():
    return pl.BlockSpec(memory_space=pltpu.SMEM)


def hbm():
    return pl.BlockSpec(memory_space=pl.ANY)


def params():
    return pltpu.CompilerParams(vmem_limit_bytes=VMEM_BYTES)


def prepare_kernel(part, where_ref, ids_hbm, factors_hbm, weight_hbm, own_ref, sent_ref, ids_ref, factors_ref, sems):
    wrows, width = weight_hbm.shape
    topk, rows = ids_ref.shape
    core, request = where_ref[1], where_ref[2]
    small = [
        pltpu.make_async_copy(ids_hbm, ids_ref, sems.at[2]),
        pltpu.make_async_copy(factors_hbm, factors_ref, sems.at[3]),
    ]
    large = []
    for i, (ref, which) in enumerate(((own_ref, core), (sent_ref, 1 - core))):
        start = pl.multiple_of(which * (width // 2) + request * part, 128)
        large.append(pltpu.make_async_copy(weight_hbm.at[:, pl.ds(start, part)], ref.at[:wrows], sems.at[i]))
    for copy in small + large:
        copy.start()
    for copy in small:
        copy.wait()
    per_row = part // rows
    factors = factors_ref[...]
    big = factors.astype(BF16).astype(F32)
    middle = (factors - big).astype(BF16).astype(F32)
    named = (ids_ref[...].astype(F32), big, middle, factors - big - middle)
    items = [kind[k : k + 1] for kind in named for k in range(topk)]
    items += [jnp.zeros((1, rows), F32)] * (-len(items) % per_row)
    lines = [jnp.concatenate(items[i : i + per_row], axis=1) for i in range(0, len(items), per_row)]
    lines.append(jnp.zeros((TABLE_ROWS - len(lines), part), F32))
    table = jnp.concatenate(lines, axis=0).astype(BF16)
    own_ref[wrows:] = table
    sent_ref[wrows:] = table
    for copy in large:
        copy.wait()


def prepare(part, where, ids, factors, weight):
    shape = jax.ShapeDtypeStruct((weight.shape[0] + TABLE_ROWS, part), BF16)
    arrays = [pltpu.with_memory_space_constraint(x, pltpu.HBM) for x in (ids, factors, weight)]
    return pl.pallas_call(
        functools.partial(prepare_kernel, part),
        out_shape=[shape] * 2,
        in_specs=[smem()] + [hbm()] * 3,
        out_specs=[vmem()] * 2,
        scratch_shapes=[
            pltpu.VMEM(ids.shape, ids.dtype),
            pltpu.VMEM(factors.shape, factors.dtype),
            pltpu.SemaphoreType.DMA((4,)),
        ],
        compiler_params=params(),
        cost_estimate=pl.CostEstimate(flops=0, bytes_accessed=2 * weight.size, transcendentals=0),
        name="prepare",
    )(where, *arrays)


def small_call(kernel, name, shapes, operands, moved):
    return pl.pallas_call(
        kernel,
        out_shape=shapes,
        in_specs=[smem()] + [vmem()] * (len(operands) - 1),
        out_specs=[vmem()] * len(shapes),
        compiler_params=params(),
        cost_estimate=pl.CostEstimate(flops=0, bytes_accessed=moved, transcendentals=0),
        name=name,
    )(*operands)


def pack_kernel(count, part, where_ref, attn_hbm, residual_hbm, *refs):
    width = attn_hbm.shape[1]
    outs, sems = refs[:-1], refs[-1]
    copies = []
    for shift, out_ref in enumerate(outs):
        moves = [(attn_hbm, out_ref.at[:, :width])]
        request = lax.rem(where_ref[2] + shift, count)
        for core in range(2):
            start = pl.multiple_of(core * (width // 2) + request * part, 128)
            target = out_ref.at[:, width + core * part : width + (core + 1) * part]
            moves.append((residual_hbm.at[:, pl.ds(start, part)], target))
        for i, (source, target) in enumerate(moves):
            copies.append(pltpu.make_async_copy(source, target, sems.at[3 * shift + i]))
    for copy in copies:
        copy.start()
    for copy in copies:
        copy.wait()


def pack(count, part, where, attn, residual):
    rows, width = attn.shape
    arrays = [pltpu.with_memory_space_constraint(x, pltpu.HBM) for x in (attn, residual)]
    return pl.pallas_call(
        functools.partial(pack_kernel, count, part),
        out_shape=[jax.ShapeDtypeStruct((rows, width + 2 * part), BF16)] * count,
        in_specs=[smem(), hbm(), hbm()],
        out_specs=[vmem()] * count,
        scratch_shapes=[pltpu.SemaphoreType.DMA((3 * count,))],
        compiler_params=params(),
        cost_estimate=pl.CostEstimate(flops=0, bytes_accessed=4 * attn.size * count, transcendentals=0),
        name="pack",
    )(where, *arrays)


def beside_kernel(where_ref, *refs):
    part = refs[0].shape[1]
    for i, ref in enumerate(refs[:-1]):
        refs[-1][:, i * part : (i + 1) * part] = ref[...]


def beside(where, pieces):
    rows, part = pieces[0].shape
    shape = jax.ShapeDtypeStruct((rows, len(pieces) * part), BF16)
    return small_call(beside_kernel, "beside", [shape], [where] + pieces, 4 * rows * part * len(pieces))[0]


def weave_kernel(count, where_ref, *refs):
    out_ref = refs[-1]
    part = out_ref.shape[1] // (2 * count)
    place = 0
    for ref in refs[:-1]:
        for at in range(ref.shape[1] // (2 * part)):
            request = lax.rem(where_ref[2] + place, count)
            place += 1
            for swap in range(2):
                core = where_ref[1] if swap == 0 else 1 - where_ref[1]
                start = pl.multiple_of(core * (count * part) + request * part, 128)
                out_ref[:, pl.ds(start, part)] = ref[:, (2 * at + swap) * part : (2 * at + swap + 1) * part]


def weave(count, where, pieces):
    rows = pieces[0].shape[0]
    width = sum(p.shape[1] for p in pieces)
    shape = jax.ShapeDtypeStruct((rows, width), BF16)
    return small_call(functools.partial(weave_kernel, count), "weave", [shape], [where] + pieces, 4 * rows * width)[0]


def proj_kernel(wrows, part, blocks, visits, final, where_ref, ring_ref, *refs):
    total = None
    rows_refs = refs[:visits]
    width = rows_refs[0].shape[1] - 2 * part
    at = visits
    chips = ring_ref.shape[0] // 2
    position = ring_ref[where_ref[0] // 2]
    first_core = where_ref[1] == 0
    for offset in blocks:
        chip = ring_ref[chips + lax.rem(position + offset + chips, chips)]
        start = pl.multiple_of(chip * 2 * wrows, 128)
        columns = jnp.concatenate([r[:, pl.ds(start, 2 * wrows)] for r in rows_refs], axis=0)
        mine, other = refs[at][:wrows], refs[at + 1][:wrows]
        at += 2
        weight = jnp.concatenate([jnp.where(first_core, mine, other), jnp.where(first_core, other, mine)], axis=0)
        term = mm(columns, weight)
        total = term if total is None else total + term
    if final:
        total = total + refs[at][...]
        start = pl.multiple_of(width + where_ref[1] * part, 128)
        rows = rows_refs[0].shape[0]
        for i, out_ref in enumerate(refs[at + 1 :]):
            residual = rows_refs[i][:, pl.ds(start, part)].astype(F32)
            out_ref[...] = (residual + total[i * rows : (i + 1) * rows]).astype(BF16)
    else:
        refs[at][...] = total


def proj(wrows, blocks, where, ring, visits, weights, acc=None):
    final = acc is not None
    rows, part = visits[0].shape[0], weights[0].shape[1]
    operands = [where, ring] + visits + weights + ([acc] if final else [])
    count = len(visits)
    if final:
        outs = [jax.ShapeDtypeStruct((rows, part), BF16)] * count
    else:
        outs = [jax.ShapeDtypeStruct((rows * count, part), F32)]
    return pl.pallas_call(
        functools.partial(proj_kernel, wrows, part, blocks, count, final),
        out_shape=outs,
        in_specs=[smem()] * 2 + [vmem()] * (len(operands) - 2),
        out_specs=[vmem()] * len(outs),
        compiler_params=params(),
        cost_estimate=pl.CostEstimate(
            flops=8 * rows * count * part * wrows * len(blocks),
            bytes_accessed=4 * part * wrows * len(blocks) + 8 * rows * count * part,
            transcendentals=0,
        ),
        name="proj_final" if final else "proj_part",
    )(*operands)


def tables_kernel(wrows, slots, topk, rows, where_ref, *refs):
    pick_ref, put_ref, factor_ref = refs[-3:]
    both = 2 * rows
    expert_id = where_ref[0].astype(F32)
    row_of = lax.broadcasted_iota(jnp.int32, (both, both), 0)
    row_at = lax.broadcasted_iota(jnp.int32, (both, both), 1)
    slot_of = lax.broadcasted_iota(jnp.int32, (slots, both), 0).astype(F32)
    slot_at = lax.broadcasted_iota(jnp.int32, (both, slots), 1).astype(F32)
    for block in range(pick_ref.shape[0]):
        named = [refs[2 * block + i][wrows:].astype(F32) for i in range(2)]
        per_row = named[0].shape[1] // rows
        selected, factor = [], []
        for n in named:
            item = [n[i // per_row : i // per_row + 1, (i % per_row) * rows : (i % per_row + 1) * rows] for i in range(4 * topk)]
            hits = [item[k] == expert_id for k in range(topk)]
            values = [item[topk + k] + item[2 * topk + k] + item[3 * topk + k] for k in range(topk)]
            selected.append(sum(h.astype(F32) for h in hits))
            factor.append(sum(jnp.where(h, v, 0.0) for h, v in zip(hits, values)))
        selected = jnp.concatenate(selected, axis=1)
        factor = jnp.concatenate(factor, axis=1)
        spread = jnp.broadcast_to(selected, (both, both))
        before = jnp.sum(jnp.where(row_at < row_of, spread, 0.0), axis=1, keepdims=True)
        selected_down = jnp.sum(jnp.where(row_at == row_of, spread, 0.0), axis=1, keepdims=True)
        slot_down = jnp.where(selected_down > 0.0, before, -1.0)
        put_ref[block] = (slot_at == slot_down).astype(F32).astype(BF16)
        slot = jnp.sum(jnp.where(row_at == row_of, jnp.broadcast_to(slot_down, (both, both)), 0.0), axis=0, keepdims=True)
        taken = slot_of == slot
        pick_ref[block] = taken.astype(F32).astype(BF16)
        factor_ref[block] = jnp.sum(jnp.where(taken, factor, 0.0), axis=1, keepdims=True)


def tables(wrows, slots, topk, rows, where, blocks):
    chips = len(blocks) // 2
    both = 2 * rows
    return pl.pallas_call(
        functools.partial(tables_kernel, wrows, slots, topk, rows),
        out_shape=[
            jax.ShapeDtypeStruct((chips, slots, both), BF16),
            jax.ShapeDtypeStruct((chips, both, slots), BF16),
            jax.ShapeDtypeStruct((chips, slots, 1), F32),
        ],
        in_specs=[smem()] + [vmem()] * len(blocks),
        out_specs=[vmem()] * 3,
        compiler_params=params(),
        cost_estimate=pl.CostEstimate(flops=0, bytes_accessed=8 * chips * slots * both, transcendentals=0),
        name="tables",
    )(where, *blocks)


def expert_kernel(first, blocks, pieces, gain_ref, pick_ref, put_ref, factor_ref, gate_ref, up_ref, down_ref, *refs):
    slots, rows = pick_ref.shape[1:]
    own = rows // 2
    width = gain_ref.shape[1]
    hidden_units = gate_ref.shape[1]
    inputs = refs[: blocks * pieces]
    mine = refs[blocks * pieces : blocks * pieces + blocks]
    theirs, normed, hidden = refs[-3:]

    for b in range(blocks):
        block = jnp.concatenate([inputs[b * pieces + i][...] for i in range(pieces)], axis=0)
        taken = mm(pick_ref[first + b], block)
        scale = lax.rsqrt(jnp.sum(taken * taken, axis=1, keepdims=True) * (1.0 / width) + 1e-06)
        normed[b * slots : (b + 1) * slots, :] = (taken * scale * gain_ref[...]).astype(BF16)

    for start in range(0, hidden_units, TILE):
        columns = slice(start, min(start + TILE, hidden_units))
        gate_part = mm(normed[...], gate_ref[:, columns])
        up_part = mm(normed[...], up_ref[:, columns])
        hidden[:, columns] = (jax.nn.silu(gate_part) * up_part).astype(BF16)

    for start in range(0, width, TILE):
        columns = slice(start, start + TILE)
        result = mm(hidden[...], down_ref[:, columns])
        for b in range(blocks):
            weighted = (result[b * slots : (b + 1) * slots] * factor_ref[first + b]).astype(BF16)
            placed = mm(put_ref[first + b], weighted).astype(BF16)
            mine[b][:, columns] = placed[:own]
            theirs[b * own : (b + 1) * own, columns] = placed[own:]


def expert(first, blocks, tabs, gain, weights, inputs):
    slots, rows = tabs[0].shape[1:]
    width, hidden_units = weights[0].shape
    own = rows // 2
    m = blocks * slots
    weights = [pltpu.with_memory_space_constraint(w, pltpu.VMEM) for w in weights]
    out = pl.pallas_call(
        functools.partial(expert_kernel, first, blocks, len(inputs) // blocks),
        out_shape=[jax.ShapeDtypeStruct((own, width), BF16)] * blocks
        + [jax.ShapeDtypeStruct((blocks * own, width), BF16)],
        in_specs=[vmem()] * (7 + len(inputs)),
        out_specs=[vmem()] * (blocks + 1),
        scratch_shapes=[
            pltpu.VMEM((m, width), BF16),
            pltpu.VMEM((m, hidden_units), BF16),
        ],
        compiler_params=params(),
        cost_estimate=pl.CostEstimate(
            flops=12 * m * width * hidden_units,
            bytes_accessed=8 * blocks * rows * width,
            transcendentals=m * hidden_units,
        ),
        name="expert",
    )(gain, *tabs, *weights, *inputs)
    return out[:-1], out[-1]


def shared_kernel(count, gain_ref, gate_hbm, up_hbm, down_hbm, *refs):
    inputs, outs = refs[:count], refs[count : 2 * count]
    gate_ref, up_ref, down_ref, normed, hidden, sems = refs[2 * count :]
    units, width = gate_ref.shape
    rows = inputs[0].shape[0]
    tiles = [(start, min(256, units - start)) for start in range(0, units, 256)]
    copies = []
    for i, (start, size) in enumerate(tiles):
        span = pl.ds(start, size)
        for j, (source, target) in enumerate(((gate_hbm, gate_ref), (up_hbm, up_ref))):
            copies.append(pltpu.make_async_copy(source.at[span], target.at[span], sems.at[2 * i + j]))
    copies.append(pltpu.make_async_copy(down_hbm, down_ref, sems.at[2 * len(tiles)]))
    for copy in copies:
        copy.start()
    for i, ref in enumerate(inputs):
        x = ref[...].astype(F32)
        scale = lax.rsqrt(jnp.sum(x * x, axis=1, keepdims=True) * (1.0 / width) + 1e-06)
        normed[i * rows : (i + 1) * rows] = (x * scale * gain_ref[...]).astype(BF16)
    across = (((1,), (1,)), ((), ()))
    for i, (start, size) in enumerate(tiles):
        span = slice(start, start + size)
        copies[2 * i].wait()
        copies[2 * i + 1].wait()
        gate_part = lax.dot_general(normed[...], gate_ref[span], across, preferred_element_type=F32)
        up_part = lax.dot_general(normed[...], up_ref[span], across, preferred_element_type=F32)
        hidden[:, span] = (jax.nn.silu(gate_part) * up_part).astype(BF16)
    copies[-1].wait()
    for start in range(0, width, TILE):
        span = slice(start, start + TILE)
        result = mm(hidden[...], down_ref[:, span])
        for i, ref in enumerate(outs):
            ref[:, span] = result[i * rows : (i + 1) * rows].astype(ref.dtype)


def shared_expert(gain, weights, inputs):
    count = len(inputs)
    rows, width = inputs[0].shape
    units = weights[0].shape[0]
    weights = [pltpu.with_memory_space_constraint(w, pltpu.HBM) for w in weights]
    shapes = [jax.ShapeDtypeStruct((rows, width), F32)] + [jax.ShapeDtypeStruct((rows, width), BF16)] * (count - 1)
    return pl.pallas_call(
        functools.partial(shared_kernel, count),
        out_shape=shapes,
        in_specs=[vmem()] + [hbm()] * 3 + [vmem()] * count,
        out_specs=[vmem()] * count,
        scratch_shapes=[pltpu.VMEM((units, width), BF16)] * 3
        + [
            pltpu.VMEM((count * rows, width), BF16),
            pltpu.VMEM((count * rows, units), BF16),
            pltpu.SemaphoreType.DMA((2 * -(-units // 256) + 1,)),
        ],
        compiler_params=pltpu.CompilerParams(vmem_limit_bytes=24 * 1024 * 1024),
        cost_estimate=pl.CostEstimate(
            flops=12 * count * rows * width * units,
            bytes_accessed=6 * units * width + 4 * count * rows * width,
            transcendentals=count * rows * units,
        ),
        name="shared",
    )(gain, *weights, *inputs)


def base_kernel(*refs):
    total = refs[0][...]
    for ref in refs[1:-1]:
        total = total + ref[...].astype(F32)
    refs[-1][...] = total


def final_kernel(chunks, base_ref, *refs):
    out_ref = refs[-1]
    rows = refs[0].shape[0]
    for chunk in range(chunks):
        span = slice(chunk * rows, (chunk + 1) * rows)
        total = base_ref[span] + refs[chunk][...].astype(F32) + refs[chunks + chunk][...].astype(F32)
        out_ref[span] = total.astype(BF16)


def plain_call(kernel, name, shape, operands):
    return pl.pallas_call(
        kernel,
        out_shape=shape,
        in_specs=[vmem()] * len(operands),
        out_specs=vmem(),
        compiler_params=params(),
        cost_estimate=pl.CostEstimate(flops=0, bytes_accessed=8 * operands[0].size, transcendentals=0),
        name=name,
    )(*operands)


def add_kernel(*refs):
    total = refs[0][...].astype(F32)
    for ref in refs[1:-1]:
        total = total + ref[...].astype(F32)
    refs[-1][...] = total.astype(BF16)


def add(rows, *terms):
    width = terms[0][0].shape[1]

    def block(index):
        return pl.BlockSpec((rows, width), lambda i: (index, 0))

    return pl.pallas_call(
        add_kernel,
        grid=(1,),
        out_shape=jax.ShapeDtypeStruct((rows, width), BF16),
        in_specs=[block(index) for _, index in terms],
        out_specs=block(0),
        compiler_params=params(),
        cost_estimate=pl.CostEstimate(
            flops=rows * width * len(terms), bytes_accessed=2 * rows * width * (len(terms) + 1), transcendentals=0
        ),
        name="add",
    )(*[array for array, _ in terms])


def body(
    req_size,
    exp_size,
    attn_out,
    residual,
    out_weight,
    norm_gain,
    expert_ids,
    gate_weights,
    expert_gate,
    expert_up,
    expert_down,
    shared_gate,
    shared_up,
    shared_down,
):
    rows, width = attn_out.shape
    half = width // 2
    part = half // req_size
    topk = expert_ids.shape[1]
    wrows = out_weight.shape[0]
    capacity = min(rows, 3 * rows * topk // (2 * exp_size))
    slots = -(-2 * capacity // 16) * 16
    chips = exp_size // 2
    depth = chips // 2
    order = ring_order(chips)
    me = lax.axis_index("exp")
    request = lax.axis_index("req")
    here = jnp.stack([me, me % 2, lax.axis_index("req")]).astype(jnp.int32)
    ring = jnp.asarray([order.index(q) for q in range(chips)] + order, jnp.int32)

    steps = [(order[i], order[(i + 1) % chips]) for i in range(chips)]
    ahead = [(2 * a + c, 2 * b + c) for a, b in steps for c in range(2)]
    behind = [(b, a) for a, b in ahead]

    def to_ahead(x):
        return lax.ppermute(x, "exp", ahead)

    def to_behind(x):
        return lax.ppermute(x, "exp", behind)

    def to_core(x):
        return lax.ppermute(x, "exp", [(d, d ^ 1) for d in range(exp_size)])

    def to_request(x, shift, swap=0):
        pairs = [
            (i * exp_size + d, ((i + shift) % req_size) * exp_size + (d ^ swap))
            for i in range(req_size)
            for d in range(exp_size)
        ]
        return lax.ppermute(x, ("req", "exp"), pairs)

    weight_own, weight_sent = prepare(part, here, expert_ids.T, gate_weights.T, out_weight)
    weight_met = to_core(weight_sent)
    chains = [(weight_own, weight_own), (weight_met, weight_met)]
    arrived = [[weight_own, weight_met]]
    for _ in range(1, depth):
        chains = [(to_ahead(low), to_behind(high)) for low, high in chains]
        (low_own, high_own), (low_met, high_met) = chains
        arrived += [[low_own, low_met], [high_own, high_met]]

    weight_own, attn_out, residual = lax.optimization_barrier((weight_own, attn_out, residual))
    packed = pack(req_size, part, here, attn_out, residual)
    visits = [packed[0]] + [to_request(packed[shift], shift) for shift in range(1, req_size)]
    last = [to_ahead(arrived[-2][0]), to_behind(arrived[-1][1])]
    arrived[-2:], visits[1:] = lax.optimization_barrier((arrived[-2:], visits[1:]))
    visits += [to_core(v) for v in visits]

    early = [w for block in arrived[:-2] for w in block]
    late = last + [w for block in arrived[-2:] for w in block]
    whole = [w for block in arrived for w in block]
    places = [0] + [side * k for k in range(1, depth) for side in (-1, 1)]
    (acc,) = proj(wrows, places, here, ring, visits, whole)
    product = proj(wrows, [depth], here, ring, visits, last, acc)
    product, early = lax.optimization_barrier((product, early))
    tabs_early = tables(wrows, slots, topk, rows, here, early)
    tabs_late = tables(wrows, slots, topk, rows, here, late)

    got = {}
    for shift in reversed(range(req_size)):
        for swap in range(2):
            piece = product[swap * req_size + shift]
            if shift == 0:
                got[shift, swap] = piece if swap == 0 else to_core(piece)
            else:
                got[shift, swap] = to_request(piece, req_size - shift, swap)
    near = beside(here, [got[0, 0], got[0, 1]])
    far, tabs_early, tabs_late = lax.optimization_barrier(
        ([got[place, swap] for place in range(1, req_size) for swap in range(2)], tabs_early, tabs_late)
    )
    far = beside(here, far)
    gain = norm_gain.reshape(1, width)
    weights = [expert_gate[0], expert_up[0], expert_down[0]]

    lows, highs = [to_ahead(near)], [to_behind(near)]
    lows, highs, far = lax.optimization_barrier((lows, highs, far))
    lows.append(to_ahead(far))
    highs.append(to_behind(far))
    own_rows = weave(req_size, here, [near, far])
    results = {0: expert(0, 1, tabs_early, gain, weights, [own_rows, to_core(own_rows)])}
    lows, highs, results[0] = lax.optimization_barrier((lows, highs, results[0]))
    low, high = weave(req_size, here, lows), weave(req_size, here, highs)
    shared_rows = [own_rows]
    for shift in range(1, req_size):
        shared_rows.append(to_request(own_rows, shift))
    for k in range(1, depth):
        if k > 1:
            low, high, results[k - 1] = lax.optimization_barrier((low, high, results[k - 1]))
        if k == depth - 1:
            low, high, shared_rows = lax.optimization_barrier((low, high, shared_rows))
        first, tabs = (2 * k - 1, tabs_early) if k < depth - 1 else (1, tabs_late)
        results[k] = expert(first, 2, tabs, gain, weights, [low, to_core(low), high, to_core(high)])
        if k < depth - 1:
            low, high = to_ahead(low), to_behind(high)
        else:
            low, high = to_ahead(low[: rows // 2]), to_behind(high[rows // 2 :])
    low, high, results[depth - 1] = lax.optimization_barrier((low, high, results[depth - 1]))
    results[depth] = expert(0, 1, tabs_late, gain, weights, [low, high, to_core(low), to_core(high)])

    cut = rows // 2
    low, high = [None, None], [None, None]
    for k in range(depth - 1, 0, -1):
        (low_mine, high_mine), theirs = results[k]
        came = to_core(theirs)

        def send_low(chunk):
            terms = [(low_mine, chunk), (came, chunk)] + [(low[chunk], 0)] * (low[chunk] is not None)
            low[chunk] = to_behind(add(cut, *terms))

        def send_high(chunk):
            terms = [(high_mine, chunk), (came, 2 + chunk)] + [(high[chunk], 0)] * (high[chunk] is not None)
            high[chunk] = to_ahead(add(cut, *terms))

        if k == depth - 1:
            (mine,), theirs = results[depth]
            far = to_core(theirs)
            sums = add(cut, (mine, 1), (far, 1)), add(cut, (mine, 0), (far, 0))
            sums, shared_rows = lax.optimization_barrier((sums, shared_rows))
            shared = shared_expert(gain, [shared_gate.T, shared_up.T, shared_down.T], shared_rows)
            low[1], high[0] = to_behind(sums[0]), to_ahead(sums[1])
            came, shared = lax.optimization_barrier((came, shared))
            send_low(0)
            send_high(1)
            send_low(1)
            send_high(0)
            continue
        for chunk in range(2):
            send_low(chunk)
            send_high(1 - chunk)
    (mine,), theirs = results[0]
    backs = [to_request(shared[shift], req_size - shift) for shift in range(1, req_size)]
    terms = [shared[0], own_rows, mine, to_core(theirs)] + backs
    base = plain_call(base_kernel, "base", jax.ShapeDtypeStruct((rows, width), F32), terms)
    return plain_call(
        functools.partial(final_kernel, 2), "final", jax.ShapeDtypeStruct((rows, width), BF16), [base] + low + high
    )


def solution(mesh):
    return jax.shard_map(
        functools.partial(body, mesh.shape["req"], mesh.shape["exp"]),
        mesh=mesh,
        in_specs=(
            P(("req", "exp"), None),
            P(("req", "exp"), None),
            P("exp", None),
            P(),
            P(("req", "exp"), None),
            P(("req", "exp"), None),
            P("exp", None, None),
            P("exp", None, None),
            P("exp", None, None),
            P(None, "req"),
            P(None, "req"),
            P(None, "req"),
        ),
        out_specs=P(("req", "exp"), None),
        check_vma=False,
    )
```

profile of v0, /device:TPU:0, one launch (start us, length us, event | category | flops | bytes accessed | tf_op | source)
XLA Modules:
  0.0 163.9 jit_solution(7636900875614650090)
XLA Ops:
  0.1 1.8 %prepare.1 = (bf16[144,512]{1,0:T(8,128)(2,1)S(1)}, bf16[144,512]{1,0:T(8,128)(2,1)S(1)}) custom-call(s32[3]{0:T(128)S(1)} %pad_add_fusion.where_ref, s32[6,128]{1,0:T(8,128)} %bitcast.35, f32[6,128]{1,0:T(8,128)} %bitcast.36, bf16[128,2048]{1,0:T(8,128)(2,1)} %weight_hbm.1), custom_call_target="tpu_custom_call" | custom-call | bytes 524288 | tf_op jit(solution)/shard_map/prepare/pallas_call | solution.py:82
  1.9 2.0 %pack.1 = (bf16[128,3072]{1,0:T(8,128)(2,1)S(1)}, bf16[128,3072]{1,0:T(8,128)(2,1)S(1)}) custom-call(s32[3]{0:T(128)S(1)} %pad_add_fusion.where_ref, bf16[128,2048]{1,0:T(8,128)(2,1)} %attn_hbm, bf16[128,2048]{1,0:T(8,128)(2,1)} %residual_hbm), custom_call_target="tpu_custom_call" | custom-call | bytes 2097152 | tf_op jit(solution)/shard_map/pack/pallas_call | solution.py:132
  3.9 3.0 %collective-permute-start.13 = (bf16[128,3072]{1,0:T(8,128)(2,1)S(1)}, bf16[128,3072]{1,0:T(8,128)(2,1)S(1)}, u32[]{:S(2)}, u32[]{:S(2)}) collective-permute-start(bf16[128,3072]{1,0:T(8,128)(2,1)S(1)} %get-tuple-element.103), channel_id=1, source_target_pairs={{0,16},{1,17},{2,18},{3,19},{4,20},{5,21},{6,22},{7,23},{8,24},{9,... | collective-permute-start | bytes 2359304 | tf_op jit(solution)/shard_map/ppermute | solution.py:502
  6.9 1.6 collective-permute-start
  9.0 1.5 collective-permute-start.10
  11.0 2.6 %collective-permute-done.refs_6_.refs_2_ = bf16[144,512]{1,0:T(8,128)(2,1)S(1)} collective-permute-done((bf16[144,512]{1,0:T(8,128)(2,1)S(1)}, bf16[144,512]{1,0:T(8,128)(2,1)S(1)}, u32[]{:S(2)}, u32[]{:S(2)}) %collective-permute-start) | collective-permute-done | bytes 147488 | tf_op jit(solution)/shard_map/ppermute | solution.py:488
  13.6 1.6 collective-permute-start.1
  15.7 2.7 %collective-permute-done.10.refs_9_.refs_5_ = bf16[144,512]{1,0:T(8,128)(2,1)S(1)} collective-permute-done((bf16[144,512]{1,0:T(8,128)(2,1)S(1)}, bf16[144,512]{1,0:T(8,128)(2,1)S(1)}, u32[]{:S(2)}, u32[]{:S(2)}) %collective-permute-start.10) | collective-permute-done | bytes 147488 | tf_op jit(solution)/shard_map/ppermute | solution.py:491
  18.8 1.6 collective-permute-start.5
  20.4 1.6 collective-permute-start.2
  22.4 2.7 %collective-permute-done.11.refs_13_.refs_9_ = bf16[144,512]{1,0:T(8,128)(2,1)S(1)} collective-permute-done((bf16[144,512]{1,0:T(8,128)(2,1)S(1)}, bf16[144,512]{1,0:T(8,128)(2,1)S(1)}, u32[]{:S(2)}, u32[]{:S(2)}) %collective-permute-start.11) | collective-permute-done | bytes 147488 | tf_op jit(solution)/shard_map/ppermute | solution.py:491
  25.6 1.6 collective-permute-start.6
  27.2 1.5 collective-permute-done.9.refs_16_.refs_4_
  28.7 1.6 collective-permute-done.12.refs_17_.refs_5_
  30.8 1.6 collective-permute-start.16
  33.0 0.7 copy-done.3
  33.7 1.7 %proj_part.1.refs_6_ = f32[512,512]{1,0:T(8,128)S(1)} custom-call(s32[3]{0:T(128)S(1)} %pad_add_fusion.where_ref, s32[16]{0:T(128)S(1)} %copy-done.3, bf16[128,3072]{1,0:T(8,128)(2,1)S(1)} %get-tuple-element.101.refs_0_, bf16[128,3072]{1,0:T(8,128)(2,1)S(1)} %collective-permute-done.13.refs_1_, bf16[128,3072]{1,0:T(8,128)(2,1)S(1)} %collective-permute-done.14.refs_2_, ...), custom_call_target="tpu_custom_call" | custom-call | flops 1879048192 | bytes 3932160 | tf_op jit(solution)/shard_map/proj_part/pallas_call | solution.py:214
  35.4 1.6 collective-permute-done.16.refs_4_.refs_0_
  37.0 1.3 collective-permute-done.17.refs_5_.refs_1_
  38.3 0.9 proj_final.1
  39.3 1.3 collective-permute-done.18.refs_1_
  41.2 1.6 collective-permute-start.19
  44.2 1.1 tables.3
  45.3 1.5 tables.2
  46.8 2.8 %collective-permute-done.21.refs_0_ = bf16[128,512]{1,0:T(8,128)(2,1)S(1)} collective-permute-done((bf16[128,512]{1,0:T(8,128)(2,1)S(1)}, bf16[128,512]{1,0:T(8,128)(2,1)S(1)}, u32[]{:S(2)}, u32[]{:S(2)}) %collective-permute-start.21) | collective-permute-done | bytes 131104 | tf_op jit(solution)/shard_map/ppermute | solution.py:502
  50.2 0.7 collective-permute-done.20.refs_0_
  51.5 0.8 collective-permute-start.25
  52.2 1.6 collective-permute-start.23
  54.3 4.2 %expert.5 = (bf16[128,2048]{1,0:T(8,128)(2,1)S(1)}, bf16[128,2048]{1,0:T(8,128)(2,1)S(1)}) custom-call(f32[1,2048]{1,0:T(1,128)S(1)} %bitcast.29, bf16[5,144,256]{2,1,0:T(8,128)(2,1)S(1)} %get-tuple-element.138.pick_ref, bf16[5,256,144]{2,1,0:T(8,128)(2,1)S(1)} %get-tuple-element.139.put_ref, f32[5,144,1]{2,1,0:T(8,128)S(1)} %get-tuple-element.140.factor_ref, ...), custom_call_target="tpu_custom_call" | custom-call | flops 4982833152 | bytes 4194304 | tf_op jit(solution)/shard_map/expert/pallas_call | solution.py:315
  58.5 2.0 %collective-permute-done.23.refs_1_ = bf16[128,1024]{1,0:T(8,128)(2,1)S(1)} collective-permute-done((bf16[128,1024]{1,0:T(8,128)(2,1)S(1)}, bf16[128,1024]{1,0:T(8,128)(2,1)S(1)}, u32[]{:S(2)}, u32[]{:S(2)}) %collective-permute-start.23) | collective-permute-done | bytes 262176 | tf_op jit(solution)/shard_map/ppermute | solution.py:488
  60.5 1.3 collective-permute-done.24.refs_1_
  62.5 0.6 weave.4.refs_0_
  64.1 1.6 collective-permute-start.26
  65.7 7.2 %expert.6 = (bf16[128,2048]{1,0:T(8,128)(2,1)S(1)}, bf16[128,2048]{1,0:T(8,128)(2,1)S(1)}, bf16[256,2048]{1,0:T(8,128)(2,1)S(1)}) custom-call(f32[1,2048]{1,0:T(1,128)S(1)} %bitcast.30, bf16[5,144,256]{2,1,0:T(8,128)(2,1)S(1)} %get-tuple-element.138.pick_ref, bf16[5,256,144]{2,1,0:T(8,128)(2,1)S(1)} %get-tuple-element.139.put_ref, ...), custom_call_target="tpu_custom_call" | custom-call | flops 9965666304 | bytes 8388608 | tf_op jit(solution)/shard_map/expert/pallas_call | solution.py:315
  72.9 4.6 %collective-permute-done.27.refs_2_ = bf16[128,2048]{1,0:T(8,128)(2,1)S(1)} collective-permute-done((bf16[128,2048]{1,0:T(8,128)(2,1)S(1)}, bf16[128,2048]{1,0:T(8,128)(2,1)S(1)}, u32[]{:S(2)}, u32[]{:S(2)}) %collective-permute-start.27) | collective-permute-done | bytes 524320 | tf_op jit(solution)/shard_map/ppermute | solution.py:491
  78.8 1.6 collective-permute-start.30
  80.8 7.2 %expert.7 = (bf16[128,2048]{1,0:T(8,128)(2,1)S(1)}, bf16[128,2048]{1,0:T(8,128)(2,1)S(1)}, bf16[256,2048]{1,0:T(8,128)(2,1)S(1)}) custom-call(f32[1,2048]{1,0:T(1,128)S(1)} %bitcast.31, bf16[5,144,256]{2,1,0:T(8,128)(2,1)S(1)} %get-tuple-element.138.pick_ref, bf16[5,256,144]{2,1,0:T(8,128)(2,1)S(1)} %get-tuple-element.139.put_ref, ...), custom_call_target="tpu_custom_call" | custom-call | flops 9965666304 | bytes 8388608 | tf_op jit(solution)/shard_map/expert/pallas_call | solution.py:315
  88.0 4.3 %collective-permute-done.30.refs_0_ = bf16[128,2048]{1,0:T(8,128)(2,1)S(1)} collective-permute-done((bf16[128,2048]{1,0:T(8,128)(2,1)S(1)}, bf16[128,2048]{1,0:T(8,128)(2,1)S(1)}, u32[]{:S(2)}, u32[]{:S(2)}) %collective-permute-start.30) | collective-permute-done | bytes 524320 | tf_op jit(solution)/shard_map/ppermute | solution.py:488
  92.3 1.3 collective-permute-done.31.refs_2_
  94.2 1.6 collective-permute-start.35
  96.3 7.2 %expert.8 = (bf16[128,2048]{1,0:T(8,128)(2,1)S(1)}, bf16[128,2048]{1,0:T(8,128)(2,1)S(1)}, bf16[256,2048]{1,0:T(8,128)(2,1)S(1)}) custom-call(f32[1,2048]{1,0:T(1,128)S(1)} %bitcast.32, bf16[3,144,256]{2,1,0:T(8,128)(2,1)S(1)} %get-tuple-element.159.pick_ref, bf16[3,256,144]{2,1,0:T(8,128)(2,1)S(1)} %get-tuple-element.160.put_ref, ...), custom_call_target="tpu_custom_call" | custom-call | flops 9965666304 | bytes 8388608 | tf_op jit(solution)/shard_map/expert/pallas_call | solution.py:315
  104.2 1.0 collective-permute-done.40.refs_2_
  105.6 4.2 %expert.9 = (bf16[128,2048]{1,0:T(8,128)(2,1)S(1)}, bf16[128,2048]{1,0:T(8,128)(2,1)S(1)}) custom-call(f32[1,2048]{1,0:T(1,128)S(1)} %bitcast.33, bf16[3,144,256]{2,1,0:T(8,128)(2,1)S(1)} %get-tuple-element.159.pick_ref, bf16[3,256,144]{2,1,0:T(8,128)(2,1)S(1)} %get-tuple-element.160.put_ref, f32[3,144,1]{2,1,0:T(8,128)S(1)} %get-tuple-element.161.factor_ref, ...), custom_call_target="tpu_custom_call" | custom-call | flops 4982833152 | bytes 4194304 | tf_op jit(solution)/shard_map/expert/pallas_call | solution.py:315
  110.5 1.3 collective-permute-done.42.refs_1_
  111.9 1.6 collective-permute-start.54
  114.0 4.8 %shared.1 = (f32[128,2048]{1,0:T(8,128)S(1)}, bf16[128,2048]{1,0:T(8,128)(2,1)S(1)}) custom-call(f32[1,2048]{1,0:T(1,128)S(1)} %bitcast.34, bf16[704,2048]{1,0:T(8,128)(2,1)} %bitcast.37, bf16[704,2048]{1,0:T(8,128)(2,1)} %bitcast.38, bf16[704,2048]{1,0:T(8,128)(2,1)} %bitcast.39, bf16[128,2048]{1,0:T(8,128)(2,1)S(1)} %weave.3.refs_0_.refs_1_, ...), custom_call_target="tpu_custom_call" | custom-call | flops 4429185024 | bytes 10747904 | tf_op jit(solution)/shard_map/shared/pallas_call | solution.py:376
  118.9 1.6 collective-permute-start.58
  120.6 1.5 collective-permute-start.55
  122.1 0.9 collective-permute-start.51
  123.7 4.5 %collective-permute-done.58.refs_2_ = bf16[64,2048]{1,0:T(8,128)(2,1)S(1)} collective-permute-done((bf16[64,2048]{1,0:T(8,128)(2,1)S(1)}, bf16[64,2048]{1,0:T(8,128)(2,1)S(1)}, u32[]{:S(2)}, u32[]{:S(2)}) %collective-permute-start.58) | collective-permute-done | bytes 262176 | tf_op jit(solution)/shard_map/ppermute | solution.py:488
  128.3 1.6 collective-permute-start.59
  129.9 4.0 %collective-permute-done.55.refs_2_ = bf16[64,2048]{1,0:T(8,128)(2,1)S(1)} collective-permute-done((bf16[64,2048]{1,0:T(8,128)(2,1)S(1)}, bf16[64,2048]{1,0:T(8,128)(2,1)S(1)}, u32[]{:S(2)}, u32[]{:S(2)}) %collective-permute-start.55) | collective-permute-done | bytes 262176 | tf_op jit(solution)/shard_map/ppermute | solution.py:488
  133.9 1.6 collective-permute-start.56
  136.2 1.4 collective-permute-start.44
  137.7 1.1 collective-permute-done.59.refs_2_
  139.4 4.2 %collective-permute-done.56.refs_2_ = bf16[64,2048]{1,0:T(8,128)(2,1)S(1)} collective-permute-done((bf16[64,2048]{1,0:T(8,128)(2,1)S(1)}, bf16[64,2048]{1,0:T(8,128)(2,1)S(1)}, u32[]{:S(2)}, u32[]{:S(2)}) %collective-permute-start.56) | collective-permute-done | bytes 262176 | tf_op jit(solution)/shard_map/ppermute | solution.py:488
  143.6 1.5 collective-permute-start.60
  145.2 1.5 collective-permute-start.57
  146.8 2.9 %collective-permute-done.48.refs_2_ = bf16[64,2048]{1,0:T(8,128)(2,1)S(1)} collective-permute-done((bf16[64,2048]{1,0:T(8,128)(2,1)S(1)}, bf16[64,2048]{1,0:T(8,128)(2,1)S(1)}, u32[]{:S(2)}, u32[]{:S(2)}) %collective-permute-start.48) | collective-permute-done | bytes 262176 | tf_op jit(solution)/shard_map/ppermute | solution.py:491
  151.2 1.7 %collective-permute-done.60.refs_3_ = bf16[64,2048]{1,0:T(8,128)(2,1)S(1)} collective-permute-done((bf16[64,2048]{1,0:T(8,128)(2,1)S(1)}, bf16[64,2048]{1,0:T(8,128)(2,1)S(1)}, u32[]{:S(2)}, u32[]{:S(2)}) %collective-permute-start.60) | collective-permute-done | bytes 262176 | tf_op jit(solution)/shard_map/ppermute | solution.py:488
  152.9 3.9 %collective-permute-done.57.refs_2_ = bf16[64,2048]{1,0:T(8,128)(2,1)S(1)} collective-permute-done((bf16[64,2048]{1,0:T(8,128)(2,1)S(1)}, bf16[64,2048]{1,0:T(8,128)(2,1)S(1)}, u32[]{:S(2)}, u32[]{:S(2)}) %collective-permute-start.57) | collective-permute-done | bytes 262176 | tf_op jit(solution)/shard_map/ppermute | solution.py:488
  156.7 2.2 %collective-permute-done.53.refs_1_ = bf16[64,2048]{1,0:T(8,128)(2,1)S(1)} collective-permute-done((bf16[64,2048]{1,0:T(8,128)(2,1)S(1)}, bf16[64,2048]{1,0:T(8,128)(2,1)S(1)}, u32[]{:S(2)}, u32[]{:S(2)}) %collective-permute-start.53) | collective-permute-done | bytes 262176 | tf_op jit(solution)/shard_map/ppermute | solution.py:491
  159.0 4.0 %collective-permute-done.49.refs_0_ = bf16[64,2048]{1,0:T(8,128)(2,1)S(1)} collective-permute-done((bf16[64,2048]{1,0:T(8,128)(2,1)S(1)}, bf16[64,2048]{1,0:T(8,128)(2,1)S(1)}, u32[]{:S(2)}, u32[]{:S(2)}) %collective-permute-start.49) | collective-permute-done | bytes 262176 | tf_op jit(solution)/shard_map/ppermute | solution.py:491
  163.0 0.9 final.1
  (107 shorter events, 18.8 us)
Async XLA Ops:
  0.1 54.2 %copy-start.1 = (bf16[1,1408,2048]{2,1,0:T(8,128)(2,1)S(1)}, bf16[1,1408,2048]{2,1,0:T(8,128)(2,1)}, u32[]{:S(2)}) copy-start(bf16[1,1408,2048]{2,1,0:T(8,128)(2,1)} %param.21) | copy-start | bytes 17301508
  3.9 26.8 %collective-permute-start.13 = (bf16[128,3072]{1,0:T(8,128)(2,1)S(1)}, bf16[128,3072]{1,0:T(8,128)(2,1)S(1)}, u32[]{:S(2)}, u32[]{:S(2)}) collective-permute-start(bf16[128,3072]{1,0:T(8,128)(2,1)S(1)} %get-tuple-element.103), channel_id=1, source_target_pairs={{0,16},{1,17},{2,18},{3,19},{4,20},{5,21},{6,22},{7,23},{8,24},{9,... | collective-permute-start | bytes 2359304 | tf_op jit(solution)/shard_map/ppermute | solution.py:502
  6.9 2.0 %collective-permute-start.3 = (bf16[144,512]{1,0:T(8,128)(2,1)S(1)}, bf16[144,512]{1,0:T(8,128)(2,1)S(1)}, u32[]{:S(2)}, u32[]{:S(2)}) collective-permute-start(bf16[144,512]{1,0:T(8,128)(2,1)S(1)} %get-tuple-element.102), channel_id=1, source_target_pairs={{0,1},{1,0},{2,3},{3,2},{4,5},{5,4},{6,7},{7,6},{8,9},{9,8},{10,11... | collective-permute-start | bytes 442376 | tf_op jit(solution)/shard_map/ppermute | solution.py:494
  6.9 6.6 %collective-permute-start = (bf16[144,512]{1,0:T(8,128)(2,1)S(1)}, bf16[144,512]{1,0:T(8,128)(2,1)S(1)}, u32[]{:S(2)}, u32[]{:S(2)}) collective-permute-start(bf16[144,512]{1,0:T(8,128)(2,1)S(1)} %get-tuple-element.117.refs_4_.refs_0_), channel_id=1, source_target_pairs={{0,4},{1,5},{4,8},{5,9},{8,12},{9,13},{12,14},{13,15},{14,10},{15,... | collective-permute-start | bytes 442376 | tf_op jit(solution)/shard_map/ppermute | solution.py:488
  8.5 6.7 %collective-permute-start.7 = (bf16[144,512]{1,0:T(8,128)(2,1)S(1)}, bf16[144,512]{1,0:T(8,128)(2,1)S(1)}, u32[]{:S(2)}, u32[]{:S(2)}) collective-permute-start(bf16[144,512]{1,0:T(8,128)(2,1)S(1)} %get-tuple-element.117.refs_4_.refs_0_), channel_id=1, source_target_pairs={{4,0},{5,1},{8,4},{9,5},{12,8},{13,9},{14,12},{15,13},{10,14},{11,... | collective-permute-start | bytes 442376 | tf_op jit(solution)/shard_map/ppermute | solution.py:491
  9.0 9.4 %collective-permute-start.10 = (bf16[144,512]{1,0:T(8,128)(2,1)S(1)}, bf16[144,512]{1,0:T(8,128)(2,1)S(1)}, u32[]{:S(2)}, u32[]{:S(2)}) collective-permute-start(bf16[144,512]{1,0:T(8,128)(2,1)S(1)} %collective-permute-done.3.refs_5_.refs_1_), channel_id=1, source_target_pairs={{4,0},{5,1},{8,4},{9,5},{12,8},{13,9},{14,12},{15,13},{10,14},{11,... | collective-permute-start | bytes 442376 | tf_op jit(solution)/shard_map/ppermute | solution.py:491
  10.5 8.3 %collective-permute-start.4 = (bf16[144,512]{1,0:T(8,128)(2,1)S(1)}, bf16[144,512]{1,0:T(8,128)(2,1)S(1)}, u32[]{:S(2)}, u32[]{:S(2)}) collective-permute-start(bf16[144,512]{1,0:T(8,128)(2,1)S(1)} %collective-permute-done.3.refs_5_.refs_1_), channel_id=1, source_target_pairs={{0,4},{1,5},{4,8},{5,9},{8,12},{9,13},{12,14},{13,15},{14,10},{15,... | collective-permute-start | bytes 442376 | tf_op jit(solution)/shard_map/ppermute | solution.py:488
  13.6 6.8 %collective-permute-start.1 = (bf16[144,512]{1,0:T(8,128)(2,1)S(1)}, bf16[144,512]{1,0:T(8,128)(2,1)S(1)}, u32[]{:S(2)}, u32[]{:S(2)}) collective-permute-start(bf16[144,512]{1,0:T(8,128)(2,1)S(1)} %collective-permute-done.refs_6_.refs_2_), channel_id=1, source_target_pairs={{0,4},{1,5},{4,8},{5,9},{8,12},{9,13},{12,14},{13,15},{14,10},{15,... | collective-permute-start | bytes 442376 | tf_op jit(solution)/shard_map/ppermute | solution.py:488
  15.2 6.8 %collective-permute-start.8 = (bf16[144,512]{1,0:T(8,128)(2,1)S(1)}, bf16[144,512]{1,0:T(8,128)(2,1)S(1)}, u32[]{:S(2)}, u32[]{:S(2)}) collective-permute-start(bf16[144,512]{1,0:T(8,128)(2,1)S(1)} %collective-permute-done.7.refs_8_.refs_4_), channel_id=1, source_target_pairs={{4,0},{5,1},{8,4},{9,5},{12,8},{13,9},{14,12},{15,13},{10,14},{11,... | collective-permute-start | bytes 442376 | tf_op jit(solution)/shard_map/ppermute | solution.py:491
  18.4 6.8 %collective-permute-start.11 = (bf16[144,512]{1,0:T(8,128)(2,1)S(1)}, bf16[144,512]{1,0:T(8,128)(2,1)S(1)}, u32[]{:S(2)}, u32[]{:S(2)}) collective-permute-start(bf16[144,512]{1,0:T(8,128)(2,1)S(1)} %collective-permute-done.10.refs_9_.refs_5_), channel_id=1, source_target_pairs={{4,0},{5,1},{8,4},{9,5},{12,8},{13,9},{14,12},{15,13},{10,14},{11,... | collective-permute-start | bytes 442376 | tf_op jit(solution)/shard_map/ppermute | solution.py:491
  18.8 6.8 %collective-permute-start.5 = (bf16[144,512]{1,0:T(8,128)(2,1)S(1)}, bf16[144,512]{1,0:T(8,128)(2,1)S(1)}, u32[]{:S(2)}, u32[]{:S(2)}) collective-permute-start(bf16[144,512]{1,0:T(8,128)(2,1)S(1)} %collective-permute-done.4.refs_7_.refs_3_), channel_id=1, source_target_pairs={{0,4},{1,5},{4,8},{5,9},{8,12},{9,13},{12,14},{13,15},{14,10},{15,... | collective-permute-start | bytes 442376 | tf_op jit(solution)/shard_map/ppermute | solution.py:488
  20.4 6.8 %collective-permute-start.2 = (bf16[144,512]{1,0:T(8,128)(2,1)S(1)}, bf16[144,512]{1,0:T(8,128)(2,1)S(1)}, u32[]{:S(2)}, u32[]{:S(2)}) collective-permute-start(bf16[144,512]{1,0:T(8,128)(2,1)S(1)} %collective-permute-done.1.refs_10_.refs_6_), channel_id=1, source_target_pairs={{0,4},{1,5},{4,8},{5,9},{8,12},{9,13},{12,14},{13,15},{14,10},{15,... | collective-permute-start | bytes 442376 | tf_op jit(solution)/shard_map/ppermute | solution.py:488
  22.0 6.7 %collective-permute-start.9 = (bf16[144,512]{1,0:T(8,128)(2,1)S(1)}, bf16[144,512]{1,0:T(8,128)(2,1)S(1)}, u32[]{:S(2)}, u32[]{:S(2)}) collective-permute-start(bf16[144,512]{1,0:T(8,128)(2,1)S(1)} %collective-permute-done.8.refs_12_.refs_8_), channel_id=1, source_target_pairs={{4,0},{5,1},{8,4},{9,5},{12,8},{13,9},{14,12},{15,13},{10,14},{11,... | collective-permute-start | bytes 442376 | tf_op jit(solution)/shard_map/ppermute | solution.py:491
  25.2 5.1 %collective-permute-start.12 = (bf16[144,512]{1,0:T(8,128)(2,1)S(1)}, bf16[144,512]{1,0:T(8,128)(2,1)S(1)}, u32[]{:S(2)}, u32[]{:S(2)}) collective-permute-start(bf16[144,512]{1,0:T(8,128)(2,1)S(1)} %collective-permute-done.11.refs_13_.refs_9_), channel_id=1, source_target_pairs={{4,0},{5,1},{8,4},{9,5},{12,8},{13,9},{14,12},{15,13},{10,14},{11,... | collective-permute-start | bytes 442376 | tf_op jit(solution)/shard_map/ppermute | solution.py:491
  25.6 5.1 %collective-permute-start.6 = (bf16[144,512]{1,0:T(8,128)(2,1)S(1)}, bf16[144,512]{1,0:T(8,128)(2,1)S(1)}, u32[]{:S(2)}, u32[]{:S(2)}) collective-permute-start(bf16[144,512]{1,0:T(8,128)(2,1)S(1)} %collective-permute-done.5.refs_11_.refs_7_), channel_id=1, source_target_pairs={{0,4},{1,5},{4,8},{5,9},{8,12},{9,13},{12,14},{13,15},{14,10},{15,... | collective-permute-start | bytes 442376 | tf_op jit(solution)/shard_map/ppermute | solution.py:488
  27.2 5.6 %collective-permute-start.14 = (bf16[128,3072]{1,0:T(8,128)(2,1)S(1)}, bf16[128,3072]{1,0:T(8,128)(2,1)S(1)}, u32[]{:S(2)}, u32[]{:S(2)}) collective-permute-start(bf16[128,3072]{1,0:T(8,128)(2,1)S(1)} %get-tuple-element.101.refs_0_), channel_id=1, source_target_pairs={{0,1},{1,0},{2,3},{3,2},{4,5},{5,4},{6,7},{7,6},{8,9},{9,8},{10,11... | collective-permute-start | bytes 2359304 | tf_op jit(solution)/shard_map/ppermute | solution.py:494
  30.8 2.3 %collective-permute-start.15 = (bf16[128,3072]{1,0:T(8,128)(2,1)S(1)}, bf16[128,3072]{1,0:T(8,128)(2,1)S(1)}, u32[]{:S(2)}, u32[]{:S(2)}) collective-permute-start(bf16[128,3072]{1,0:T(8,128)(2,1)S(1)} %collective-permute-done.13.refs_1_), channel_id=1, source_target_pairs={{0,1},{1,0},{2,3},{3,2},{4,5},{5,4},{6,7},{7,6},{8,9},{9,8},{10,11... | collective-permute-start | bytes 2359304 | tf_op jit(solution)/shard_map/ppermute | solution.py:494
  30.8 6.3 %collective-permute-start.16 = (bf16[144,512]{1,0:T(8,128)(2,1)S(1)}, bf16[144,512]{1,0:T(8,128)(2,1)S(1)}, u32[]{:S(2)}, u32[]{:S(2)}) collective-permute-start(bf16[144,512]{1,0:T(8,128)(2,1)S(1)} %collective-permute-done.2.refs_14_.refs_2_), channel_id=1, source_target_pairs={{0,4},{1,5},{4,8},{5,9},{8,12},{9,13},{12,14},{13,15},{14,10},{15,... | collective-permute-start | bytes 442376 | tf_op jit(solution)/shard_map/ppermute | solution.py:488
  32.3 6.0 %collective-permute-start.17 = (bf16[144,512]{1,0:T(8,128)(2,1)S(1)}, bf16[144,512]{1,0:T(8,128)(2,1)S(1)}, u32[]{:S(2)}, u32[]{:S(2)}) collective-permute-start(bf16[144,512]{1,0:T(8,128)(2,1)S(1)} %collective-permute-done.12.refs_17_.refs_5_), channel_id=1, source_target_pairs={{4,0},{5,1},{8,4},{9,5},{12,8},{13,9},{14,12},{15,13},{10,14},{11,... | collective-permute-start | bytes 442376 | tf_op jit(solution)/shard_map/ppermute | solution.py:491
  33.7 20.6 %slice-start = ((s8[5767168]{0:T(1024)(128)(4,1)}), s8[4194304]{0:T(1024)(128)(4,1)S(1)}, s32[]{:S(2)}) async-start(s8[5767168]{0:T(1024)(128)(4,1)} %bitcast.12), calls=%async_computation | async-start | bytes 8388608
  35.4 18.9 %slice-start.1 = ((s8[5767168]{0:T(1024)(128)(4,1)}), s8[1572864]{0:T(1024)(128)(4,1)S(1)}, s32[]{:S(2)}) async-start(s8[5767168]{0:T(1024)(128)(4,1)} %bitcast.12), calls=%async_computation.1 | async-start | bytes 3145728
  39.2 1.4 collective-permute-start.18
  41.2 9.0 %collective-permute-start.19 = (bf16[128,1024]{1,0:T(8,128)(2,1)S(1)}, bf16[128,1024]{1,0:T(8,128)(2,1)S(1)}, u32[]{:S(2)}, u32[]{:S(2)}) collective-permute-start(bf16[128,1024]{1,0:T(8,128)(2,1)S(1)} %beside.2.refs_0_), channel_id=1, source_target_pairs={{0,4},{1,5},{4,8},{5,9},{8,12},{9,13},{12,14},{13,15},{14,10},{15,... | collective-permute-start | bytes 786440 | tf_op jit(solution)/shard_map/ppermute | solution.py:488
  42.8 8.1 %collective-permute-start.20 = (bf16[128,1024]{1,0:T(8,128)(2,1)S(1)}, bf16[128,1024]{1,0:T(8,128)(2,1)S(1)}, u32[]{:S(2)}, u32[]{:S(2)}) collective-permute-start(bf16[128,1024]{1,0:T(8,128)(2,1)S(1)} %beside.2.refs_0_), channel_id=1, source_target_pairs={{4,0},{5,1},{8,4},{9,5},{12,8},{13,9},{14,12},{15,13},{10,14},{11,... | collective-permute-start | bytes 786440 | tf_op jit(solution)/shard_map/ppermute | solution.py:491
  43.2 6.4 %collective-permute-start.21 = (bf16[128,512]{1,0:T(8,128)(2,1)S(1)}, bf16[128,512]{1,0:T(8,128)(2,1)S(1)}, u32[]{:S(2)}, u32[]{:S(2)}) collective-permute-start(bf16[128,512]{1,0:T(8,128)(2,1)S(1)} %get-tuple-element.115), channel_id=1, source_target_pairs={{0,16},{1,17},{2,18},{3,19},{4,20},{5,21},{6,22},{7,23},{8,24},{9,... | collective-permute-start | bytes 393224 | tf_op jit(solution)/shard_map/ppermute | solution.py:502
  43.8 5.9 %collective-permute-start.22 = (bf16[128,512]{1,0:T(8,128)(2,1)S(1)}, bf16[128,512]{1,0:T(8,128)(2,1)S(1)}, u32[]{:S(2)}, u32[]{:S(2)}) collective-permute-start(bf16[128,512]{1,0:T(8,128)(2,1)S(1)} %get-tuple-element.116), channel_id=1, source_target_pairs={{0,17},{1,16},{2,19},{3,18},{4,21},{5,20},{6,23},{7,22},{8,25},{9,... | collective-permute-start | bytes 393224 | tf_op jit(solution)/shard_map/ppermute | solution.py:502
  51.5 2.8 %collective-permute-start.25 = (bf16[128,2048]{1,0:T(8,128)(2,1)S(1)}, bf16[128,2048]{1,0:T(8,128)(2,1)S(1)}, u32[]{:S(2)}, u32[]{:S(2)}) collective-permute-start(bf16[128,2048]{1,0:T(8,128)(2,1)S(1)} %weave.3.refs_0_.refs_1_), channel_id=1, source_target_pairs={{0,1},{1,0},{2,3},{3,2},{4,5},{5,4},{6,7},{7,6},{8,9},{9,8},{10,11... | collective-permute-start | bytes 1572872 | tf_op jit(solution)/shard_map/ppermute | solution.py:494
  52.2 8.3 %collective-permute-start.23 = (bf16[128,1024]{1,0:T(8,128)(2,1)S(1)}, bf16[128,1024]{1,0:T(8,128)(2,1)S(1)}, u32[]{:S(2)}, u32[]{:S(2)}) collective-permute-start(bf16[128,1024]{1,0:T(8,128)(2,1)S(1)} %beside.3.refs_1_), channel_id=1, source_target_pairs={{0,4},{1,5},{4,8},{5,9},{8,12},{9,13},{12,14},{13,15},{14,10},{15,... | collective-permute-start | bytes 786440 | tf_op jit(solution)/shard_map/ppermute | solution.py:488
  53.8 8.0 %collective-permute-start.24 = (bf16[128,1024]{1,0:T(8,128)(2,1)S(1)}, bf16[128,1024]{1,0:T(8,128)(2,1)S(1)}, u32[]{:S(2)}, u32[]{:S(2)}) collective-permute-start(bf16[128,1024]{1,0:T(8,128)(2,1)S(1)} %beside.3.refs_1_), channel_id=1, source_target_pairs={{4,0},{5,1},{8,4},{9,5},{12,8},{13,9},{14,12},{15,13},{10,14},{11,... | collective-permute-start | bytes 786440 | tf_op jit(solution)/shard_map/ppermute | solution.py:491
  62.4 3.3 %collective-permute-start.29 = (bf16[128,2048]{1,0:T(8,128)(2,1)S(1)}, bf16[128,2048]{1,0:T(8,128)(2,1)S(1)}, u32[]{:S(2)}, u32[]{:S(2)}) collective-permute-start(bf16[128,2048]{1,0:T(8,128)(2,1)S(1)} %weave.5.refs_2_), channel_id=1, source_target_pairs={{0,1},{1,0},{2,3},{3,2},{4,5},{5,4},{6,7},{7,6},{8,9},{9,8},{10,11... | collective-permute-start | bytes 1572872 | tf_op jit(solution)/shard_map/ppermute | solution.py:494
  63.1 2.6 %collective-permute-start.28 = (bf16[128,2048]{1,0:T(8,128)(2,1)S(1)}, bf16[128,2048]{1,0:T(8,128)(2,1)S(1)}, u32[]{:S(2)}, u32[]{:S(2)}) collective-permute-start(bf16[128,2048]{1,0:T(8,128)(2,1)S(1)} %weave.4.refs_0_), channel_id=1, source_target_pairs={{0,1},{1,0},{2,3},{3,2},{4,5},{5,4},{6,7},{7,6},{8,9},{9,8},{10,11... | collective-permute-start | bytes 1572872 | tf_op jit(solution)/shard_map/ppermute | solution.py:494
  63.6 13.9 %collective-permute-start.27 = (bf16[128,2048]{1,0:T(8,128)(2,1)S(1)}, bf16[128,2048]{1,0:T(8,128)(2,1)S(1)}, u32[]{:S(2)}, u32[]{:S(2)}) collective-permute-start(bf16[128,2048]{1,0:T(8,128)(2,1)S(1)} %weave.5.refs_2_), channel_id=1, source_target_pairs={{4,0},{5,1},{8,4},{9,5},{12,8},{13,9},{14,12},{15,13},{10,14},{11,... | collective-permute-start | bytes 1572872 | tf_op jit(solution)/shard_map/ppermute | solution.py:491
  64.1 13.7 %collective-permute-start.26 = (bf16[128,2048]{1,0:T(8,128)(2,1)S(1)}, bf16[128,2048]{1,0:T(8,128)(2,1)S(1)}, u32[]{:S(2)}, u32[]{:S(2)}) collective-permute-start(bf16[128,2048]{1,0:T(8,128)(2,1)S(1)} %weave.4.refs_0_), channel_id=1, source_target_pairs={{0,4},{1,5},{4,8},{5,9},{8,12},{9,13},{12,14},{13,15},{14,10},{15,... | collective-permute-start | bytes 1572872 | tf_op jit(solution)/shard_map/ppermute | solution.py:488
  77.8 3.1 %collective-permute-start.32 = (bf16[128,2048]{1,0:T(8,128)(2,1)S(1)}, bf16[128,2048]{1,0:T(8,128)(2,1)S(1)}, u32[]{:S(2)}, u32[]{:S(2)}) collective-permute-start(bf16[128,2048]{1,0:T(8,128)(2,1)S(1)} %collective-permute-done.26.refs_0_), channel_id=1, source_target_pairs={{0,1},{1,0},{2,3},{3,2},{4,5},{5,4},{6,7},{7,6},{8,9},{9,8},{10,11... | collective-permute-start | bytes 1572872 | tf_op jit(solution)/shard_map/ppermute | solution.py:494
  77.8 3.1 %collective-permute-start.33 = (bf16[128,2048]{1,0:T(8,128)(2,1)S(1)}, bf16[128,2048]{1,0:T(8,128)(2,1)S(1)}, u32[]{:S(2)}, u32[]{:S(2)}) collective-permute-start(bf16[128,2048]{1,0:T(8,128)(2,1)S(1)} %collective-permute-done.27.refs_2_), channel_id=1, source_target_pairs={{0,1},{1,0},{2,3},{3,2},{4,5},{5,4},{6,7},{7,6},{8,9},{9,8},{10,11... | collective-permute-start | bytes 1572872 | tf_op jit(solution)/shard_map/ppermute | solution.py:494
  78.3 15.4 %collective-permute-start.34 = (bf16[128,2048]{1,0:T(8,128)(2,1)S(1)}, bf16[128,2048]{1,0:T(8,128)(2,1)S(1)}, u32[]{:S(2)}, u32[]{:S(2)}) collective-permute-start(bf16[128,2048]{1,0:T(8,128)(2,1)S(1)} %weave.3.refs_0_.refs_1_), channel_id=1, source_target_pairs={{0,16},{1,17},{2,18},{3,19},{4,20},{5,21},{6,22},{7,23},{8,24},{9,... | collective-permute-start | bytes 1572872 | tf_op jit(solution)/shard_map/ppermute | solution.py:502
  78.8 13.6 %collective-permute-start.30 = (bf16[128,2048]{1,0:T(8,128)(2,1)S(1)}, bf16[128,2048]{1,0:T(8,128)(2,1)S(1)}, u32[]{:S(2)}, u32[]{:S(2)}) collective-permute-start(bf16[128,2048]{1,0:T(8,128)(2,1)S(1)} %collective-permute-done.26.refs_0_), channel_id=1, source_target_pairs={{0,4},{1,5},{4,8},{5,9},{8,12},{9,13},{12,14},{13,15},{14,10},{15,... | collective-permute-start | bytes 1572872 | tf_op jit(solution)/shard_map/ppermute | solution.py:488
  80.4 13.3 %collective-permute-start.31 = (bf16[128,2048]{1,0:T(8,128)(2,1)S(1)}, bf16[128,2048]{1,0:T(8,128)(2,1)S(1)}, u32[]{:S(2)}, u32[]{:S(2)}) collective-permute-start(bf16[128,2048]{1,0:T(8,128)(2,1)S(1)} %collective-permute-done.27.refs_2_), channel_id=1, source_target_pairs={{4,0},{5,1},{8,4},{9,5},{12,8},{13,9},{14,12},{15,13},{10,14},{11,... | collective-permute-start | bytes 1572872 | tf_op jit(solution)/shard_map/ppermute | solution.py:491
  93.6 2.6 %collective-permute-start.37 = (bf16[128,2048]{1,0:T(8,128)(2,1)S(1)}, bf16[128,2048]{1,0:T(8,128)(2,1)S(1)}, u32[]{:S(2)}, u32[]{:S(2)}) collective-permute-start(bf16[128,2048]{1,0:T(8,128)(2,1)S(1)} %collective-permute-done.30.refs_0_), channel_id=1, source_target_pairs={{0,1},{1,0},{2,3},{3,2},{4,5},{5,4},{6,7},{7,6},{8,9},{9,8},{10,11... | collective-permute-start | bytes 1572872 | tf_op jit(solution)/shard_map/ppermute | solution.py:494
  93.6 2.7 %collective-permute-start.38 = (bf16[128,2048]{1,0:T(8,128)(2,1)S(1)}, bf16[128,2048]{1,0:T(8,128)(2,1)S(1)}, u32[]{:S(2)}, u32[]{:S(2)}) collective-permute-start(bf16[128,2048]{1,0:T(8,128)(2,1)S(1)} %collective-permute-done.31.refs_2_), channel_id=1, source_target_pairs={{0,1},{1,0},{2,3},{3,2},{4,5},{5,4},{6,7},{7,6},{8,9},{9,8},{10,11... | collective-permute-start | bytes 1572872 | tf_op jit(solution)/shard_map/ppermute | solution.py:494
  94.2 9.3 %collective-permute-start.35 = (bf16[64,2048]{1,0:T(8,128)(2,1)S(1)}, bf16[64,2048]{1,0:T(8,128)(2,1)S(1)}, u32[]{:S(2)}, u32[]{:S(2)}) collective-permute-start(bf16[64,2048]{1,0:T(8,128)(2,1)S(1)} %slice.6), channel_id=1, source_target_pairs={{0,4},{1,5},{4,8},{5,9},{8,12},{9,13},{12,14},{13,15},{14,10},{15,... | collective-permute-start | bytes 786440 | tf_op jit(solution)/shard_map/ppermute | solution.py:488
  95.8 7.9 %collective-permute-start.36 = (bf16[64,2048]{1,0:T(8,128)(2,1)S(1)}, bf16[64,2048]{1,0:T(8,128)(2,1)S(1)}, u32[]{:S(2)}, u32[]{:S(2)}) collective-permute-start(bf16[64,2048]{1,0:T(8,128)(2,1)S(1)} %slice.7), channel_id=1, source_target_pairs={{4,0},{5,1},{8,4},{9,5},{12,8},{13,9},{14,12},{15,13},{10,14},{11,... | collective-permute-start | bytes 786440 | tf_op jit(solution)/shard_map/ppermute | solution.py:491
  103.7 1.5 collective-permute-start.40
  103.7 1.9 %collective-permute-start.41 = (bf16[64,2048]{1,0:T(8,128)(2,1)S(1)}, bf16[64,2048]{1,0:T(8,128)(2,1)S(1)}, u32[]{:S(2)}, u32[]{:S(2)}) collective-permute-start(bf16[64,2048]{1,0:T(8,128)(2,1)S(1)} %collective-permute-done.36.refs_1_), channel_id=1, source_target_pairs={{0,1},{1,0},{2,3},{3,2},{4,5},{5,4},{6,7},{7,6},{8,9},{9,8},{10,11... | collective-permute-start | bytes 786440 | tf_op jit(solution)/shard_map/ppermute | solution.py:494
  104.2 14.6 %collective-permute-start.39 = (bf16[256,2048]{1,0:T(8,128)(2,1)S(1)}, bf16[256,2048]{1,0:T(8,128)(2,1)S(1)}, u32[]{:S(2)}, u32[]{:S(2)}) collective-permute-start(bf16[256,2048]{1,0:T(8,128)(2,1)S(1)} %get-tuple-element.165), channel_id=1, source_target_pairs={{0,1},{1,0},{2,3},{3,2},{4,5},{5,4},{6,7},{7,6},{8,9},{9,8},{10,11... | collective-permute-start | bytes 3145736 | tf_op jit(solution)/shard_map/ppermute | solution.py:494
  109.8 2.0 %collective-permute-start.42 = (bf16[128,2048]{1,0:T(8,128)(2,1)S(1)}, bf16[128,2048]{1,0:T(8,128)(2,1)S(1)}, u32[]{:S(2)}, u32[]{:S(2)}) collective-permute-start(bf16[128,2048]{1,0:T(8,128)(2,1)S(1)} %get-tuple-element.169), channel_id=1, source_target_pairs={{0,1},{1,0},{2,3},{3,2},{4,5},{5,4},{6,7},{7,6},{8,9},{9,8},{10,11... | collective-permute-start | bytes 1572872 | tf_op jit(solution)/shard_map/ppermute | solution.py:494
  110.0 13.1 %collective-permute-start.46 = (bf16[256,2048]{1,0:T(8,128)(2,1)S(1)}, bf16[256,2048]{1,0:T(8,128)(2,1)S(1)}, u32[]{:S(2)}, u32[]{:S(2)}) collective-permute-start(bf16[256,2048]{1,0:T(8,128)(2,1)S(1)} %get-tuple-element.183), channel_id=1, source_target_pairs={{0,1},{1,0},{2,3},{3,2},{4,5},{5,4},{6,7},{7,6},{8,9},{9,8},{10,11... | collective-permute-start | bytes 3145736 | tf_op jit(solution)/shard_map/ppermute | solution.py:494
  110.4 25.2 %collective-permute-start.45 = (bf16[256,2048]{1,0:T(8,128)(2,1)S(1)}, bf16[256,2048]{1,0:T(8,128)(2,1)S(1)}, u32[]{:S(2)}, u32[]{:S(2)}) collective-permute-start(bf16[256,2048]{1,0:T(8,128)(2,1)S(1)} %get-tuple-element.181), channel_id=1, source_target_pairs={{0,1},{1,0},{2,3},{3,2},{4,5},{5,4},{6,7},{7,6},{8,9},{9,8},{10,11... | collective-permute-start | bytes 3145736 | tf_op jit(solution)/shard_map/ppermute | solution.py:494
  111.9 8.6 %collective-permute-start.54 = (bf16[64,2048]{1,0:T(8,128)(2,1)S(1)}, bf16[64,2048]{1,0:T(8,128)(2,1)S(1)}, u32[]{:S(2)}, u32[]{:S(2)}) collective-permute-start(bf16[64,2048]{1,0:T(8,128)(2,1)S(1)} %add.24), channel_id=1, source_target_pairs={{0,4},{1,5},{4,8},{5,9},{8,12},{9,13},{12,14},{13,15},{14,10},{15,... | collective-permute-start | bytes 786440 | tf_op jit(solution)/shard_map/ppermute | solution.py:488
  113.5 8.6 %collective-permute-start.50 = (bf16[64,2048]{1,0:T(8,128)(2,1)S(1)}, bf16[64,2048]{1,0:T(8,128)(2,1)S(1)}, u32[]{:S(2)}, u32[]{:S(2)}) collective-permute-start(bf16[64,2048]{1,0:T(8,128)(2,1)S(1)} %add.23), channel_id=1, source_target_pairs={{4,0},{5,1},{8,4},{9,5},{12,8},{13,9},{14,12},{15,13},{10,14},{11,... | collective-permute-start | bytes 786440 | tf_op jit(solution)/shard_map/ppermute | solution.py:491
  118.9 9.3 %collective-permute-start.58 = (bf16[64,2048]{1,0:T(8,128)(2,1)S(1)}, bf16[64,2048]{1,0:T(8,128)(2,1)S(1)}, u32[]{:S(2)}, u32[]{:S(2)}) collective-permute-start(bf16[64,2048]{1,0:T(8,128)(2,1)S(1)} %add.34), channel_id=1, source_target_pairs={{0,4},{1,5},{4,8},{5,9},{8,12},{9,13},{12,14},{13,15},{14,10},{15,... | collective-permute-start | bytes 786440 | tf_op jit(solution)/shard_map/ppermute | solution.py:488
  120.6 13.2 %collective-permute-start.55 = (bf16[64,2048]{1,0:T(8,128)(2,1)S(1)}, bf16[64,2048]{1,0:T(8,128)(2,1)S(1)}, u32[]{:S(2)}, u32[]{:S(2)}) collective-permute-start(bf16[64,2048]{1,0:T(8,128)(2,1)S(1)} %add.31), channel_id=1, source_target_pairs={{0,4},{1,5},{4,8},{5,9},{8,12},{9,13},{12,14},{13,15},{14,10},{15,... | collective-permute-start | bytes 786440 | tf_op jit(solution)/shard_map/ppermute | solution.py:488
  122.1 11.8 %collective-permute-start.51 = (bf16[64,2048]{1,0:T(8,128)(2,1)S(1)}, bf16[64,2048]{1,0:T(8,128)(2,1)S(1)}, u32[]{:S(2)}, u32[]{:S(2)}) collective-permute-start(bf16[64,2048]{1,0:T(8,128)(2,1)S(1)} %add.28), channel_id=1, source_target_pairs={{4,0},{5,1},{8,4},{9,5},{12,8},{13,9},{14,12},{15,13},{10,14},{11,... | collective-permute-start | bytes 786440 | tf_op jit(solution)/shard_map/ppermute | solution.py:491
  123.2 13.0 %collective-permute-start.47 = (bf16[64,2048]{1,0:T(8,128)(2,1)S(1)}, bf16[64,2048]{1,0:T(8,128)(2,1)S(1)}, u32[]{:S(2)}, u32[]{:S(2)}) collective-permute-start(bf16[64,2048]{1,0:T(8,128)(2,1)S(1)} %add.25), channel_id=1, source_target_pairs={{4,0},{5,1},{8,4},{9,5},{12,8},{13,9},{14,12},{15,13},{10,14},{11,... | collective-permute-start | bytes 786440 | tf_op jit(solution)/shard_map/ppermute | solution.py:491
  128.3 10.5 %collective-permute-start.59 = (bf16[64,2048]{1,0:T(8,128)(2,1)S(1)}, bf16[64,2048]{1,0:T(8,128)(2,1)S(1)}, u32[]{:S(2)}, u32[]{:S(2)}) collective-permute-start(bf16[64,2048]{1,0:T(8,128)(2,1)S(1)} %add.35), channel_id=1, source_target_pairs={{0,4},{1,5},{4,8},{5,9},{8,12},{9,13},{12,14},{13,15},{14,10},{15,... | collective-permute-start | bytes 786440 | tf_op jit(solution)/shard_map/ppermute | solution.py:488
  133.8 16.5 %collective-permute-start.43 = (bf16[128,2048]{1,0:T(8,128)(2,1)S(1)}, bf16[128,2048]{1,0:T(8,128)(2,1)S(1)}, u32[]{:S(2)}, u32[]{:S(2)}) collective-permute-start(bf16[128,2048]{1,0:T(8,128)(2,1)S(1)} %get-tuple-element.178), channel_id=1, source_target_pairs={{0,1},{1,0},{2,3},{3,2},{4,5},{5,4},{6,7},{7,6},{8,9},{9,8},{10,11... | collective-permute-start | bytes 1572872 | tf_op jit(solution)/shard_map/ppermute | solution.py:494
  133.9 9.7 %collective-permute-start.56 = (bf16[64,2048]{1,0:T(8,128)(2,1)S(1)}, bf16[64,2048]{1,0:T(8,128)(2,1)S(1)}, u32[]{:S(2)}, u32[]{:S(2)}) collective-permute-start(bf16[64,2048]{1,0:T(8,128)(2,1)S(1)} %add.32), channel_id=1, source_target_pairs={{0,4},{1,5},{4,8},{5,9},{8,12},{9,13},{12,14},{13,15},{14,10},{15,... | collective-permute-start | bytes 786440 | tf_op jit(solution)/shard_map/ppermute | solution.py:488
  135.6 9.6 %collective-permute-start.52 = (bf16[64,2048]{1,0:T(8,128)(2,1)S(1)}, bf16[64,2048]{1,0:T(8,128)(2,1)S(1)}, u32[]{:S(2)}, u32[]{:S(2)}) collective-permute-start(bf16[64,2048]{1,0:T(8,128)(2,1)S(1)} %add.29), channel_id=1, source_target_pairs={{4,0},{5,1},{8,4},{9,5},{12,8},{13,9},{14,12},{15,13},{10,14},{11,... | collective-permute-start | bytes 786440 | tf_op jit(solution)/shard_map/ppermute | solution.py:491
  136.2 14.7 %collective-permute-start.44 = (bf16[128,2048]{1,0:T(8,128)(2,1)S(1)}, bf16[128,2048]{1,0:T(8,128)(2,1)S(1)}, u32[]{:S(2)}, u32[]{:S(2)}) collective-permute-start(bf16[128,2048]{1,0:T(8,128)(2,1)S(1)} %get-tuple-element.179), channel_id=1, source_target_pairs={{0,16},{1,17},{2,18},{3,19},{4,20},{5,21},{6,22},{7,23},{8,24},{9,... | collective-permute-start | bytes 1572872 | tf_op jit(solution)/shard_map/ppermute | solution.py:502
  138.8 10.9 %collective-permute-start.48 = (bf16[64,2048]{1,0:T(8,128)(2,1)S(1)}, bf16[64,2048]{1,0:T(8,128)(2,1)S(1)}, u32[]{:S(2)}, u32[]{:S(2)}) collective-permute-start(bf16[64,2048]{1,0:T(8,128)(2,1)S(1)} %add.26), channel_id=1, source_target_pairs={{4,0},{5,1},{8,4},{9,5},{12,8},{13,9},{14,12},{15,13},{10,14},{11,... | collective-permute-start | bytes 786440 | tf_op jit(solution)/shard_map/ppermute | solution.py:491
  143.6 9.2 %collective-permute-start.60 = (bf16[64,2048]{1,0:T(8,128)(2,1)S(1)}, bf16[64,2048]{1,0:T(8,128)(2,1)S(1)}, u32[]{:S(2)}, u32[]{:S(2)}) collective-permute-start(bf16[64,2048]{1,0:T(8,128)(2,1)S(1)} %add.36), channel_id=1, source_target_pairs={{0,4},{1,5},{4,8},{5,9},{8,12},{9,13},{12,14},{13,15},{14,10},{15,... | collective-permute-start | bytes 786440 | tf_op jit(solution)/shard_map/ppermute | solution.py:488
  145.2 11.5 %collective-permute-start.57 = (bf16[64,2048]{1,0:T(8,128)(2,1)S(1)}, bf16[64,2048]{1,0:T(8,128)(2,1)S(1)}, u32[]{:S(2)}, u32[]{:S(2)}) collective-permute-start(bf16[64,2048]{1,0:T(8,128)(2,1)S(1)} %add.33), channel_id=1, source_target_pairs={{0,4},{1,5},{4,8},{5,9},{8,12},{9,13},{12,14},{13,15},{14,10},{15,... | collective-permute-start | bytes 786440 | tf_op jit(solution)/shard_map/ppermute | solution.py:488
  149.7 9.2 %collective-permute-start.53 = (bf16[64,2048]{1,0:T(8,128)(2,1)S(1)}, bf16[64,2048]{1,0:T(8,128)(2,1)S(1)}, u32[]{:S(2)}, u32[]{:S(2)}) collective-permute-start(bf16[64,2048]{1,0:T(8,128)(2,1)S(1)} %add.30), channel_id=1, source_target_pairs={{4,0},{5,1},{8,4},{9,5},{12,8},{13,9},{14,12},{15,13},{10,14},{11,... | collective-permute-start | bytes 786440 | tf_op jit(solution)/shard_map/ppermute | solution.py:491
  150.4 12.6 %collective-permute-start.49 = (bf16[64,2048]{1,0:T(8,128)(2,1)S(1)}, bf16[64,2048]{1,0:T(8,128)(2,1)S(1)}, u32[]{:S(2)}, u32[]{:S(2)}) collective-permute-start(bf16[64,2048]{1,0:T(8,128)(2,1)S(1)} %add.27), channel_id=1, source_target_pairs={{4,0},{5,1},{8,4},{9,5},{12,8},{13,9},{14,12},{15,13},{10,14},{11,... | collective-permute-start | bytes 786440 | tf_op jit(solution)/shard_map/ppermute | solution.py:491
  (3 other events, 38.4 us)
where the time goes:
time: 164 us
  waiting for transfers between devices  64.7 us (39%)
  Pallas kernels  49.1 us (30%)
  starting transfers between devices  48.9 us (30%)
    ppermute x19, waiting for transfers between devices, to_ahead(): return lax.ppermute(x, 'exp', ahead)  30.4 us
    pallas_call x5, Pallas kernels, expert(): pl.pallas_call(functools.partial(expert_kernel, first, blocks, len(inputs...  30 us
    ppermute x19, starting transfers between devices, to_ahead(): return lax.ppermute(x, 'exp', ahead)  28.5 us
    ppermute x19, waiting for transfers between devices, to_behind(): return lax.ppermute(x, 'exp', behind)  27.1 us
    ppermute x19, starting transfers between devices, to_behind(): return lax.ppermute(x, 'exp', behind)  10.7 us
    ppermute x5, starting transfers between devices, to_request(): return lax.ppermute(x, ('req', 'exp'), pairs)  5.91 us
    pallas_call x1, Pallas kernels, shared_expert(): pl.pallas_call(functools.partial(shared_kernel, count), out_shape=shapes,...  4.83 us
    ppermute x18, waiting for transfers between devices, to_core(): return lax.ppermute(x, 'exp', [(d, d ^ 1) for d in range(exp_size)])  4.27 us
  transfers between devices with their start and end apart: 61, of which 31 were waited for; matrix products, arithmetic and copies ran while one was open for 0% of the time, Pallas kernels for 25%

commit v1 on v0

--- a/solution.py
+++ b/solution.py
@@ -44,21 +44,27 @@
     return pltpu.CompilerParams(vmem_limit_bytes=VMEM_BYTES)
 
 
-def prepare_kernel(part, where_ref, ids_hbm, factors_hbm, weight_hbm, own_ref, sent_ref, ids_ref, factors_ref, sems):
+def prepare_kernel(count, part, where_ref, ids_hbm, factors_hbm, weight_hbm, attn_hbm, residual_hbm, own_ref, sent_ref, *refs):
+    packs = refs[:count]
+    ids_ref, factors_ref, sems = refs[count:]
     wrows, width = weight_hbm.shape
     topk, rows = ids_ref.shape
     core, request = where_ref[1], where_ref[2]
-    small = [
-        pltpu.make_async_copy(ids_hbm, ids_ref, sems.at[2]),
-        pltpu.make_async_copy(factors_hbm, factors_ref, sems.at[3]),
-    ]
-    large = []
-    for i, (ref, which) in enumerate(((own_ref, core), (sent_ref, 1 - core))):
+    moves = [(ids_hbm, ids_ref), (factors_hbm, factors_ref)]
+    for ref, which in ((own_ref, core), (sent_ref, 1 - core)):
         start = pl.multiple_of(which * (width // 2) + request * part, 128)
-        large.append(pltpu.make_async_copy(weight_hbm.at[:, pl.ds(start, part)], ref.at[:wrows], sems.at[i]))
-    for copy in small + large:
+        moves.append((weight_hbm.at[:, pl.ds(start, part)], ref.at[:wrows]))
+    for shift, ref in enumerate(packs):
+        moves.append((attn_hbm, ref.at[:, :width]))
+        other = lax.rem(request + shift, count)
+        for half in range(2):
+            start = pl.multiple_of(half * (width // 2) + other * part, 128)
+            target = ref.at[:, width + half * part : width + (half + 1) * part]
+            moves.append((residual_hbm.at[:, pl.ds(start, part)], target))
+    copies = [pltpu.make_async_copy(source, target, sems.at[i]) for i, (source, target) in enumerate(moves)]
+    for copy in copies:
         copy.start()
-    for copy in small:
+    for copy in copies[:2]:
         copy.wait()
     per_row = part // rows
     factors = factors_ref[...]
@@ -72,27 +78,30 @@
     table = jnp.concatenate(lines, axis=0).astype(BF16)
     own_ref[wrows:] = table
     sent_ref[wrows:] = table
-    for copy in large:
+    for copy in copies[2:]:
         copy.wait()
 
 
-def prepare(part, where, ids, factors, weight):
+def prepare(count, part, where, ids, factors, weight, attn, residual):
+    rows, width = attn.shape
     shape = jax.ShapeDtypeStruct((weight.shape[0] + TABLE_ROWS, part), BF16)
-    arrays = [pltpu.with_memory_space_constraint(x, pltpu.HBM) for x in (ids, factors, weight)]
-    return pl.pallas_call(
-        functools.partial(prepare_kernel, part),
-        out_shape=[shape] * 2,
-        in_specs=[smem()] + [hbm()] * 3,
-        out_specs=[vmem()] * 2,
+    packed = jax.ShapeDtypeStruct((rows, width + 2 * part), BF16)
+    arrays = [pltpu.with_memory_space_constraint(x, pltpu.HBM) for x in (ids, factors, weight, attn, residual)]
+    out = pl.pallas_call(
+        functools.partial(prepare_kernel, count, part),
+        out_shape=[shape] * 2 + [packed] * count,
+        in_specs=[smem()] + [hbm()] * 5,
+        out_specs=[vmem()] * (2 + count),
         scratch_shapes=[
             pltpu.VMEM(ids.shape, ids.dtype),
             pltpu.VMEM(factors.shape, factors.dtype),
-            pltpu.SemaphoreType.DMA((4,)),
+            pltpu.SemaphoreType.DMA((4 + 3 * count,)),
         ],
         compiler_params=params(),
-        cost_estimate=pl.CostEstimate(flops=0, bytes_accessed=2 * weight.size, transcendentals=0),
+        cost_estimate=pl.CostEstimate(flops=0, bytes_accessed=8 * attn.size, transcendentals=0),
         name="prepare",
     )(where, *arrays)
+    return out[0], out[1], out[2:]
 
 
 def small_call(kernel, name, shapes, operands, moved):
@@ -105,40 +114,6 @@
         cost_estimate=pl.CostEstimate(flops=0, bytes_accessed=moved, transcendentals=0),
         name=name,
     )(*operands)
-
-
-def pack_kernel(count, part, where_ref, attn_hbm, residual_hbm, *refs):
-    width = attn_hbm.shape[1]
-    outs, sems = refs[:-1], refs[-1]
-    copies = []
-    for shift, out_ref in enumerate(outs):
-        moves = [(attn_hbm, out_ref.at[:, :width])]
-        request = lax.rem(where_ref[2] + shift, count)
-        for core in range(2):
-            start = pl.multiple_of(core * (width // 2) + request * part, 128)
-            target = out_ref.at[:, width + core * part : width + (core + 1) * part]
-            moves.append((residual_hbm.at[:, pl.ds(start, part)], target))
-        for i, (source, target) in enumerate(moves):
-            copies.append(pltpu.make_async_copy(source, target, sems.at[3 * shift + i]))
-    for copy in copies:
-        copy.start()
-    for copy in copies:
-        copy.wait()
-
-
-def pack(count, part, where, attn, residual):
-    rows, width = attn.shape
-    arrays = [pltpu.with_memory_space_constraint(x, pltpu.HBM) for x in (attn, residual)]
-    return pl.pallas_call(
-        functools.partial(pack_kernel, count, part),
-        out_shape=[jax.ShapeDtypeStruct((rows, width + 2 * part), BF16)] * count,
-        in_specs=[smem(), hbm(), hbm()],
-        out_specs=[vmem()] * count,
-        scratch_shapes=[pltpu.SemaphoreType.DMA((3 * count,))],
-        compiler_params=params(),
-        cost_estimate=pl.CostEstimate(flops=0, bytes_accessed=4 * attn.size * count, transcendentals=0),
-        name="pack",
-    )(where, *arrays)
 
 
 def beside_kernel(where_ref, *refs):
@@ -324,7 +299,7 @@
         ],
         compiler_params=params(),
         cost_estimate=pl.CostEstimate(
-            flops=12 * m * width * hidden_units,
+            flops=2 * m * width * hidden_units,
             bytes_accessed=8 * blocks * rows * width,
             transcendentals=m * hidden_units,
         ),
@@ -334,8 +309,8 @@
 
 
 def shared_kernel(count, gain_ref, gate_hbm, up_hbm, down_hbm, *refs):
-    inputs, outs = refs[:count], refs[count : 2 * count]
-    gate_ref, up_ref, down_ref, normed, hidden, sems = refs[2 * count :]
+    inputs, outs = refs[:count], refs[count + 1 : 2 * count + 1]
+    gate_ref, up_ref, down_ref, normed, hidden, sems = refs[2 * count + 1 :]
     units, width = gate_ref.shape
     rows = inputs[0].shape[0]
     tiles = [(start, min(256, units - start)) for start in range(0, units, 256)]
@@ -367,7 +342,7 @@
             ref[:, span] = result[i * rows : (i + 1) * rows].astype(ref.dtype)
 
 
-def shared_expert(gain, weights, inputs):
+def shared_expert(gain, weights, inputs, after):
     count = len(inputs)
     rows, width = inputs[0].shape
     units = weights[0].shape[0]
@@ -376,7 +351,7 @@
     return pl.pallas_call(
         functools.partial(shared_kernel, count),
         out_shape=shapes,
-        in_specs=[vmem()] + [hbm()] * 3 + [vmem()] * count,
+        in_specs=[vmem()] + [hbm()] * 3 + [vmem()] * count + [hbm()],
         out_specs=[vmem()] * count,
         scratch_shapes=[pltpu.VMEM((units, width), BF16)] * 3
         + [
@@ -391,7 +366,7 @@
             transcendentals=count * rows * units,
         ),
         name="shared",
-    )(gain, *weights, *inputs)
+    )(gain, *weights, *inputs, after)
 
 
 def base_kernel(*refs):
@@ -422,31 +397,31 @@
     )(*operands)
 
 
-def add_kernel(*refs):
+def add_kernel(count, *refs):
     total = refs[0][...].astype(F32)
-    for ref in refs[1:-1]:
+    for ref in refs[1:count]:
         total = total + ref[...].astype(F32)
     refs[-1][...] = total.astype(BF16)
 
 
-def add(rows, *terms):
+def add(rows, after, *terms):
     width = terms[0][0].shape[1]
 
     def block(index):
         return pl.BlockSpec((rows, width), lambda i: (index, 0))
 
     return pl.pallas_call(
-        add_kernel,
+        functools.partial(add_kernel, len(terms)),
         grid=(1,),
         out_shape=jax.ShapeDtypeStruct((rows, width), BF16),
-        in_specs=[block(index) for _, index in terms],
+        in_specs=[block(index) for _, index in terms] + [hbm()] * len(after),
         out_specs=block(0),
         compiler_params=params(),
         cost_estimate=pl.CostEstimate(
             flops=rows * width * len(terms), bytes_accessed=2 * rows * width * (len(terms) + 1), transcendentals=0
         ),
         name="add",
-    )(*[array for array, _ in terms])
+    )(*[array for array, _ in terms], *after)
 
 
 def body(
@@ -501,7 +476,9 @@
         ]
         return lax.ppermute(x, ("req", "exp"), pairs)
 
-    weight_own, weight_sent = prepare(part, here, expert_ids.T, gate_weights.T, out_weight)
+    weight_own, weight_sent, packed = prepare(
+        req_size, part, here, expert_ids.T, gate_weights.T, out_weight, attn_out, residual
+    )
     weight_met = to_core(weight_sent)
     chains = [(weight_own, weight_own), (weight_met, weight_met)]
     arrived = [[weight_own, weight_met]]
@@ -510,8 +487,6 @@
         (low_own, high_own), (low_met, high_met) = chains
         arrived += [[low_own, low_met], [high_own, high_met]]
 
-    weight_own, attn_out, residual = lax.optimization_barrier((weight_own, attn_out, residual))
-    packed = pack(req_size, part, here, attn_out, residual)
     visits = [packed[0]] + [to_request(packed[shift], shift) for shift in range(1, req_size)]
     last = [to_ahead(arrived[-2][0]), to_behind(arrived[-1][1])]
     arrived[-2:], visits[1:] = lax.optimization_barrier((arrived[-2:], visits[1:]))
@@ -551,57 +526,64 @@
     results = {0: expert(0, 1, tabs_early, gain, weights, [own_rows, to_core(own_rows)])}
     lows, highs, results[0] = lax.optimization_barrier((lows, highs, results[0]))
     low, high = weave(req_size, here, lows), weave(req_size, here, highs)
-    shared_rows = [own_rows]
-    for shift in range(1, req_size):
-        shared_rows.append(to_request(own_rows, shift))
+    came = {}
+    theirs = results[0][1]
     for k in range(1, depth):
         if k > 1:
-            low, high, results[k - 1] = lax.optimization_barrier((low, high, results[k - 1]))
-        if k == depth - 1:
+            low, high, results[k - 1], came[k - 2] = lax.optimization_barrier(
+                (low, high, results[k - 1], came[k - 2])
+            )
+            theirs = results[k - 1][1]
+        if k == min(2, depth - 1):
             low, high, shared_rows = lax.optimization_barrier((low, high, shared_rows))
+        others = to_core(low), to_core(high)
+        came[k - 1] = to_core(theirs)
+        if k == 1:
+            others, own_rows = lax.optimization_barrier((others, own_rows))
+            shared_rows = [own_rows]
+            for shift in range(1, req_size):
+                shared_rows.append(to_request(own_rows, shift))
         first, tabs = (2 * k - 1, tabs_early) if k < depth - 1 else (1, tabs_late)
-        results[k] = expert(first, 2, tabs, gain, weights, [low, to_core(low), high, to_core(high)])
+        results[k] = expert(first, 2, tabs, gain, weights, [low, others[0], high, others[1]])
         if k < depth - 1:
             low, high = to_ahead(low), to_behind(high)
         else:
             low, high = to_ahead(low[: rows // 2]), to_behind(high[rows // 2 :])
-    low, high, results[depth - 1] = lax.optimization_barrier((low, high, results[depth - 1]))
+    low, high, results[depth - 1], came[depth - 2] = lax.optimization_barrier(
+        (low, high, results[depth - 1], came[depth - 2])
+    )
     results[depth] = expert(0, 1, tabs_late, gain, weights, [low, high, to_core(low), to_core(high)])
 
     cut = rows // 2
-    low, high = [None, None], [None, None]
+    came[depth - 1], came[depth] = to_core(results[depth - 1][1]), to_core(results[depth][1])
+
+    def step(after, k, low_chunk, low, high):
+        low_mine, high_mine = results[k][0]
+        low_terms = [(low_mine, low_chunk), (came[k], low_chunk)] + [(x, 0) for x in low]
+        high_terms = [(high_mine, 1 - low_chunk), (came[k], 3 - low_chunk)] + [(x, 0) for x in high]
+        low_sum = add(cut, after, *low_terms)
+        high_sum = add(cut, [low_sum], *high_terms)
+        return [high_sum], [to_behind(low_sum)], [to_ahead(high_sum)]
+
+    (mine,), _ = results[depth]
+    low_sum = add(cut, [], (mine, 1), (came[depth], 1))
+    high_sum = add(cut, [low_sum], (mine, 0), (came[depth], 0))
+    first = [to_behind(low_sum)], [to_ahead(high_sum)]
+    second = [], []
+    after = [high_sum]
     for k in range(depth - 1, 0, -1):
-        (low_mine, high_mine), theirs = results[k]
-        came = to_core(theirs)
-
-        def send_low(chunk):
-            terms = [(low_mine, chunk), (came, chunk)] + [(low[chunk], 0)] * (low[chunk] is not None)
-            low[chunk] = to_behind(add(cut, *terms))
-
-        def send_high(chunk):
-            terms = [(high_mine, chunk), (came, 2 + chunk)] + [(high[chunk], 0)] * (high[chunk] is not None)
-            high[chunk] = to_ahead(add(cut, *terms))
-
+        if k == 1:
+            (mine,), _ = results[0]
+            backs = [to_request(shared[shift], req_size - shift) for shift in range(1, req_size)]
+            terms = [shared[0], own_rows, mine, came[0]] + backs
+            base = plain_call(base_kernel, "base", jax.ShapeDtypeStruct((rows, width), F32), terms)
+            after = after + [base]
+        after, *second = step(after, k, 0, *second)
         if k == depth - 1:
-            (mine,), theirs = results[depth]
-            far = to_core(theirs)
-            sums = add(cut, (mine, 1), (far, 1)), add(cut, (mine, 0), (far, 0))
-            sums, shared_rows = lax.optimization_barrier((sums, shared_rows))
-            shared = shared_expert(gain, [shared_gate.T, shared_up.T, shared_down.T], shared_rows)
-            low[1], high[0] = to_behind(sums[0]), to_ahead(sums[1])
-            came, shared = lax.optimization_barrier((came, shared))
-            send_low(0)
-            send_high(1)
-            send_low(1)
-            send_high(0)
-            continue
-        for chunk in range(2):
-            send_low(chunk)
-            send_high(1 - chunk)
-    (mine,), theirs = results[0]
-    backs = [to_request(shared[shift], req_size - shift) for shift in range(1, req_size)]
-    terms = [shared[0], own_rows, mine, to_core(theirs)] + backs
-    base = plain_call(base_kernel, "base", jax.ShapeDtypeStruct((rows, width), F32), terms)
+            shared = shared_expert(gain, [shared_gate.T, shared_up.T, shared_down.T], shared_rows, after[0])
+            after = [shared[0]]
+        after, *first = step(after, k, 1, *first)
+    low, high = [second[0][0], first[0][0]], [first[1][0], second[1][0]]
     return plain_call(
         functools.partial(final_kernel, 2), "final", jax.ShapeDtypeStruct((rows, width), BF16), [base] + low + high
     )

time: 164 us -> 162 us (0.988)
    ppermute x19, waiting for transfers between devices: 30.4 us -> 26.2 us  [to_ahead(): return lax.ppermute(x, 'exp', ahead)]
    ppermute x18, waiting for transfers between devices: 4.27 us -> 7.77 us  [to_core(): return lax.ppermute(x, 'exp', [(d, d ^ 1) for d in range(exp_size)])]
    ppermute x5, waiting for transfers between devices: 2.86 us -> 5.08 us  [to_request(): return lax.ppermute(x, ('req', 'exp'), pairs)]
    pallas_call x16 -> x15, Pallas kernels: 5.05 us -> 3.59 us  [the longest x1 2.37 us: prepare(): pl.pallas_call(functools.partial(prepare_kernel, count, part), out_shape=...]
  transfers between devices with their start and end apart: 61 -> 61, of which waited for: 31 -> 37; matrix products, arithmetic and copies ran while one was open for 0% -> 0% of each run, Pallas kernels for 25% -> 26%
where the time goes in v1:
time: 162 us
  waiting for transfers between devices  65.3 us (40%)
  starting transfers between devices  47.8 us (30%)
  Pallas kernels  47.7 us (29%)
    pallas_call x5, Pallas kernels, expert(): pl.pallas_call(functools.partial(expert_kernel, first, blocks, len(inputs...  30.1 us
    ppermute x19, starting transfers between devices, to_ahead(): return lax.ppermute(x, 'exp', ahead)  28.9 us
    ppermute x19, waiting for transfers between devices, to_behind(): return lax.ppermute(x, 'exp', behind)  26.3 us
    ppermute x19, waiting for transfers between devices, to_ahead(): return lax.ppermute(x, 'exp', ahead)  26.2 us
    ppermute x19, starting transfers between devices, to_behind(): return lax.ppermute(x, 'exp', behind)  10.3 us
    ppermute x18, waiting for transfers between devices, to_core(): return lax.ppermute(x, 'exp', [(d, d ^ 1) for d in range(exp_size)])  7.77 us
    ppermute x5, starting transfers between devices, to_request(): return lax.ppermute(x, ('req', 'exp'), pairs)  5.14 us
    ppermute x5, waiting for transfers between devices, to_request(): return lax.ppermute(x, ('req', 'exp'), pairs)  5.08 us
  transfers between devices with their start and end apart: 61, of which 37 were waited for; matrix products, arithmetic and copies ran while one was open for 0% of the time, Pallas kernels for 26%

profile of v1, /device:TPU:0, one launch (start us, length us, event | category | flops | bytes accessed | tf_op | source)
XLA Modules:
  0.0 162.0 jit_solution(14200659425730843250)
XLA Ops:
  0.1 2.4 %prepare.1 = (bf16[144,512]{1,0:T(8,128)(2,1)S(1)}, bf16[144,512]{1,0:T(8,128)(2,1)S(1)}, bf16[128,3072]{1,0:T(8,128)(2,1)S(1)}, bf16[128,3072]{1,0:T(8,128)(2,1)S(1)}) custom-call(s32[3]{0:T(128)S(1)} %pad_add_fusion.where_ref, s32[6,128]{1,0:T(8,128)} %bitcast.35, f32[6,128]{1,0:T(8,128)} %bitcast.36, bf16[128,2048]{1,0:T(8,128)(2,1)} %weight_hbm.1, ...), custom_call_target="tpu_custom_call" | custom-call | bytes 2097152 | tf_op jit(solution)/shard_map/prepare/pallas_call | solution.py:90
  2.5 3.0 %collective-permute-start.13 = (bf16[128,3072]{1,0:T(8,128)(2,1)S(1)}, bf16[128,3072]{1,0:T(8,128)(2,1)S(1)}, u32[]{:S(2)}, u32[]{:S(2)}) collective-permute-start(bf16[128,3072]{1,0:T(8,128)(2,1)S(1)} %get-tuple-element.98), channel_id=1, source_target_pairs={{0,16},{1,17},{2,18},{3,19},{4,20},{5,21},{6,22},{7,23},{8,24},{9,... | collective-permute-start | bytes 2359304 | tf_op jit(solution)/shard_map/ppermute | solution.py:477
  5.5 1.6 collective-permute-start
  7.5 1.5 collective-permute-start.10
  9.5 2.6 %collective-permute-done.refs_6_.refs_2_ = bf16[144,512]{1,0:T(8,128)(2,1)S(1)} collective-permute-done((bf16[144,512]{1,0:T(8,128)(2,1)S(1)}, bf16[144,512]{1,0:T(8,128)(2,1)S(1)}, u32[]{:S(2)}, u32[]{:S(2)}) %collective-permute-start) | collective-permute-done | bytes 147488 | tf_op jit(solution)/shard_map/ppermute | solution.py:463
  12.1 1.6 collective-permute-start.1
  14.2 2.7 %collective-permute-done.10.refs_9_.refs_5_ = bf16[144,512]{1,0:T(8,128)(2,1)S(1)} collective-permute-done((bf16[144,512]{1,0:T(8,128)(2,1)S(1)}, bf16[144,512]{1,0:T(8,128)(2,1)S(1)}, u32[]{:S(2)}, u32[]{:S(2)}) %collective-permute-start.10) | collective-permute-done | bytes 147488 | tf_op jit(solution)/shard_map/ppermute | solution.py:466
  17.3 1.6 collective-permute-start.5
  18.9 1.6 collective-permute-start.2
  21.0 2.7 %collective-permute-done.11.refs_13_.refs_9_ = bf16[144,512]{1,0:T(8,128)(2,1)S(1)} collective-permute-done((bf16[144,512]{1,0:T(8,128)(2,1)S(1)}, bf16[144,512]{1,0:T(8,128)(2,1)S(1)}, u32[]{:S(2)}, u32[]{:S(2)}) %collective-permute-start.11) | collective-permute-done | bytes 147488 | tf_op jit(solution)/shard_map/ppermute | solution.py:466
  24.1 1.6 collective-permute-start.6
  25.7 1.5 collective-permute-done.9.refs_16_.refs_4_
  27.2 1.6 collective-permute-done.12.refs_17_.refs_5_
  29.3 1.6 collective-permute-start.16
  32.2 1.7 %proj_part.1.refs_6_ = f32[512,512]{1,0:T(8,128)S(1)} custom-call(s32[3]{0:T(128)S(1)} %pad_add_fusion.where_ref, s32[16]{0:T(128)S(1)} %copy-done.3, bf16[128,3072]{1,0:T(8,128)(2,1)S(1)} %get-tuple-element.95.refs_0_, bf16[128,3072]{1,0:T(8,128)(2,1)S(1)} %collective-permute-done.13.refs_1_, bf16[128,3072]{1,0:T(8,128)(2,1)S(1)} %collective-permute-done.14.refs_2_, ...), custom_call_target="tpu_custom_call" | custom-call | flops 1879048192 | bytes 3932160 | tf_op jit(solution)/shard_map/proj_part/pallas_call | solution.py:189
  33.9 1.6 collective-permute-done.16.refs_4_.refs_0_
  35.5 1.3 collective-permute-done.17.refs_5_.refs_1_
  36.8 0.9 proj_final.1
  37.8 1.3 collective-permute-done.18.refs_1_
  39.7 1.6 %collective-permute-start.19 = (bf16[128,1024]{1,0:T(8,128)(2,1)S(1)}, bf16[128,1024]{1,0:T(8,128)(2,1)S(1)}, u32[]{:S(2)}, u32[]{:S(2)}) collective-permute-start(bf16[128,1024]{1,0:T(8,128)(2,1)S(1)} %beside.2.refs_0_), channel_id=1, source_target_pairs={{0,4},{1,5},{4,8},{5,9},{8,12},{9,13},{12,14},{13,15},{14,10},{15,... | collective-permute-start | bytes 786440 | tf_op jit(solution)/shard_map/ppermute | solution.py:463
  42.7 1.1 tables.3
  43.8 1.5 tables.2
  45.3 2.8 %collective-permute-done.21.refs_0_ = bf16[128,512]{1,0:T(8,128)(2,1)S(1)} collective-permute-done((bf16[128,512]{1,0:T(8,128)(2,1)S(1)}, bf16[128,512]{1,0:T(8,128)(2,1)S(1)}, u32[]{:S(2)}, u32[]{:S(2)}) %collective-permute-start.21) | collective-permute-done | bytes 131104 | tf_op jit(solution)/shard_map/ppermute | solution.py:477
  50.0 0.8 collective-permute-start.25
  50.8 1.6 collective-permute-start.23
  52.8 4.2 %expert.5 = (bf16[128,2048]{1,0:T(8,128)(2,1)S(1)}, bf16[128,2048]{1,0:T(8,128)(2,1)S(1)}) custom-call(f32[1,2048]{1,0:T(1,128)S(1)} %bitcast.29, bf16[5,144,256]{2,1,0:T(8,128)(2,1)S(1)} %get-tuple-element.133.pick_ref, bf16[5,256,144]{2,1,0:T(8,128)(2,1)S(1)} %get-tuple-element.134.put_ref, f32[5,144,1]{2,1,0:T(8,128)S(1)} %get-tuple-element.135.factor_ref, ...), custom_call_target="tpu_custom_call" | custom-call | flops 830472192 | bytes 4194304 | tf_op jit(solution)/shard_map/expert/pallas_call | solution.py:290
  57.0 2.0 %collective-permute-done.23.refs_1_ = bf16[128,1024]{1,0:T(8,128)(2,1)S(1)} collective-permute-done((bf16[128,1024]{1,0:T(8,128)(2,1)S(1)}, bf16[128,1024]{1,0:T(8,128)(2,1)S(1)}, u32[]{:S(2)}, u32[]{:S(2)}) %collective-permute-start.23) | collective-permute-done | bytes 262176 | tf_op jit(solution)/shard_map/ppermute | solution.py:463
  59.0 1.3 collective-permute-done.24.refs_1_
  62.6 1.6 collective-permute-start.26
  64.8 7.2 %expert.6 = (bf16[128,2048]{1,0:T(8,128)(2,1)S(1)}, bf16[128,2048]{1,0:T(8,128)(2,1)S(1)}, bf16[256,2048]{1,0:T(8,128)(2,1)S(1)}) custom-call(f32[1,2048]{1,0:T(1,128)S(1)} %bitcast.30, bf16[5,144,256]{2,1,0:T(8,128)(2,1)S(1)} %get-tuple-element.133.pick_ref, bf16[5,256,144]{2,1,0:T(8,128)(2,1)S(1)} %get-tuple-element.134.put_ref, ...), custom_call_target="tpu_custom_call" | custom-call | flops 1660944384 | bytes 8388608 | tf_op jit(solution)/shard_map/expert/pallas_call | solution.py:290
  72.0 4.0 %collective-permute-done.27.refs_2_ = bf16[128,2048]{1,0:T(8,128)(2,1)S(1)} collective-permute-done((bf16[128,2048]{1,0:T(8,128)(2,1)S(1)}, bf16[128,2048]{1,0:T(8,128)(2,1)S(1)}, u32[]{:S(2)}, u32[]{:S(2)}) %collective-permute-start.27) | collective-permute-done | bytes 524320 | tf_op jit(solution)/shard_map/ppermute | solution.py:466
  76.3 2.2 %collective-permute-done.31.refs_1_ = bf16[128,2048]{1,0:T(8,128)(2,1)S(1)} collective-permute-done((bf16[128,2048]{1,0:T(8,128)(2,1)S(1)}, bf16[128,2048]{1,0:T(8,128)(2,1)S(1)}, u32[]{:S(2)}, u32[]{:S(2)}) %collective-permute-start.31) | collective-permute-done | bytes 524320 | tf_op jit(solution)/shard_map/ppermute | solution.py:477
  79.0 1.5 collective-permute-start.32
  81.2 7.2 %expert.7 = (bf16[128,2048]{1,0:T(8,128)(2,1)S(1)}, bf16[128,2048]{1,0:T(8,128)(2,1)S(1)}, bf16[256,2048]{1,0:T(8,128)(2,1)S(1)}) custom-call(f32[1,2048]{1,0:T(1,128)S(1)} %bitcast.31, bf16[5,144,256]{2,1,0:T(8,128)(2,1)S(1)} %get-tuple-element.133.pick_ref, bf16[5,256,144]{2,1,0:T(8,128)(2,1)S(1)} %get-tuple-element.134.put_ref, ...), custom_call_target="tpu_custom_call" | custom-call | flops 1660944384 | bytes 8388608 | tf_op jit(solution)/shard_map/expert/pallas_call | solution.py:290
  88.4 4.5 %collective-permute-done.32.refs_0_ = bf16[128,2048]{1,0:T(8,128)(2,1)S(1)} collective-permute-done((bf16[128,2048]{1,0:T(8,128)(2,1)S(1)}, bf16[128,2048]{1,0:T(8,128)(2,1)S(1)}, u32[]{:S(2)}, u32[]{:S(2)}) %collective-permute-start.32) | collective-permute-done | bytes 524320 | tf_op jit(solution)/shard_map/ppermute | solution.py:463
  92.9 1.2 collective-permute-done.33.refs_2_
  94.7 1.5 collective-permute-start.37
  96.8 0.8 collective-permute-done.39.refs_1_
  97.5 0.7 collective-permute-done.40.refs_3_
  98.3 7.2 %expert.8 = (bf16[128,2048]{1,0:T(8,128)(2,1)S(1)}, bf16[128,2048]{1,0:T(8,128)(2,1)S(1)}, bf16[256,2048]{1,0:T(8,128)(2,1)S(1)}) custom-call(f32[1,2048]{1,0:T(1,128)S(1)} %bitcast.32, bf16[3,144,256]{2,1,0:T(8,128)(2,1)S(1)} %get-tuple-element.161.pick_ref, bf16[3,256,144]{2,1,0:T(8,128)(2,1)S(1)} %get-tuple-element.162.put_ref, ...), custom_call_target="tpu_custom_call" | custom-call | flops 1660944384 | bytes 8388608 | tf_op jit(solution)/shard_map/expert/pallas_call | solution.py:290
  106.2 2.4 %collective-permute-done.43.refs_2_ = bf16[64,2048]{1,0:T(8,128)(2,1)S(1)} collective-permute-done((bf16[64,2048]{1,0:T(8,128)(2,1)S(1)}, bf16[64,2048]{1,0:T(8,128)(2,1)S(1)}, u32[]{:S(2)}, u32[]{:S(2)}) %collective-permute-start.43) | collective-permute-done | bytes 262176 | tf_op jit(solution)/shard_map/ppermute | solution.py:469
  109.0 4.2 %expert.9 = (bf16[128,2048]{1,0:T(8,128)(2,1)S(1)}, bf16[128,2048]{1,0:T(8,128)(2,1)S(1)}) custom-call(f32[1,2048]{1,0:T(1,128)S(1)} %bitcast.33, bf16[3,144,256]{2,1,0:T(8,128)(2,1)S(1)} %get-tuple-element.161.pick_ref, bf16[3,256,144]{2,1,0:T(8,128)(2,1)S(1)} %get-tuple-element.162.put_ref, f32[3,144,1]{2,1,0:T(8,128)S(1)} %get-tuple-element.163.factor_ref, ...), custom_call_target="tpu_custom_call" | custom-call | flops 830472192 | bytes 4194304 | tf_op jit(solution)/shard_map/expert/pallas_call | solution.py:290
  113.4 1.8 %collective-permute-done.45.refs_1_ = bf16[128,2048]{1,0:T(8,128)(2,1)S(1)} collective-permute-done((bf16[128,2048]{1,0:T(8,128)(2,1)S(1)}, bf16[128,2048]{1,0:T(8,128)(2,1)S(1)}, u32[]{:S(2)}, u32[]{:S(2)}) %collective-permute-start.45) | collective-permute-done | bytes 524320 | tf_op jit(solution)/shard_map/ppermute | solution.py:469
  115.9 1.6 collective-permute-start.48
  118.1 4.8 %shared.1 = (f32[128,2048]{1,0:T(8,128)S(1)}, bf16[128,2048]{1,0:T(8,128)(2,1)S(1)}) custom-call(f32[1,2048]{1,0:T(1,128)S(1)} %bitcast.34, bf16[704,2048]{1,0:T(8,128)(2,1)} %bitcast.37, bf16[704,2048]{1,0:T(8,128)(2,1)} %bitcast.38, bf16[704,2048]{1,0:T(8,128)(2,1)} %bitcast.39, bf16[128,2048]{1,0:T(8,128)(2,1)S(1)} %weave.3.refs_0_.refs_1_, ...), custom_call_target="tpu_custom_call" | custom-call | flops 4429185024 | bytes 10747904 | tf_op jit(solution)/shard_map/shared/pallas_call | solution.py:351
  123.6 1.6 collective-permute-start.53
  125.9 1.6 collective-permute-start.51
  127.5 2.6 %collective-permute-done.47.refs_2_ = bf16[64,2048]{1,0:T(8,128)(2,1)S(1)} collective-permute-done((bf16[64,2048]{1,0:T(8,128)(2,1)S(1)}, bf16[64,2048]{1,0:T(8,128)(2,1)S(1)}, u32[]{:S(2)}, u32[]{:S(2)}) %collective-permute-start.47) | collective-permute-done | bytes 262176 | tf_op jit(solution)/shard_map/ppermute | solution.py:466
  130.7 2.1 %collective-permute-done.53.refs_2_ = bf16[64,2048]{1,0:T(8,128)(2,1)S(1)} collective-permute-done((bf16[64,2048]{1,0:T(8,128)(2,1)S(1)}, bf16[64,2048]{1,0:T(8,128)(2,1)S(1)}, u32[]{:S(2)}, u32[]{:S(2)}) %collective-permute-start.53) | collective-permute-done | bytes 262176 | tf_op jit(solution)/shard_map/ppermute | solution.py:463
  132.9 1.6 collective-permute-start.56
  134.5 1.2 collective-permute-done.52.refs_2_
  136.3 2.1 %collective-permute-done.51.refs_2_ = bf16[64,2048]{1,0:T(8,128)(2,1)S(1)} collective-permute-done((bf16[64,2048]{1,0:T(8,128)(2,1)S(1)}, bf16[64,2048]{1,0:T(8,128)(2,1)S(1)}, u32[]{:S(2)}, u32[]{:S(2)}) %collective-permute-start.51) | collective-permute-done | bytes 262176 | tf_op jit(solution)/shard_map/ppermute | solution.py:463
  138.5 1.6 collective-permute-start.58
  140.4 0.9 collective-permute-done.50.refs_2_
  141.4 2.6 %collective-permute-done.56.refs_2_ = bf16[64,2048]{1,0:T(8,128)(2,1)S(1)} collective-permute-done((bf16[64,2048]{1,0:T(8,128)(2,1)S(1)}, bf16[64,2048]{1,0:T(8,128)(2,1)S(1)}, u32[]{:S(2)}, u32[]{:S(2)}) %collective-permute-start.56) | collective-permute-done | bytes 262176 | tf_op jit(solution)/shard_map/ppermute | solution.py:463
  144.2 2.0 %collective-permute-done.55.refs_2_ = bf16[64,2048]{1,0:T(8,128)(2,1)S(1)} collective-permute-done((bf16[64,2048]{1,0:T(8,128)(2,1)S(1)}, bf16[64,2048]{1,0:T(8,128)(2,1)S(1)}, u32[]{:S(2)}, u32[]{:S(2)}) %collective-permute-start.55) | collective-permute-done | bytes 262176 | tf_op jit(solution)/shard_map/ppermute | solution.py:466
  146.2 1.4 collective-permute-done.58.refs_2_
  147.8 1.6 collective-permute-start.59
  149.8 1.6 collective-permute-start.60
  151.9 5.1 %collective-permute-done.59.refs_2_ = bf16[64,2048]{1,0:T(8,128)(2,1)S(1)} collective-permute-done((bf16[64,2048]{1,0:T(8,128)(2,1)S(1)}, bf16[64,2048]{1,0:T(8,128)(2,1)S(1)}, u32[]{:S(2)}, u32[]{:S(2)}) %collective-permute-start.59) | collective-permute-done | bytes 262176 | tf_op jit(solution)/shard_map/ppermute | solution.py:463
  156.9 1.3 collective-permute-done.57.refs_1_
  158.2 1.5 collective-permute-done.60.refs_3_
  159.7 1.3 collective-permute-done.54.refs_0_
  161.0 0.9 final.1
  (106 shorter events, 21.5 us)
Async XLA Ops:
  0.1 52.7 %copy-start.1 = (bf16[1,1408,2048]{2,1,0:T(8,128)(2,1)S(1)}, bf16[1,1408,2048]{2,1,0:T(8,128)(2,1)}, u32[]{:S(2)}) copy-start(bf16[1,1408,2048]{2,1,0:T(8,128)(2,1)} %param.21) | copy-start | bytes 17301508
  2.5 26.8 %collective-permute-start.13 = (bf16[128,3072]{1,0:T(8,128)(2,1)S(1)}, bf16[128,3072]{1,0:T(8,128)(2,1)S(1)}, u32[]{:S(2)}, u32[]{:S(2)}) collective-permute-start(bf16[128,3072]{1,0:T(8,128)(2,1)S(1)} %get-tuple-element.98), channel_id=1, source_target_pairs={{0,16},{1,17},{2,18},{3,19},{4,20},{5,21},{6,22},{7,23},{8,24},{9,... | collective-permute-start | bytes 2359304 | tf_op jit(solution)/shard_map/ppermute | solution.py:477
  5.5 2.0 %collective-permute-start.3 = (bf16[144,512]{1,0:T(8,128)(2,1)S(1)}, bf16[144,512]{1,0:T(8,128)(2,1)S(1)}, u32[]{:S(2)}, u32[]{:S(2)}) collective-permute-start(bf16[144,512]{1,0:T(8,128)(2,1)S(1)} %get-tuple-element.97), channel_id=1, source_target_pairs={{0,1},{1,0},{2,3},{3,2},{4,5},{5,4},{6,7},{7,6},{8,9},{9,8},{10,11... | collective-permute-start | bytes 442376 | tf_op jit(solution)/shard_map/ppermute | solution.py:469
  5.5 6.6 %collective-permute-start = (bf16[144,512]{1,0:T(8,128)(2,1)S(1)}, bf16[144,512]{1,0:T(8,128)(2,1)S(1)}, u32[]{:S(2)}, u32[]{:S(2)}) collective-permute-start(bf16[144,512]{1,0:T(8,128)(2,1)S(1)} %get-tuple-element.112.refs_4_.refs_0_), channel_id=1, source_target_pairs={{0,4},{1,5},{4,8},{5,9},{8,12},{9,13},{12,14},{13,15},{14,10},{15,... | collective-permute-start | bytes 442376 | tf_op jit(solution)/shard_map/ppermute | solution.py:463
  7.0 6.7 %collective-permute-start.7 = (bf16[144,512]{1,0:T(8,128)(2,1)S(1)}, bf16[144,512]{1,0:T(8,128)(2,1)S(1)}, u32[]{:S(2)}, u32[]{:S(2)}) collective-permute-start(bf16[144,512]{1,0:T(8,128)(2,1)S(1)} %get-tuple-element.112.refs_4_.refs_0_), channel_id=1, source_target_pairs={{4,0},{5,1},{8,4},{9,5},{12,8},{13,9},{14,12},{15,13},{10,14},{11,... | collective-permute-start | bytes 442376 | tf_op jit(solution)/shard_map/ppermute | solution.py:466
  7.5 9.4 %collective-permute-start.10 = (bf16[144,512]{1,0:T(8,128)(2,1)S(1)}, bf16[144,512]{1,0:T(8,128)(2,1)S(1)}, u32[]{:S(2)}, u32[]{:S(2)}) collective-permute-start(bf16[144,512]{1,0:T(8,128)(2,1)S(1)} %collective-permute-done.3.refs_5_.refs_1_), channel_id=1, source_target_pairs={{4,0},{5,1},{8,4},{9,5},{12,8},{13,9},{14,12},{15,13},{10,14},{11,... | collective-permute-start | bytes 442376 | tf_op jit(solution)/shard_map/ppermute | solution.py:466
  9.0 8.3 %collective-permute-start.4 = (bf16[144,512]{1,0:T(8,128)(2,1)S(1)}, bf16[144,512]{1,0:T(8,128)(2,1)S(1)}, u32[]{:S(2)}, u32[]{:S(2)}) collective-permute-start(bf16[144,512]{1,0:T(8,128)(2,1)S(1)} %collective-permute-done.3.refs_5_.refs_1_), channel_id=1, source_target_pairs={{0,4},{1,5},{4,8},{5,9},{8,12},{9,13},{12,14},{13,15},{14,10},{15,... | collective-permute-start | bytes 442376 | tf_op jit(solution)/shard_map/ppermute | solution.py:463
  12.1 6.8 %collective-permute-start.1 = (bf16[144,512]{1,0:T(8,128)(2,1)S(1)}, bf16[144,512]{1,0:T(8,128)(2,1)S(1)}, u32[]{:S(2)}, u32[]{:S(2)}) collective-permute-start(bf16[144,512]{1,0:T(8,128)(2,1)S(1)} %collective-permute-done.refs_6_.refs_2_), channel_id=1, source_target_pairs={{0,4},{1,5},{4,8},{5,9},{8,12},{9,13},{12,14},{13,15},{14,10},{15,... | collective-permute-start | bytes 442376 | tf_op jit(solution)/shard_map/ppermute | solution.py:463
  13.7 6.8 %collective-permute-start.8 = (bf16[144,512]{1,0:T(8,128)(2,1)S(1)}, bf16[144,512]{1,0:T(8,128)(2,1)S(1)}, u32[]{:S(2)}, u32[]{:S(2)}) collective-permute-start(bf16[144,512]{1,0:T(8,128)(2,1)S(1)} %collective-permute-done.7.refs_8_.refs_4_), channel_id=1, source_target_pairs={{4,0},{5,1},{8,4},{9,5},{12,8},{13,9},{14,12},{15,13},{10,14},{11,... | collective-permute-start | bytes 442376 | tf_op jit(solution)/shard_map/ppermute | solution.py:466
  16.9 6.8 %collective-permute-start.11 = (bf16[144,512]{1,0:T(8,128)(2,1)S(1)}, bf16[144,512]{1,0:T(8,128)(2,1)S(1)}, u32[]{:S(2)}, u32[]{:S(2)}) collective-permute-start(bf16[144,512]{1,0:T(8,128)(2,1)S(1)} %collective-permute-done.10.refs_9_.refs_5_), channel_id=1, source_target_pairs={{4,0},{5,1},{8,4},{9,5},{12,8},{13,9},{14,12},{15,13},{10,14},{11,... | collective-permute-start | bytes 442376 | tf_op jit(solution)/shard_map/ppermute | solution.py:466
  17.3 6.8 %collective-permute-start.5 = (bf16[144,512]{1,0:T(8,128)(2,1)S(1)}, bf16[144,512]{1,0:T(8,128)(2,1)S(1)}, u32[]{:S(2)}, u32[]{:S(2)}) collective-permute-start(bf16[144,512]{1,0:T(8,128)(2,1)S(1)} %collective-permute-done.4.refs_7_.refs_3_), channel_id=1, source_target_pairs={{0,4},{1,5},{4,8},{5,9},{8,12},{9,13},{12,14},{13,15},{14,10},{15,... | collective-permute-start | bytes 442376 | tf_op jit(solution)/shard_map/ppermute | solution.py:463
  18.9 6.8 %collective-permute-start.2 = (bf16[144,512]{1,0:T(8,128)(2,1)S(1)}, bf16[144,512]{1,0:T(8,128)(2,1)S(1)}, u32[]{:S(2)}, u32[]{:S(2)}) collective-permute-start(bf16[144,512]{1,0:T(8,128)(2,1)S(1)} %collective-permute-done.1.refs_10_.refs_6_), channel_id=1, source_target_pairs={{0,4},{1,5},{4,8},{5,9},{8,12},{9,13},{12,14},{13,15},{14,10},{15,... | collective-permute-start | bytes 442376 | tf_op jit(solution)/shard_map/ppermute | solution.py:463
  20.5 6.7 %collective-permute-start.9 = (bf16[144,512]{1,0:T(8,128)(2,1)S(1)}, bf16[144,512]{1,0:T(8,128)(2,1)S(1)}, u32[]{:S(2)}, u32[]{:S(2)}) collective-permute-start(bf16[144,512]{1,0:T(8,128)(2,1)S(1)} %collective-permute-done.8.refs_12_.refs_8_), channel_id=1, source_target_pairs={{4,0},{5,1},{8,4},{9,5},{12,8},{13,9},{14,12},{15,13},{10,14},{11,... | collective-permute-start | bytes 442376 | tf_op jit(solution)/shard_map/ppermute | solution.py:466
  23.7 5.1 %collective-permute-start.12 = (bf16[144,512]{1,0:T(8,128)(2,1)S(1)}, bf16[144,512]{1,0:T(8,128)(2,1)S(1)}, u32[]{:S(2)}, u32[]{:S(2)}) collective-permute-start(bf16[144,512]{1,0:T(8,128)(2,1)S(1)} %collective-permute-done.11.refs_13_.refs_9_), channel_id=1, source_target_pairs={{4,0},{5,1},{8,4},{9,5},{12,8},{13,9},{14,12},{15,13},{10,14},{11,... | collective-permute-start | bytes 442376 | tf_op jit(solution)/shard_map/ppermute | solution.py:466
  24.1 5.1 %collective-permute-start.6 = (bf16[144,512]{1,0:T(8,128)(2,1)S(1)}, bf16[144,512]{1,0:T(8,128)(2,1)S(1)}, u32[]{:S(2)}, u32[]{:S(2)}) collective-permute-start(bf16[144,512]{1,0:T(8,128)(2,1)S(1)} %collective-permute-done.5.refs_11_.refs_7_), channel_id=1, source_target_pairs={{0,4},{1,5},{4,8},{5,9},{8,12},{9,13},{12,14},{13,15},{14,10},{15,... | collective-permute-start | bytes 442376 | tf_op jit(solution)/shard_map/ppermute | solution.py:463
  25.7 5.6 %collective-permute-start.14 = (bf16[128,3072]{1,0:T(8,128)(2,1)S(1)}, bf16[128,3072]{1,0:T(8,128)(2,1)S(1)}, u32[]{:S(2)}, u32[]{:S(2)}) collective-permute-start(bf16[128,3072]{1,0:T(8,128)(2,1)S(1)} %get-tuple-element.95.refs_0_), channel_id=1, source_target_pairs={{0,1},{1,0},{2,3},{3,2},{4,5},{5,4},{6,7},{7,6},{8,9},{9,8},{10,11... | collective-permute-start | bytes 2359304 | tf_op jit(solution)/shard_map/ppermute | solution.py:469
  29.3 2.3 %collective-permute-start.15 = (bf16[128,3072]{1,0:T(8,128)(2,1)S(1)}, bf16[128,3072]{1,0:T(8,128)(2,1)S(1)}, u32[]{:S(2)}, u32[]{:S(2)}) collective-permute-start(bf16[128,3072]{1,0:T(8,128)(2,1)S(1)} %collective-permute-done.13.refs_1_), channel_id=1, source_target_pairs={{0,1},{1,0},{2,3},{3,2},{4,5},{5,4},{6,7},{7,6},{8,9},{9,8},{10,11... | collective-permute-start | bytes 2359304 | tf_op jit(solution)/shard_map/ppermute | solution.py:469
  29.3 6.3 %collective-permute-start.16 = (bf16[144,512]{1,0:T(8,128)(2,1)S(1)}, bf16[144,512]{1,0:T(8,128)(2,1)S(1)}, u32[]{:S(2)}, u32[]{:S(2)}) collective-permute-start(bf16[144,512]{1,0:T(8,128)(2,1)S(1)} %collective-permute-done.2.refs_14_.refs_2_), channel_id=1, source_target_pairs={{0,4},{1,5},{4,8},{5,9},{8,12},{9,13},{12,14},{13,15},{14,10},{15,... | collective-permute-start | bytes 442376 | tf_op jit(solution)/shard_map/ppermute | solution.py:463
  30.9 6.0 %collective-permute-start.17 = (bf16[144,512]{1,0:T(8,128)(2,1)S(1)}, bf16[144,512]{1,0:T(8,128)(2,1)S(1)}, u32[]{:S(2)}, u32[]{:S(2)}) collective-permute-start(bf16[144,512]{1,0:T(8,128)(2,1)S(1)} %collective-permute-done.12.refs_17_.refs_5_), channel_id=1, source_target_pairs={{4,0},{5,1},{8,4},{9,5},{12,8},{13,9},{14,12},{15,13},{10,14},{11,... | collective-permute-start | bytes 442376 | tf_op jit(solution)/shard_map/ppermute | solution.py:466
  32.2 20.6 %slice-start = ((s8[5767168]{0:T(1024)(128)(4,1)}), s8[4194304]{0:T(1024)(128)(4,1)S(1)}, s32[]{:S(2)}) async-start(s8[5767168]{0:T(1024)(128)(4,1)} %bitcast.12), calls=%async_computation | async-start | bytes 8388608
  33.9 18.9 %slice-start.1 = ((s8[5767168]{0:T(1024)(128)(4,1)}), s8[1572864]{0:T(1024)(128)(4,1)S(1)}, s32[]{:S(2)}) async-start(s8[5767168]{0:T(1024)(128)(4,1)} %bitcast.12), calls=%async_computation.1 | async-start | bytes 3145728
  37.7 1.4 collective-permute-start.18
  39.7 9.0 %collective-permute-start.19 = (bf16[128,1024]{1,0:T(8,128)(2,1)S(1)}, bf16[128,1024]{1,0:T(8,128)(2,1)S(1)}, u32[]{:S(2)}, u32[]{:S(2)}) collective-permute-start(bf16[128,1024]{1,0:T(8,128)(2,1)S(1)} %beside.2.refs_0_), channel_id=1, source_target_pairs={{0,4},{1,5},{4,8},{5,9},{8,12},{9,13},{12,14},{13,15},{14,10},{15,... | collective-permute-start | bytes 786440 | tf_op jit(solution)/shard_map/ppermute | solution.py:463
  41.3 8.1 %collective-permute-start.20 = (bf16[128,1024]{1,0:T(8,128)(2,1)S(1)}, bf16[128,1024]{1,0:T(8,128)(2,1)S(1)}, u32[]{:S(2)}, u32[]{:S(2)}) collective-permute-start(bf16[128,1024]{1,0:T(8,128)(2,1)S(1)} %beside.2.refs_0_), channel_id=1, source_target_pairs={{4,0},{5,1},{8,4},{9,5},{12,8},{13,9},{14,12},{15,13},{10,14},{11,... | collective-permute-start | bytes 786440 | tf_op jit(solution)/shard_map/ppermute | solution.py:466
  41.8 6.4 %collective-permute-start.21 = (bf16[128,512]{1,0:T(8,128)(2,1)S(1)}, bf16[128,512]{1,0:T(8,128)(2,1)S(1)}, u32[]{:S(2)}, u32[]{:S(2)}) collective-permute-start(bf16[128,512]{1,0:T(8,128)(2,1)S(1)} %get-tuple-element.110), channel_id=1, source_target_pairs={{0,16},{1,17},{2,18},{3,19},{4,20},{5,21},{6,22},{7,23},{8,24},{9,... | collective-permute-start | bytes 393224 | tf_op jit(solution)/shard_map/ppermute | solution.py:477
  42.3 5.9 %collective-permute-start.22 = (bf16[128,512]{1,0:T(8,128)(2,1)S(1)}, bf16[128,512]{1,0:T(8,128)(2,1)S(1)}, u32[]{:S(2)}, u32[]{:S(2)}) collective-permute-start(bf16[128,512]{1,0:T(8,128)(2,1)S(1)} %get-tuple-element.111), channel_id=1, source_target_pairs={{0,17},{1,16},{2,19},{3,18},{4,21},{5,20},{6,23},{7,22},{8,25},{9,... | collective-permute-start | bytes 393224 | tf_op jit(solution)/shard_map/ppermute | solution.py:477
  50.0 2.8 %collective-permute-start.25 = (bf16[128,2048]{1,0:T(8,128)(2,1)S(1)}, bf16[128,2048]{1,0:T(8,128)(2,1)S(1)}, u32[]{:S(2)}, u32[]{:S(2)}) collective-permute-start(bf16[128,2048]{1,0:T(8,128)(2,1)S(1)} %weave.3.refs_0_.refs_1_), channel_id=1, source_target_pairs={{0,1},{1,0},{2,3},{3,2},{4,5},{5,4},{6,7},{7,6},{8,9},{9,8},{10,11... | collective-permute-start | bytes 1572872 | tf_op jit(solution)/shard_map/ppermute | solution.py:469
  50.8 8.3 %collective-permute-start.23 = (bf16[128,1024]{1,0:T(8,128)(2,1)S(1)}, bf16[128,1024]{1,0:T(8,128)(2,1)S(1)}, u32[]{:S(2)}, u32[]{:S(2)}) collective-permute-start(bf16[128,1024]{1,0:T(8,128)(2,1)S(1)} %beside.3.refs_1_), channel_id=1, source_target_pairs={{0,4},{1,5},{4,8},{5,9},{8,12},{9,13},{12,14},{13,15},{14,10},{15,... | collective-permute-start | bytes 786440 | tf_op jit(solution)/shard_map/ppermute | solution.py:463
  52.3 8.0 %collective-permute-start.24 = (bf16[128,1024]{1,0:T(8,128)(2,1)S(1)}, bf16[128,1024]{1,0:T(8,128)(2,1)S(1)}, u32[]{:S(2)}, u32[]{:S(2)}) collective-permute-start(bf16[128,1024]{1,0:T(8,128)(2,1)S(1)} %beside.3.refs_1_), channel_id=1, source_target_pairs={{4,0},{5,1},{8,4},{9,5},{12,8},{13,9},{14,12},{15,13},{10,14},{11,... | collective-permute-start | bytes 786440 | tf_op jit(solution)/shard_map/ppermute | solution.py:466
  60.9 3.3 %collective-permute-start.29 = (bf16[128,2048]{1,0:T(8,128)(2,1)S(1)}, bf16[128,2048]{1,0:T(8,128)(2,1)S(1)}, u32[]{:S(2)}, u32[]{:S(2)}) collective-permute-start(bf16[128,2048]{1,0:T(8,128)(2,1)S(1)} %weave.5.refs_2_), channel_id=1, source_target_pairs={{0,1},{1,0},{2,3},{3,2},{4,5},{5,4},{6,7},{7,6},{8,9},{9,8},{10,11... | collective-permute-start | bytes 1572872 | tf_op jit(solution)/shard_map/ppermute | solution.py:469
  61.6 2.6 %collective-permute-start.28 = (bf16[128,2048]{1,0:T(8,128)(2,1)S(1)}, bf16[128,2048]{1,0:T(8,128)(2,1)S(1)}, u32[]{:S(2)}, u32[]{:S(2)}) collective-permute-start(bf16[128,2048]{1,0:T(8,128)(2,1)S(1)} %weave.4.refs_0_), channel_id=1, source_target_pairs={{0,1},{1,0},{2,3},{3,2},{4,5},{5,4},{6,7},{7,6},{8,9},{9,8},{10,11... | collective-permute-start | bytes 1572872 | tf_op jit(solution)/shard_map/ppermute | solution.py:469
  62.1 13.9 %collective-permute-start.27 = (bf16[128,2048]{1,0:T(8,128)(2,1)S(1)}, bf16[128,2048]{1,0:T(8,128)(2,1)S(1)}, u32[]{:S(2)}, u32[]{:S(2)}) collective-permute-start(bf16[128,2048]{1,0:T(8,128)(2,1)S(1)} %weave.5.refs_2_), channel_id=1, source_target_pairs={{4,0},{5,1},{8,4},{9,5},{12,8},{13,9},{14,12},{15,13},{10,14},{11,... | collective-permute-start | bytes 1572872 | tf_op jit(solution)/shard_map/ppermute | solution.py:466
  62.6 13.7 %collective-permute-start.26 = (bf16[128,2048]{1,0:T(8,128)(2,1)S(1)}, bf16[128,2048]{1,0:T(8,128)(2,1)S(1)}, u32[]{:S(2)}, u32[]{:S(2)}) collective-permute-start(bf16[128,2048]{1,0:T(8,128)(2,1)S(1)} %weave.4.refs_0_), channel_id=1, source_target_pairs={{0,4},{1,5},{4,8},{5,9},{8,12},{9,13},{12,14},{13,15},{14,10},{15,... | collective-permute-start | bytes 1572872 | tf_op jit(solution)/shard_map/ppermute | solution.py:463
  64.2 12.1 %collective-permute-start.30 = (bf16[128,2048]{1,0:T(8,128)(2,1)S(1)}, bf16[128,2048]{1,0:T(8,128)(2,1)S(1)}, u32[]{:S(2)}, u32[]{:S(2)}) collective-permute-start(bf16[128,2048]{1,0:T(8,128)(2,1)S(1)} %get-tuple-element.147), channel_id=1, source_target_pairs={{0,1},{1,0},{2,3},{3,2},{4,5},{5,4},{6,7},{7,6},{8,9},{9,8},{10,11... | collective-permute-start | bytes 1572872 | tf_op jit(solution)/shard_map/ppermute | solution.py:469
  64.2 14.3 %collective-permute-start.31 = (bf16[128,2048]{1,0:T(8,128)(2,1)S(1)}, bf16[128,2048]{1,0:T(8,128)(2,1)S(1)}, u32[]{:S(2)}, u32[]{:S(2)}) collective-permute-start(bf16[128,2048]{1,0:T(8,128)(2,1)S(1)} %weave.3.refs_0_.refs_1_), channel_id=1, source_target_pairs={{0,16},{1,17},{2,18},{3,19},{4,20},{5,21},{6,22},{7,23},{8,24},{9,... | collective-permute-start | bytes 1572872 | tf_op jit(solution)/shard_map/ppermute | solution.py:477
  76.3 17.8 %collective-permute-start.36 = (bf16[256,2048]{1,0:T(8,128)(2,1)S(1)}, bf16[256,2048]{1,0:T(8,128)(2,1)S(1)}, u32[]{:S(2)}, u32[]{:S(2)}) collective-permute-start(bf16[256,2048]{1,0:T(8,128)(2,1)S(1)} %get-tuple-element.158), channel_id=1, source_target_pairs={{0,1},{1,0},{2,3},{3,2},{4,5},{5,4},{6,7},{7,6},{8,9},{9,8},{10,11... | collective-permute-start | bytes 3145736 | tf_op jit(solution)/shard_map/ppermute | solution.py:469
  78.5 2.5 %collective-permute-start.34 = (bf16[128,2048]{1,0:T(8,128)(2,1)S(1)}, bf16[128,2048]{1,0:T(8,128)(2,1)S(1)}, u32[]{:S(2)}, u32[]{:S(2)}) collective-permute-start(bf16[128,2048]{1,0:T(8,128)(2,1)S(1)} %collective-permute-done.26.refs_0_), channel_id=1, source_target_pairs={{0,1},{1,0},{2,3},{3,2},{4,5},{5,4},{6,7},{7,6},{8,9},{9,8},{10,11... | collective-permute-start | bytes 1572872 | tf_op jit(solution)/shard_map/ppermute | solution.py:469
  78.5 2.7 %collective-permute-start.35 = (bf16[128,2048]{1,0:T(8,128)(2,1)S(1)}, bf16[128,2048]{1,0:T(8,128)(2,1)S(1)}, u32[]{:S(2)}, u32[]{:S(2)}) collective-permute-start(bf16[128,2048]{1,0:T(8,128)(2,1)S(1)} %collective-permute-done.27.refs_2_), channel_id=1, source_target_pairs={{0,1},{1,0},{2,3},{3,2},{4,5},{5,4},{6,7},{7,6},{8,9},{9,8},{10,11... | collective-permute-start | bytes 1572872 | tf_op jit(solution)/shard_map/ppermute | solution.py:469
  79.0 13.8 %collective-permute-start.32 = (bf16[128,2048]{1,0:T(8,128)(2,1)S(1)}, bf16[128,2048]{1,0:T(8,128)(2,1)S(1)}, u32[]{:S(2)}, u32[]{:S(2)}) collective-permute-start(bf16[128,2048]{1,0:T(8,128)(2,1)S(1)} %collective-permute-done.26.refs_0_), channel_id=1, source_target_pairs={{0,4},{1,5},{4,8},{5,9},{8,12},{9,13},{12,14},{13,15},{14,10},{15,... | collective-permute-start | bytes 1572872 | tf_op jit(solution)/shard_map/ppermute | solution.py:463
  80.6 13.6 %collective-permute-start.33 = (bf16[128,2048]{1,0:T(8,128)(2,1)S(1)}, bf16[128,2048]{1,0:T(8,128)(2,1)S(1)}, u32[]{:S(2)}, u32[]{:S(2)}) collective-permute-start(bf16[128,2048]{1,0:T(8,128)(2,1)S(1)} %collective-permute-done.27.refs_2_), channel_id=1, source_target_pairs={{4,0},{5,1},{8,4},{9,5},{12,8},{13,9},{14,12},{15,13},{10,14},{11,... | collective-permute-start | bytes 1572872 | tf_op jit(solution)/shard_map/ppermute | solution.py:466
  94.1 11.4 %collective-permute-start.41 = (bf16[256,2048]{1,0:T(8,128)(2,1)S(1)}, bf16[256,2048]{1,0:T(8,128)(2,1)S(1)}, u32[]{:S(2)}, u32[]{:S(2)}) collective-permute-start(bf16[256,2048]{1,0:T(8,128)(2,1)S(1)} %get-tuple-element.167), channel_id=1, source_target_pairs={{0,1},{1,0},{2,3},{3,2},{4,5},{5,4},{6,7},{7,6},{8,9},{9,8},{10,11... | collective-permute-start | bytes 3145736 | tf_op jit(solution)/shard_map/ppermute | solution.py:469
  94.1 3.4 %collective-permute-start.39 = (bf16[128,2048]{1,0:T(8,128)(2,1)S(1)}, bf16[128,2048]{1,0:T(8,128)(2,1)S(1)}, u32[]{:S(2)}, u32[]{:S(2)}) collective-permute-start(bf16[128,2048]{1,0:T(8,128)(2,1)S(1)} %collective-permute-done.32.refs_0_), channel_id=1, source_target_pairs={{0,1},{1,0},{2,3},{3,2},{4,5},{5,4},{6,7},{7,6},{8,9},{9,8},{10,11... | collective-permute-start | bytes 1572872 | tf_op jit(solution)/shard_map/ppermute | solution.py:469
  94.6 3.6 %collective-permute-start.40 = (bf16[128,2048]{1,0:T(8,128)(2,1)S(1)}, bf16[128,2048]{1,0:T(8,128)(2,1)S(1)}, u32[]{:S(2)}, u32[]{:S(2)}) collective-permute-start(bf16[128,2048]{1,0:T(8,128)(2,1)S(1)} %collective-permute-done.33.refs_2_), channel_id=1, source_target_pairs={{0,1},{1,0},{2,3},{3,2},{4,5},{5,4},{6,7},{7,6},{8,9},{9,8},{10,11... | collective-permute-start | bytes 1572872 | tf_op jit(solution)/shard_map/ppermute | solution.py:469
  94.7 10.8 %collective-permute-start.37 = (bf16[64,2048]{1,0:T(8,128)(2,1)S(1)}, bf16[64,2048]{1,0:T(8,128)(2,1)S(1)}, u32[]{:S(2)}, u32[]{:S(2)}) collective-permute-start(bf16[64,2048]{1,0:T(8,128)(2,1)S(1)} %slice.6), channel_id=1, source_target_pairs={{0,4},{1,5},{4,8},{5,9},{8,12},{9,13},{12,14},{13,15},{14,10},{15,... | collective-permute-start | bytes 786440 | tf_op jit(solution)/shard_map/ppermute | solution.py:463
  96.2 9.3 %collective-permute-start.38 = (bf16[64,2048]{1,0:T(8,128)(2,1)S(1)}, bf16[64,2048]{1,0:T(8,128)(2,1)S(1)}, u32[]{:S(2)}, u32[]{:S(2)}) collective-permute-start(bf16[64,2048]{1,0:T(8,128)(2,1)S(1)} %slice.7), channel_id=1, source_target_pairs={{4,0},{5,1},{8,4},{9,5},{12,8},{13,9},{14,12},{15,13},{10,14},{11,... | collective-permute-start | bytes 786440 | tf_op jit(solution)/shard_map/ppermute | solution.py:466
  105.5 11.9 %collective-permute-start.42 = (bf16[256,2048]{1,0:T(8,128)(2,1)S(1)}, bf16[256,2048]{1,0:T(8,128)(2,1)S(1)}, u32[]{:S(2)}, u32[]{:S(2)}) collective-permute-start(bf16[256,2048]{1,0:T(8,128)(2,1)S(1)} %get-tuple-element.169), channel_id=1, source_target_pairs={{0,1},{1,0},{2,3},{3,2},{4,5},{5,4},{6,7},{7,6},{8,9},{9,8},{10,11... | collective-permute-start | bytes 3145736 | tf_op jit(solution)/shard_map/ppermute | solution.py:469
  105.7 2.9 %collective-permute-start.43 = (bf16[64,2048]{1,0:T(8,128)(2,1)S(1)}, bf16[64,2048]{1,0:T(8,128)(2,1)S(1)}, u32[]{:S(2)}, u32[]{:S(2)}) collective-permute-start(bf16[64,2048]{1,0:T(8,128)(2,1)S(1)} %collective-permute-done.37.refs_0_), channel_id=1, source_target_pairs={{0,1},{1,0},{2,3},{3,2},{4,5},{5,4},{6,7},{7,6},{8,9},{9,8},{10,11... | collective-permute-start | bytes 786440 | tf_op jit(solution)/shard_map/ppermute | solution.py:469
  106.1 2.9 %collective-permute-start.44 = (bf16[64,2048]{1,0:T(8,128)(2,1)S(1)}, bf16[64,2048]{1,0:T(8,128)(2,1)S(1)}, u32[]{:S(2)}, u32[]{:S(2)}) collective-permute-start(bf16[64,2048]{1,0:T(8,128)(2,1)S(1)} %collective-permute-done.38.refs_1_), channel_id=1, source_target_pairs={{0,1},{1,0},{2,3},{3,2},{4,5},{5,4},{6,7},{7,6},{8,9},{9,8},{10,11... | collective-permute-start | bytes 786440 | tf_op jit(solution)/shard_map/ppermute | solution.py:469
  113.2 2.0 %collective-permute-start.45 = (bf16[128,2048]{1,0:T(8,128)(2,1)S(1)}, bf16[128,2048]{1,0:T(8,128)(2,1)S(1)}, u32[]{:S(2)}, u32[]{:S(2)}) collective-permute-start(bf16[128,2048]{1,0:T(8,128)(2,1)S(1)} %get-tuple-element.174), channel_id=1, source_target_pairs={{0,1},{1,0},{2,3},{3,2},{4,5},{5,4},{6,7},{7,6},{8,9},{9,8},{10,11... | collective-permute-start | bytes 1572872 | tf_op jit(solution)/shard_map/ppermute | solution.py:469
  115.3 9.9 %collective-permute-start.49 = (bf16[64,2048]{1,0:T(8,128)(2,1)S(1)}, bf16[64,2048]{1,0:T(8,128)(2,1)S(1)}, u32[]{:S(2)}, u32[]{:S(2)}) collective-permute-start(bf16[64,2048]{1,0:T(8,128)(2,1)S(1)} %add.23.refs_2_), channel_id=1, source_target_pairs={{4,0},{5,1},{8,4},{9,5},{12,8},{13,9},{14,12},{15,13},{10,14},{11,... | collective-permute-start | bytes 786440 | tf_op jit(solution)/shard_map/ppermute | solution.py:466
  115.9 9.9 %collective-permute-start.48 = (bf16[64,2048]{1,0:T(8,128)(2,1)S(1)}, bf16[64,2048]{1,0:T(8,128)(2,1)S(1)}, u32[]{:S(2)}, u32[]{:S(2)}) collective-permute-start(bf16[64,2048]{1,0:T(8,128)(2,1)S(1)} %add.24.refs_2_), channel_id=1, source_target_pairs={{0,4},{1,5},{4,8},{5,9},{8,12},{9,13},{12,14},{13,15},{14,10},{15,... | collective-permute-start | bytes 786440 | tf_op jit(solution)/shard_map/ppermute | solution.py:463
  117.5 12.6 %collective-permute-start.47 = (bf16[64,2048]{1,0:T(8,128)(2,1)S(1)}, bf16[64,2048]{1,0:T(8,128)(2,1)S(1)}, u32[]{:S(2)}, u32[]{:S(2)}) collective-permute-start(bf16[64,2048]{1,0:T(8,128)(2,1)S(1)} %add.25.refs_2_), channel_id=1, source_target_pairs={{4,0},{5,1},{8,4},{9,5},{12,8},{13,9},{14,12},{15,13},{10,14},{11,... | collective-permute-start | bytes 786440 | tf_op jit(solution)/shard_map/ppermute | solution.py:466
  123.0 17.2 %collective-permute-start.46 = (bf16[128,2048]{1,0:T(8,128)(2,1)S(1)}, bf16[128,2048]{1,0:T(8,128)(2,1)S(1)}, u32[]{:S(2)}, u32[]{:S(2)}) collective-permute-start(bf16[128,2048]{1,0:T(8,128)(2,1)S(1)} %get-tuple-element.178), channel_id=1, source_target_pairs={{0,16},{1,17},{2,18},{3,19},{4,20},{5,21},{6,22},{7,23},{8,24},{9,... | collective-permute-start | bytes 1572872 | tf_op jit(solution)/shard_map/ppermute | solution.py:477
  123.6 9.2 %collective-permute-start.53 = (bf16[64,2048]{1,0:T(8,128)(2,1)S(1)}, bf16[64,2048]{1,0:T(8,128)(2,1)S(1)}, u32[]{:S(2)}, u32[]{:S(2)}) collective-permute-start(bf16[64,2048]{1,0:T(8,128)(2,1)S(1)} %add.26.refs_2_), channel_id=1, source_target_pairs={{0,4},{1,5},{4,8},{5,9},{8,12},{9,13},{12,14},{13,15},{14,10},{15,... | collective-permute-start | bytes 786440 | tf_op jit(solution)/shard_map/ppermute | solution.py:463
  125.2 10.5 %collective-permute-start.52 = (bf16[64,2048]{1,0:T(8,128)(2,1)S(1)}, bf16[64,2048]{1,0:T(8,128)(2,1)S(1)}, u32[]{:S(2)}, u32[]{:S(2)}) collective-permute-start(bf16[64,2048]{1,0:T(8,128)(2,1)S(1)} %add.27.refs_3_), channel_id=1, source_target_pairs={{4,0},{5,1},{8,4},{9,5},{12,8},{13,9},{14,12},{15,13},{10,14},{11,... | collective-permute-start | bytes 786440 | tf_op jit(solution)/shard_map/ppermute | solution.py:466
  125.9 12.6 %collective-permute-start.51 = (bf16[64,2048]{1,0:T(8,128)(2,1)S(1)}, bf16[64,2048]{1,0:T(8,128)(2,1)S(1)}, u32[]{:S(2)}, u32[]{:S(2)}) collective-permute-start(bf16[64,2048]{1,0:T(8,128)(2,1)S(1)} %add.28.refs_3_), channel_id=1, source_target_pairs={{0,4},{1,5},{4,8},{5,9},{8,12},{9,13},{12,14},{13,15},{14,10},{15,... | collective-permute-start | bytes 786440 | tf_op jit(solution)/shard_map/ppermute | solution.py:463
  130.2 11.1 %collective-permute-start.50 = (bf16[64,2048]{1,0:T(8,128)(2,1)S(1)}, bf16[64,2048]{1,0:T(8,128)(2,1)S(1)}, u32[]{:S(2)}, u32[]{:S(2)}) collective-permute-start(bf16[64,2048]{1,0:T(8,128)(2,1)S(1)} %add.29.refs_3_), channel_id=1, source_target_pairs={{4,0},{5,1},{8,4},{9,5},{12,8},{13,9},{14,12},{15,13},{10,14},{11,... | collective-permute-start | bytes 786440 | tf_op jit(solution)/shard_map/ppermute | solution.py:466
  132.9 11.1 %collective-permute-start.56 = (bf16[64,2048]{1,0:T(8,128)(2,1)S(1)}, bf16[64,2048]{1,0:T(8,128)(2,1)S(1)}, u32[]{:S(2)}, u32[]{:S(2)}) collective-permute-start(bf16[64,2048]{1,0:T(8,128)(2,1)S(1)} %add.30.refs_3_), channel_id=1, source_target_pairs={{0,4},{1,5},{4,8},{5,9},{8,12},{9,13},{12,14},{13,15},{14,10},{15,... | collective-permute-start | bytes 786440 | tf_op jit(solution)/shard_map/ppermute | solution.py:463
  135.8 10.3 %collective-permute-start.55 = (bf16[64,2048]{1,0:T(8,128)(2,1)S(1)}, bf16[64,2048]{1,0:T(8,128)(2,1)S(1)}, u32[]{:S(2)}, u32[]{:S(2)}) collective-permute-start(bf16[64,2048]{1,0:T(8,128)(2,1)S(1)} %add.31.refs_3_), channel_id=1, source_target_pairs={{4,0},{5,1},{8,4},{9,5},{12,8},{13,9},{14,12},{15,13},{10,14},{11,... | collective-permute-start | bytes 786440 | tf_op jit(solution)/shard_map/ppermute | solution.py:466
  138.5 9.1 %collective-permute-start.58 = (bf16[64,2048]{1,0:T(8,128)(2,1)S(1)}, bf16[64,2048]{1,0:T(8,128)(2,1)S(1)}, u32[]{:S(2)}, u32[]{:S(2)}) collective-permute-start(bf16[64,2048]{1,0:T(8,128)(2,1)S(1)} %add.32.refs_3_), channel_id=1, source_target_pairs={{0,4},{1,5},{4,8},{5,9},{8,12},{9,13},{12,14},{13,15},{14,10},{15,... | collective-permute-start | bytes 786440 | tf_op jit(solution)/shard_map/ppermute | solution.py:463
  147.8 9.2 %collective-permute-start.59 = (bf16[64,2048]{1,0:T(8,128)(2,1)S(1)}, bf16[64,2048]{1,0:T(8,128)(2,1)S(1)}, u32[]{:S(2)}, u32[]{:S(2)}) collective-permute-start(bf16[64,2048]{1,0:T(8,128)(2,1)S(1)} %add.36), channel_id=1, source_target_pairs={{0,4},{1,5},{4,8},{5,9},{8,12},{9,13},{12,14},{13,15},{14,10},{15,... | collective-permute-start | bytes 786440 | tf_op jit(solution)/shard_map/ppermute | solution.py:463
  149.4 8.8 %collective-permute-start.57 = (bf16[64,2048]{1,0:T(8,128)(2,1)S(1)}, bf16[64,2048]{1,0:T(8,128)(2,1)S(1)}, u32[]{:S(2)}, u32[]{:S(2)}) collective-permute-start(bf16[64,2048]{1,0:T(8,128)(2,1)S(1)} %add.35.refs_3_), channel_id=1, source_target_pairs={{4,0},{5,1},{8,4},{9,5},{12,8},{13,9},{14,12},{15,13},{10,14},{11,... | collective-permute-start | bytes 786440 | tf_op jit(solution)/shard_map/ppermute | solution.py:466
  149.8 9.9 %collective-permute-start.60 = (bf16[64,2048]{1,0:T(8,128)(2,1)S(1)}, bf16[64,2048]{1,0:T(8,128)(2,1)S(1)}, u32[]{:S(2)}, u32[]{:S(2)}) collective-permute-start(bf16[64,2048]{1,0:T(8,128)(2,1)S(1)} %add.34.refs_3_), channel_id=1, source_target_pairs={{0,4},{1,5},{4,8},{5,9},{8,12},{9,13},{12,14},{13,15},{14,10},{15,... | collective-permute-start | bytes 786440 | tf_op jit(solution)/shard_map/ppermute | solution.py:463
  151.4 9.6 %collective-permute-start.54 = (bf16[64,2048]{1,0:T(8,128)(2,1)S(1)}, bf16[64,2048]{1,0:T(8,128)(2,1)S(1)}, u32[]{:S(2)}, u32[]{:S(2)}) collective-permute-start(bf16[64,2048]{1,0:T(8,128)(2,1)S(1)} %add.33.refs_3_), channel_id=1, source_target_pairs={{4,0},{5,1},{8,4},{9,5},{12,8},{13,9},{14,12},{15,13},{10,14},{11,... | collective-permute-start | bytes 786440 | tf_op jit(solution)/shard_map/ppermute | solution.py:466
  (3 other events, 38.4 us)

commit v2 on v1

--- a/solution.py
+++ b/solution.py
@@ -376,13 +376,10 @@
     refs[-1][...] = total
 
 
-def final_kernel(chunks, base_ref, *refs):
-    out_ref = refs[-1]
-    rows = refs[0].shape[0]
-    for chunk in range(chunks):
-        span = slice(chunk * rows, (chunk + 1) * rows)
-        total = base_ref[span] + refs[chunk][...].astype(F32) + refs[chunks + chunk][...].astype(F32)
-        out_ref[span] = total.astype(BF16)
+def half_sum_kernel(base_ref, top_ref, bottom_ref, out_ref):
+    rows = top_ref.shape[0]
+    for span, ref in ((slice(0, rows), top_ref), (slice(rows, 2 * rows), bottom_ref)):
+        out_ref[span] = (base_ref[span] + ref[...].astype(F32)).astype(out_ref.dtype)
 
 
 def plain_call(kernel, name, shape, operands):
@@ -530,16 +527,17 @@
     theirs = results[0][1]
     for k in range(1, depth):
         if k > 1:
-            low, high, results[k - 1], came[k - 2] = lax.optimization_barrier(
-                (low, high, results[k - 1], came[k - 2])
-            )
+            low, high, results[k - 1] = lax.optimization_barrier((low, high, results[k - 1]))
+            if k == 2:
+                low, high, came[0] = lax.optimization_barrier((low, high, came[0]))
             theirs = results[k - 1][1]
-        if k == min(2, depth - 1):
+        if k == depth - 1:
             low, high, shared_rows = lax.optimization_barrier((low, high, shared_rows))
         others = to_core(low), to_core(high)
+        if k == depth - 1:
+            others, theirs = lax.optimization_barrier((others, theirs))
         came[k - 1] = to_core(theirs)
         if k == 1:
-            others, own_rows = lax.optimization_barrier((others, own_rows))
             shared_rows = [own_rows]
             for shift in range(1, req_size):
                 shared_rows.append(to_request(own_rows, shift))
@@ -549,12 +547,11 @@
             low, high = to_ahead(low), to_behind(high)
         else:
             low, high = to_ahead(low[: rows // 2]), to_behind(high[rows // 2 :])
-    low, high, results[depth - 1], came[depth - 2] = lax.optimization_barrier(
-        (low, high, results[depth - 1], came[depth - 2])
-    )
+    low, high, results[depth - 1], came[1] = lax.optimization_barrier((low, high, results[depth - 1], came[1]))
     results[depth] = expert(0, 1, tabs_late, gain, weights, [low, high, to_core(low), to_core(high)])
 
     cut = rows // 2
+    came, results[depth] = lax.optimization_barrier((came, results[depth]))
     came[depth - 1], came[depth] = to_core(results[depth - 1][1]), to_core(results[depth][1])
 
     def step(after, k, low_chunk, low, high):
@@ -583,9 +580,12 @@
             shared = shared_expert(gain, [shared_gate.T, shared_up.T, shared_down.T], shared_rows, after[0])
             after = [shared[0]]
         after, *first = step(after, k, 1, *first)
-    low, high = [second[0][0], first[0][0]], [first[1][0], second[1][0]]
+    shape = base.shape
+    part_sum = plain_call(
+        half_sum_kernel, "part_sum", jax.ShapeDtypeStruct(shape, F32), [base, second[0][0], second[1][0]]
+    )
     return plain_call(
-        functools.partial(final_kernel, 2), "final", jax.ShapeDtypeStruct((rows, width), BF16), [base] + low + high
+        half_sum_kernel, "final", jax.ShapeDtypeStruct(shape, BF16), [part_sum, first[1][0], first[0][0]]
     )
 
 

time: 162 us -> 159 us (0.981)
  waiting for transfers between devices: 65.3 us -> 62.3 us
    ppermute x19, waiting for transfers between devices: 26.3 us -> 24.1 us  [to_behind(): return lax.ppermute(x, 'exp', behind)]
    ppermute x5, waiting for transfers between devices: 5.08 us -> 3.08 us  [to_request(): return lax.ppermute(x, ('req', 'exp'), pairs)]
  transfers between devices with their start and end apart: 61 -> 61, of which waited for: 37 -> 35; matrix products, arithmetic and copies ran while one was open for 0% -> 0% of each run, Pallas kernels for 26% -> 26%
where the time goes in v2:
time: 159 us
  waiting for transfers between devices  62.3 us (39%)
  Pallas kernels  47.8 us (30%)
  starting transfers between devices  47.8 us (30%)
    pallas_call x5, Pallas kernels, expert(): pl.pallas_call(functools.partial(expert_kernel, first, blocks, len(inputs...  30.1 us
    ppermute x19, starting transfers between devices, to_ahead(): return lax.ppermute(x, 'exp', ahead)  29 us
    ppermute x19, waiting for transfers between devices, to_ahead(): return lax.ppermute(x, 'exp', ahead)  26.8 us
    ppermute x19, waiting for transfers between devices, to_behind(): return lax.ppermute(x, 'exp', behind)  24.1 us
    ppermute x19, starting transfers between devices, to_behind(): return lax.ppermute(x, 'exp', behind)  10.3 us
    ppermute x18, waiting for transfers between devices, to_core(): return lax.ppermute(x, 'exp', [(d, d ^ 1) for d in range(exp_size)])  8.43 us
    ppermute x5, starting transfers between devices, to_request(): return lax.ppermute(x, ('req', 'exp'), pairs)  5.07 us
    pallas_call x1, Pallas kernels, shared_expert(): pl.pallas_call(functools.partial(shared_kernel, count), out_shape=shapes,...  4.83 us
  transfers between devices with their start and end apart: 61, of which 35 were waited for; matrix products, arithmetic and copies ran while one was open for 0% of the time, Pallas kernels for 26%

profile of v2, /device:TPU:0, one launch (start us, length us, event | category | flops | bytes accessed | tf_op | source)
XLA Modules:
  0.0 159.0 jit_solution(12390731792127732939)
XLA Ops:
  0.1 2.4 %prepare.1 = (bf16[144,512]{1,0:T(8,128)(2,1)S(1)}, bf16[144,512]{1,0:T(8,128)(2,1)S(1)}, bf16[128,3072]{1,0:T(8,128)(2,1)S(1)}, bf16[128,3072]{1,0:T(8,128)(2,1)S(1)}) custom-call(s32[3]{0:T(128)S(1)} %pad_add_fusion.where_ref, s32[6,128]{1,0:T(8,128)} %bitcast.35, f32[6,128]{1,0:T(8,128)} %bitcast.36, bf16[128,2048]{1,0:T(8,128)(2,1)} %weight_hbm.1, ...), custom_call_target="tpu_custom_call" | custom-call | bytes 2097152 | tf_op jit(solution)/shard_map/prepare/pallas_call | solution.py:90
  2.5 3.0 %collective-permute-start.13 = (bf16[128,3072]{1,0:T(8,128)(2,1)S(1)}, bf16[128,3072]{1,0:T(8,128)(2,1)S(1)}, u32[]{:S(2)}, u32[]{:S(2)}) collective-permute-start(bf16[128,3072]{1,0:T(8,128)(2,1)S(1)} %get-tuple-element.104), channel_id=1, source_target_pairs={{0,16},{1,17},{2,18},{3,19},{4,20},{5,21},{6,22},{7,23},{8,24},{9,... | collective-permute-start | bytes 2359304 | tf_op jit(solution)/shard_map/ppermute | solution.py:474
  5.5 1.6 collective-permute-start
  7.5 1.5 collective-permute-start.10
  9.5 2.6 %collective-permute-done.refs_6_.refs_2_ = bf16[144,512]{1,0:T(8,128)(2,1)S(1)} collective-permute-done((bf16[144,512]{1,0:T(8,128)(2,1)S(1)}, bf16[144,512]{1,0:T(8,128)(2,1)S(1)}, u32[]{:S(2)}, u32[]{:S(2)}) %collective-permute-start) | collective-permute-done | bytes 147488 | tf_op jit(solution)/shard_map/ppermute | solution.py:460
  12.1 1.6 collective-permute-start.1
  14.2 2.7 %collective-permute-done.10.refs_9_.refs_5_ = bf16[144,512]{1,0:T(8,128)(2,1)S(1)} collective-permute-done((bf16[144,512]{1,0:T(8,128)(2,1)S(1)}, bf16[144,512]{1,0:T(8,128)(2,1)S(1)}, u32[]{:S(2)}, u32[]{:S(2)}) %collective-permute-start.10) | collective-permute-done | bytes 147488 | tf_op jit(solution)/shard_map/ppermute | solution.py:463
  17.3 1.6 collective-permute-start.5
  18.9 1.6 collective-permute-start.2
  21.0 2.7 %collective-permute-done.11.refs_13_.refs_9_ = bf16[144,512]{1,0:T(8,128)(2,1)S(1)} collective-permute-done((bf16[144,512]{1,0:T(8,128)(2,1)S(1)}, bf16[144,512]{1,0:T(8,128)(2,1)S(1)}, u32[]{:S(2)}, u32[]{:S(2)}) %collective-permute-start.11) | collective-permute-done | bytes 147488 | tf_op jit(solution)/shard_map/ppermute | solution.py:463
  24.1 1.6 collective-permute-start.6
  25.7 1.5 collective-permute-done.9.refs_16_.refs_4_
  27.2 1.6 collective-permute-done.12.refs_17_.refs_5_
  29.3 1.6 collective-permute-start.16
  31.6 0.7 copy-done.3
  32.2 1.7 %proj_part.1.refs_6_ = f32[512,512]{1,0:T(8,128)S(1)} custom-call(s32[3]{0:T(128)S(1)} %pad_add_fusion.where_ref, s32[16]{0:T(128)S(1)} %copy-done.3, bf16[128,3072]{1,0:T(8,128)(2,1)S(1)} %get-tuple-element.101.refs_0_, bf16[128,3072]{1,0:T(8,128)(2,1)S(1)} %collective-permute-done.13.refs_1_, bf16[128,3072]{1,0:T(8,128)(2,1)S(1)} %collective-permute-done.14.refs_2_, ...), custom_call_target="tpu_custom_call" | custom-call | flops 1879048192 | bytes 3932160 | tf_op jit(solution)/shard_map/proj_part/pallas_call | solution.py:189
  34.0 1.6 collective-permute-done.16.refs_4_.refs_0_
  35.5 1.3 collective-permute-done.17.refs_5_.refs_1_
  36.8 0.9 proj_final.1
  37.8 1.3 collective-permute-done.18.refs_1_
  39.7 1.6 %collective-permute-start.19 = (bf16[128,1024]{1,0:T(8,128)(2,1)S(1)}, bf16[128,1024]{1,0:T(8,128)(2,1)S(1)}, u32[]{:S(2)}, u32[]{:S(2)}) collective-permute-start(bf16[128,1024]{1,0:T(8,128)(2,1)S(1)} %beside.2.refs_0_), channel_id=1, source_target_pairs={{0,4},{1,5},{4,8},{5,9},{8,12},{9,13},{12,14},{13,15},{14,10},{15,... | collective-permute-start | bytes 786440 | tf_op jit(solution)/shard_map/ppermute | solution.py:460
  42.7 1.1 tables.3
  43.8 1.5 tables.2
  45.3 2.8 %collective-permute-done.21.refs_0_ = bf16[128,512]{1,0:T(8,128)(2,1)S(1)} collective-permute-done((bf16[128,512]{1,0:T(8,128)(2,1)S(1)}, bf16[128,512]{1,0:T(8,128)(2,1)S(1)}, u32[]{:S(2)}, u32[]{:S(2)}) %collective-permute-start.21) | collective-permute-done | bytes 131104 | tf_op jit(solution)/shard_map/ppermute | solution.py:474
  48.7 0.7 collective-permute-done.20.refs_0_
  50.0 0.8 collective-permute-start.25
  50.8 1.6 collective-permute-start.23
  52.8 4.2 %expert.5 = (bf16[128,2048]{1,0:T(8,128)(2,1)S(1)}, bf16[128,2048]{1,0:T(8,128)(2,1)S(1)}) custom-call(f32[1,2048]{1,0:T(1,128)S(1)} %bitcast.29, bf16[5,144,256]{2,1,0:T(8,128)(2,1)S(1)} %get-tuple-element.139.pick_ref, bf16[5,256,144]{2,1,0:T(8,128)(2,1)S(1)} %get-tuple-element.140.put_ref, f32[5,144,1]{2,1,0:T(8,128)S(1)} %get-tuple-element.141.factor_ref, ...), custom_call_target="tpu_custom_call" | custom-call | flops 830472192 | bytes 4194304 | tf_op jit(solution)/shard_map/expert/pallas_call | solution.py:290
  57.0 2.0 %collective-permute-done.23.refs_1_ = bf16[128,1024]{1,0:T(8,128)(2,1)S(1)} collective-permute-done((bf16[128,1024]{1,0:T(8,128)(2,1)S(1)}, bf16[128,1024]{1,0:T(8,128)(2,1)S(1)}, u32[]{:S(2)}, u32[]{:S(2)}) %collective-permute-start.23) | collective-permute-done | bytes 262176 | tf_op jit(solution)/shard_map/ppermute | solution.py:460
  59.0 1.3 collective-permute-done.24.refs_1_
  62.6 1.6 collective-permute-start.26
  64.2 7.2 %expert.6 = (bf16[128,2048]{1,0:T(8,128)(2,1)S(1)}, bf16[128,2048]{1,0:T(8,128)(2,1)S(1)}, bf16[256,2048]{1,0:T(8,128)(2,1)S(1)}) custom-call(f32[1,2048]{1,0:T(1,128)S(1)} %bitcast.30, bf16[5,144,256]{2,1,0:T(8,128)(2,1)S(1)} %get-tuple-element.139.pick_ref, bf16[5,256,144]{2,1,0:T(8,128)(2,1)S(1)} %get-tuple-element.140.put_ref, ...), custom_call_target="tpu_custom_call" | custom-call | flops 1660944384 | bytes 8388608 | tf_op jit(solution)/shard_map/expert/pallas_call | solution.py:290
  71.4 4.6 %collective-permute-done.27.refs_2_ = bf16[128,2048]{1,0:T(8,128)(2,1)S(1)} collective-permute-done((bf16[128,2048]{1,0:T(8,128)(2,1)S(1)}, bf16[128,2048]{1,0:T(8,128)(2,1)S(1)}, u32[]{:S(2)}, u32[]{:S(2)}) %collective-permute-start.27) | collective-permute-done | bytes 524320 | tf_op jit(solution)/shard_map/ppermute | solution.py:463
  76.8 1.5 collective-permute-start.31
  79.4 7.2 %expert.7 = (bf16[128,2048]{1,0:T(8,128)(2,1)S(1)}, bf16[128,2048]{1,0:T(8,128)(2,1)S(1)}, bf16[256,2048]{1,0:T(8,128)(2,1)S(1)}) custom-call(f32[1,2048]{1,0:T(1,128)S(1)} %bitcast.31, bf16[5,144,256]{2,1,0:T(8,128)(2,1)S(1)} %get-tuple-element.139.pick_ref, bf16[5,256,144]{2,1,0:T(8,128)(2,1)S(1)} %get-tuple-element.140.put_ref, ...), custom_call_target="tpu_custom_call" | custom-call | flops 1660944384 | bytes 8388608 | tf_op jit(solution)/shard_map/expert/pallas_call | solution.py:290
  86.6 4.0 %collective-permute-done.31.refs_0_ = bf16[128,2048]{1,0:T(8,128)(2,1)S(1)} collective-permute-done((bf16[128,2048]{1,0:T(8,128)(2,1)S(1)}, bf16[128,2048]{1,0:T(8,128)(2,1)S(1)}, u32[]{:S(2)}, u32[]{:S(2)}) %collective-permute-start.31) | collective-permute-done | bytes 524320 | tf_op jit(solution)/shard_map/ppermute | solution.py:460
  90.6 1.2 collective-permute-done.32.refs_2_
  92.6 1.4 collective-permute-done.38.refs_1_
  94.0 0.7 collective-permute-done.39.refs_3_
  94.9 1.6 collective-permute-start.36
  97.0 7.2 %expert.8 = (bf16[128,2048]{1,0:T(8,128)(2,1)S(1)}, bf16[128,2048]{1,0:T(8,128)(2,1)S(1)}, bf16[256,2048]{1,0:T(8,128)(2,1)S(1)}) custom-call(f32[1,2048]{1,0:T(1,128)S(1)} %bitcast.32, bf16[3,144,256]{2,1,0:T(8,128)(2,1)S(1)} %get-tuple-element.165.pick_ref, bf16[3,256,144]{2,1,0:T(8,128)(2,1)S(1)} %get-tuple-element.166.put_ref, ...), custom_call_target="tpu_custom_call" | custom-call | flops 1660944384 | bytes 8388608 | tf_op jit(solution)/shard_map/expert/pallas_call | solution.py:290
  105.3 2.5 %collective-permute-done.43.refs_2_ = bf16[64,2048]{1,0:T(8,128)(2,1)S(1)} collective-permute-done((bf16[64,2048]{1,0:T(8,128)(2,1)S(1)}, bf16[64,2048]{1,0:T(8,128)(2,1)S(1)}, u32[]{:S(2)}, u32[]{:S(2)}) %collective-permute-start.43) | collective-permute-done | bytes 262176 | tf_op jit(solution)/shard_map/ppermute | solution.py:466
  108.2 4.2 %expert.9 = (bf16[128,2048]{1,0:T(8,128)(2,1)S(1)}, bf16[128,2048]{1,0:T(8,128)(2,1)S(1)}) custom-call(f32[1,2048]{1,0:T(1,128)S(1)} %bitcast.33, bf16[3,144,256]{2,1,0:T(8,128)(2,1)S(1)} %get-tuple-element.165.pick_ref, bf16[3,256,144]{2,1,0:T(8,128)(2,1)S(1)} %get-tuple-element.166.put_ref, f32[3,144,1]{2,1,0:T(8,128)S(1)} %get-tuple-element.167.factor_ref, ...), custom_call_target="tpu_custom_call" | custom-call | flops 830472192 | bytes 4194304 | tf_op jit(solution)/shard_map/expert/pallas_call | solution.py:290
  112.7 1.8 %collective-permute-done.45.refs_1_ = bf16[128,2048]{1,0:T(8,128)(2,1)S(1)} collective-permute-done((bf16[128,2048]{1,0:T(8,128)(2,1)S(1)}, bf16[128,2048]{1,0:T(8,128)(2,1)S(1)}, u32[]{:S(2)}, u32[]{:S(2)}) %collective-permute-start.45) | collective-permute-done | bytes 524320 | tf_op jit(solution)/shard_map/ppermute | solution.py:466
  115.1 1.6 collective-permute-start.48
  117.4 4.8 %shared.1 = (f32[128,2048]{1,0:T(8,128)S(1)}, bf16[128,2048]{1,0:T(8,128)(2,1)S(1)}) custom-call(f32[1,2048]{1,0:T(1,128)S(1)} %bitcast.34, bf16[704,2048]{1,0:T(8,128)(2,1)} %bitcast.37, bf16[704,2048]{1,0:T(8,128)(2,1)} %bitcast.38, bf16[704,2048]{1,0:T(8,128)(2,1)} %bitcast.39, bf16[128,2048]{1,0:T(8,128)(2,1)S(1)} %weave.3.refs_0_.refs_1_, ...), custom_call_target="tpu_custom_call" | custom-call | flops 4429185024 | bytes 10747904 | tf_op jit(solution)/shard_map/shared/pallas_call | solution.py:351
  122.2 0.6 collective-permute-start.46
  122.8 1.6 collective-permute-start.53
  125.1 1.6 %collective-permute-start.51 = (bf16[64,2048]{1,0:T(8,128)(2,1)S(1)}, bf16[64,2048]{1,0:T(8,128)(2,1)S(1)}, u32[]{:S(2)}, u32[]{:S(2)}) collective-permute-start(bf16[64,2048]{1,0:T(8,128)(2,1)S(1)} %add.28.refs_3_), channel_id=1, source_target_pairs={{0,4},{1,5},{4,8},{5,9},{8,12},{9,13},{12,14},{13,15},{14,10},{15,... | collective-permute-start | bytes 786440 | tf_op jit(solution)/shard_map/ppermute | solution.py:460
  126.7 2.6 %collective-permute-done.47.refs_2_ = bf16[64,2048]{1,0:T(8,128)(2,1)S(1)} collective-permute-done((bf16[64,2048]{1,0:T(8,128)(2,1)S(1)}, bf16[64,2048]{1,0:T(8,128)(2,1)S(1)}, u32[]{:S(2)}, u32[]{:S(2)}) %collective-permute-start.47) | collective-permute-done | bytes 262176 | tf_op jit(solution)/shard_map/ppermute | solution.py:463
  130.0 2.1 %collective-permute-done.53.refs_2_ = bf16[64,2048]{1,0:T(8,128)(2,1)S(1)} collective-permute-done((bf16[64,2048]{1,0:T(8,128)(2,1)S(1)}, bf16[64,2048]{1,0:T(8,128)(2,1)S(1)}, u32[]{:S(2)}, u32[]{:S(2)}) %collective-permute-start.53) | collective-permute-done | bytes 262176 | tf_op jit(solution)/shard_map/ppermute | solution.py:460
  132.2 1.6 %collective-permute-start.55 = (bf16[64,2048]{1,0:T(8,128)(2,1)S(1)}, bf16[64,2048]{1,0:T(8,128)(2,1)S(1)}, u32[]{:S(2)}, u32[]{:S(2)}) collective-permute-start(bf16[64,2048]{1,0:T(8,128)(2,1)S(1)} %add.30.refs_3_), channel_id=1, source_target_pairs={{0,4},{1,5},{4,8},{5,9},{8,12},{9,13},{12,14},{13,15},{14,10},{15,... | collective-permute-start | bytes 786440 | tf_op jit(solution)/shard_map/ppermute | solution.py:460
  133.8 1.2 collective-permute-done.52.refs_2_
  135.6 2.1 %collective-permute-done.51.refs_2_ = bf16[64,2048]{1,0:T(8,128)(2,1)S(1)} collective-permute-done((bf16[64,2048]{1,0:T(8,128)(2,1)S(1)}, bf16[64,2048]{1,0:T(8,128)(2,1)S(1)}, u32[]{:S(2)}, u32[]{:S(2)}) %collective-permute-start.51) | collective-permute-done | bytes 262176 | tf_op jit(solution)/shard_map/ppermute | solution.py:460
  137.8 1.6 %collective-permute-start.57 = (bf16[64,2048]{1,0:T(8,128)(2,1)S(1)}, bf16[64,2048]{1,0:T(8,128)(2,1)S(1)}, u32[]{:S(2)}, u32[]{:S(2)}) collective-permute-start(bf16[64,2048]{1,0:T(8,128)(2,1)S(1)} %add.32.refs_3_), channel_id=1, source_target_pairs={{0,4},{1,5},{4,8},{5,9},{8,12},{9,13},{12,14},{13,15},{14,10},{15,... | collective-permute-start | bytes 786440 | tf_op jit(solution)/shard_map/ppermute | solution.py:460
  139.7 0.9 collective-permute-done.50.refs_2_
  141.2 2.1 %collective-permute-done.55.refs_2_ = bf16[64,2048]{1,0:T(8,128)(2,1)S(1)} collective-permute-done((bf16[64,2048]{1,0:T(8,128)(2,1)S(1)}, bf16[64,2048]{1,0:T(8,128)(2,1)S(1)}, u32[]{:S(2)}, u32[]{:S(2)}) %collective-permute-start.55) | collective-permute-done | bytes 262176 | tf_op jit(solution)/shard_map/ppermute | solution.py:460
  143.4 1.6 %collective-permute-start.56 = (bf16[64,2048]{1,0:T(8,128)(2,1)S(1)}, bf16[64,2048]{1,0:T(8,128)(2,1)S(1)}, u32[]{:S(2)}, u32[]{:S(2)}) collective-permute-start(bf16[64,2048]{1,0:T(8,128)(2,1)S(1)} %add.34.refs_3_), channel_id=1, source_target_pairs={{0,4},{1,5},{4,8},{5,9},{8,12},{9,13},{12,14},{13,15},{14,10},{15,... | collective-permute-start | bytes 786440 | tf_op jit(solution)/shard_map/ppermute | solution.py:460
  145.0 1.2 collective-permute-done.58.refs_2_
  146.3 2.6 %collective-permute-done.57.refs_2_ = bf16[64,2048]{1,0:T(8,128)(2,1)S(1)} collective-permute-done((bf16[64,2048]{1,0:T(8,128)(2,1)S(1)}, bf16[64,2048]{1,0:T(8,128)(2,1)S(1)}, u32[]{:S(2)}, u32[]{:S(2)}) %collective-permute-start.57) | collective-permute-done | bytes 262176 | tf_op jit(solution)/shard_map/ppermute | solution.py:460
  149.0 1.6 %collective-permute-start.59 = (bf16[64,2048]{1,0:T(8,128)(2,1)S(1)}, bf16[64,2048]{1,0:T(8,128)(2,1)S(1)}, u32[]{:S(2)}, u32[]{:S(2)}) collective-permute-start(bf16[64,2048]{1,0:T(8,128)(2,1)S(1)} %add.36), channel_id=1, source_target_pairs={{0,4},{1,5},{4,8},{5,9},{8,12},{9,13},{12,14},{13,15},{14,10},{15,... | collective-permute-start | bytes 786440 | tf_op jit(solution)/shard_map/ppermute | solution.py:460
  151.1 3.4 %collective-permute-done.56.bottom_ref = bf16[64,2048]{1,0:T(8,128)(2,1)S(1)} collective-permute-done((bf16[64,2048]{1,0:T(8,128)(2,1)S(1)}, bf16[64,2048]{1,0:T(8,128)(2,1)S(1)}, u32[]{:S(2)}, u32[]{:S(2)}) %collective-permute-start.56) | collective-permute-done | bytes 262176 | tf_op jit(solution)/shard_map/ppermute | solution.py:460
  154.6 3.5 %collective-permute-done.59.top_ref = bf16[64,2048]{1,0:T(8,128)(2,1)S(1)} collective-permute-done((bf16[64,2048]{1,0:T(8,128)(2,1)S(1)}, bf16[64,2048]{1,0:T(8,128)(2,1)S(1)}, u32[]{:S(2)}, u32[]{:S(2)}) %collective-permute-start.59) | collective-permute-done | bytes 262176 | tf_op jit(solution)/shard_map/ppermute | solution.py:460
  158.1 0.9 final.1
  (107 shorter events, 20.2 us)
Async XLA Ops:
  0.1 52.7 %copy-start.1 = (bf16[1,1408,2048]{2,1,0:T(8,128)(2,1)S(1)}, bf16[1,1408,2048]{2,1,0:T(8,128)(2,1)}, u32[]{:S(2)}) copy-start(bf16[1,1408,2048]{2,1,0:T(8,128)(2,1)} %param.21) | copy-start | bytes 17301508
  2.5 26.8 %collective-permute-start.13 = (bf16[128,3072]{1,0:T(8,128)(2,1)S(1)}, bf16[128,3072]{1,0:T(8,128)(2,1)S(1)}, u32[]{:S(2)}, u32[]{:S(2)}) collective-permute-start(bf16[128,3072]{1,0:T(8,128)(2,1)S(1)} %get-tuple-element.104), channel_id=1, source_target_pairs={{0,16},{1,17},{2,18},{3,19},{4,20},{5,21},{6,22},{7,23},{8,24},{9,... | collective-permute-start | bytes 2359304 | tf_op jit(solution)/shard_map/ppermute | solution.py:474
  5.5 2.0 %collective-permute-start.3 = (bf16[144,512]{1,0:T(8,128)(2,1)S(1)}, bf16[144,512]{1,0:T(8,128)(2,1)S(1)}, u32[]{:S(2)}, u32[]{:S(2)}) collective-permute-start(bf16[144,512]{1,0:T(8,128)(2,1)S(1)} %get-tuple-element.103), channel_id=1, source_target_pairs={{0,1},{1,0},{2,3},{3,2},{4,5},{5,4},{6,7},{7,6},{8,9},{9,8},{10,11... | collective-permute-start | bytes 442376 | tf_op jit(solution)/shard_map/ppermute | solution.py:466
  5.5 6.6 %collective-permute-start = (bf16[144,512]{1,0:T(8,128)(2,1)S(1)}, bf16[144,512]{1,0:T(8,128)(2,1)S(1)}, u32[]{:S(2)}, u32[]{:S(2)}) collective-permute-start(bf16[144,512]{1,0:T(8,128)(2,1)S(1)} %get-tuple-element.118.refs_4_.refs_0_), channel_id=1, source_target_pairs={{0,4},{1,5},{4,8},{5,9},{8,12},{9,13},{12,14},{13,15},{14,10},{15,... | collective-permute-start | bytes 442376 | tf_op jit(solution)/shard_map/ppermute | solution.py:460
  7.0 6.7 %collective-permute-start.7 = (bf16[144,512]{1,0:T(8,128)(2,1)S(1)}, bf16[144,512]{1,0:T(8,128)(2,1)S(1)}, u32[]{:S(2)}, u32[]{:S(2)}) collective-permute-start(bf16[144,512]{1,0:T(8,128)(2,1)S(1)} %get-tuple-element.118.refs_4_.refs_0_), channel_id=1, source_target_pairs={{4,0},{5,1},{8,4},{9,5},{12,8},{13,9},{14,12},{15,13},{10,14},{11,... | collective-permute-start | bytes 442376 | tf_op jit(solution)/shard_map/ppermute | solution.py:463
  7.5 9.4 %collective-permute-start.10 = (bf16[144,512]{1,0:T(8,128)(2,1)S(1)}, bf16[144,512]{1,0:T(8,128)(2,1)S(1)}, u32[]{:S(2)}, u32[]{:S(2)}) collective-permute-start(bf16[144,512]{1,0:T(8,128)(2,1)S(1)} %collective-permute-done.3.refs_5_.refs_1_), channel_id=1, source_target_pairs={{4,0},{5,1},{8,4},{9,5},{12,8},{13,9},{14,12},{15,13},{10,14},{11,... | collective-permute-start | bytes 442376 | tf_op jit(solution)/shard_map/ppermute | solution.py:463
  9.0 8.3 %collective-permute-start.4 = (bf16[144,512]{1,0:T(8,128)(2,1)S(1)}, bf16[144,512]{1,0:T(8,128)(2,1)S(1)}, u32[]{:S(2)}, u32[]{:S(2)}) collective-permute-start(bf16[144,512]{1,0:T(8,128)(2,1)S(1)} %collective-permute-done.3.refs_5_.refs_1_), channel_id=1, source_target_pairs={{0,4},{1,5},{4,8},{5,9},{8,12},{9,13},{12,14},{13,15},{14,10},{15,... | collective-permute-start | bytes 442376 | tf_op jit(solution)/shard_map/ppermute | solution.py:460
  12.1 6.8 %collective-permute-start.1 = (bf16[144,512]{1,0:T(8,128)(2,1)S(1)}, bf16[144,512]{1,0:T(8,128)(2,1)S(1)}, u32[]{:S(2)}, u32[]{:S(2)}) collective-permute-start(bf16[144,512]{1,0:T(8,128)(2,1)S(1)} %collective-permute-done.refs_6_.refs_2_), channel_id=1, source_target_pairs={{0,4},{1,5},{4,8},{5,9},{8,12},{9,13},{12,14},{13,15},{14,10},{15,... | collective-permute-start | bytes 442376 | tf_op jit(solution)/shard_map/ppermute | solution.py:460
  13.7 6.8 %collective-permute-start.8 = (bf16[144,512]{1,0:T(8,128)(2,1)S(1)}, bf16[144,512]{1,0:T(8,128)(2,1)S(1)}, u32[]{:S(2)}, u32[]{:S(2)}) collective-permute-start(bf16[144,512]{1,0:T(8,128)(2,1)S(1)} %collective-permute-done.7.refs_8_.refs_4_), channel_id=1, source_target_pairs={{4,0},{5,1},{8,4},{9,5},{12,8},{13,9},{14,12},{15,13},{10,14},{11,... | collective-permute-start | bytes 442376 | tf_op jit(solution)/shard_map/ppermute | solution.py:463
  16.9 6.8 %collective-permute-start.11 = (bf16[144,512]{1,0:T(8,128)(2,1)S(1)}, bf16[144,512]{1,0:T(8,128)(2,1)S(1)}, u32[]{:S(2)}, u32[]{:S(2)}) collective-permute-start(bf16[144,512]{1,0:T(8,128)(2,1)S(1)} %collective-permute-done.10.refs_9_.refs_5_), channel_id=1, source_target_pairs={{4,0},{5,1},{8,4},{9,5},{12,8},{13,9},{14,12},{15,13},{10,14},{11,... | collective-permute-start | bytes 442376 | tf_op jit(solution)/shard_map/ppermute | solution.py:463
  17.3 6.8 %collective-permute-start.5 = (bf16[144,512]{1,0:T(8,128)(2,1)S(1)}, bf16[144,512]{1,0:T(8,128)(2,1)S(1)}, u32[]{:S(2)}, u32[]{:S(2)}) collective-permute-start(bf16[144,512]{1,0:T(8,128)(2,1)S(1)} %collective-permute-done.4.refs_7_.refs_3_), channel_id=1, source_target_pairs={{0,4},{1,5},{4,8},{5,9},{8,12},{9,13},{12,14},{13,15},{14,10},{15,... | collective-permute-start | bytes 442376 | tf_op jit(solution)/shard_map/ppermute | solution.py:460
  18.9 6.8 %collective-permute-start.2 = (bf16[144,512]{1,0:T(8,128)(2,1)S(1)}, bf16[144,512]{1,0:T(8,128)(2,1)S(1)}, u32[]{:S(2)}, u32[]{:S(2)}) collective-permute-start(bf16[144,512]{1,0:T(8,128)(2,1)S(1)} %collective-permute-done.1.refs_10_.refs_6_), channel_id=1, source_target_pairs={{0,4},{1,5},{4,8},{5,9},{8,12},{9,13},{12,14},{13,15},{14,10},{15,... | collective-permute-start | bytes 442376 | tf_op jit(solution)/shard_map/ppermute | solution.py:460
  20.5 6.7 %collective-permute-start.9 = (bf16[144,512]{1,0:T(8,128)(2,1)S(1)}, bf16[144,512]{1,0:T(8,128)(2,1)S(1)}, u32[]{:S(2)}, u32[]{:S(2)}) collective-permute-start(bf16[144,512]{1,0:T(8,128)(2,1)S(1)} %collective-permute-done.8.refs_12_.refs_8_), channel_id=1, source_target_pairs={{4,0},{5,1},{8,4},{9,5},{12,8},{13,9},{14,12},{15,13},{10,14},{11,... | collective-permute-start | bytes 442376 | tf_op jit(solution)/shard_map/ppermute | solution.py:463
  23.7 5.1 %collective-permute-start.12 = (bf16[144,512]{1,0:T(8,128)(2,1)S(1)}, bf16[144,512]{1,0:T(8,128)(2,1)S(1)}, u32[]{:S(2)}, u32[]{:S(2)}) collective-permute-start(bf16[144,512]{1,0:T(8,128)(2,1)S(1)} %collective-permute-done.11.refs_13_.refs_9_), channel_id=1, source_target_pairs={{4,0},{5,1},{8,4},{9,5},{12,8},{13,9},{14,12},{15,13},{10,14},{11,... | collective-permute-start | bytes 442376 | tf_op jit(solution)/shard_map/ppermute | solution.py:463
  24.1 5.1 %collective-permute-start.6 = (bf16[144,512]{1,0:T(8,128)(2,1)S(1)}, bf16[144,512]{1,0:T(8,128)(2,1)S(1)}, u32[]{:S(2)}, u32[]{:S(2)}) collective-permute-start(bf16[144,512]{1,0:T(8,128)(2,1)S(1)} %collective-permute-done.5.refs_11_.refs_7_), channel_id=1, source_target_pairs={{0,4},{1,5},{4,8},{5,9},{8,12},{9,13},{12,14},{13,15},{14,10},{15,... | collective-permute-start | bytes 442376 | tf_op jit(solution)/shard_map/ppermute | solution.py:460
  25.7 5.6 %collective-permute-start.14 = (bf16[128,3072]{1,0:T(8,128)(2,1)S(1)}, bf16[128,3072]{1,0:T(8,128)(2,1)S(1)}, u32[]{:S(2)}, u32[]{:S(2)}) collective-permute-start(bf16[128,3072]{1,0:T(8,128)(2,1)S(1)} %get-tuple-element.101.refs_0_), channel_id=1, source_target_pairs={{0,1},{1,0},{2,3},{3,2},{4,5},{5,4},{6,7},{7,6},{8,9},{9,8},{10,11... | collective-permute-start | bytes 2359304 | tf_op jit(solution)/shard_map/ppermute | solution.py:466
  29.3 2.3 %collective-permute-start.15 = (bf16[128,3072]{1,0:T(8,128)(2,1)S(1)}, bf16[128,3072]{1,0:T(8,128)(2,1)S(1)}, u32[]{:S(2)}, u32[]{:S(2)}) collective-permute-start(bf16[128,3072]{1,0:T(8,128)(2,1)S(1)} %collective-permute-done.13.refs_1_), channel_id=1, source_target_pairs={{0,1},{1,0},{2,3},{3,2},{4,5},{5,4},{6,7},{7,6},{8,9},{9,8},{10,11... | collective-permute-start | bytes 2359304 | tf_op jit(solution)/shard_map/ppermute | solution.py:466
  29.3 6.3 %collective-permute-start.16 = (bf16[144,512]{1,0:T(8,128)(2,1)S(1)}, bf16[144,512]{1,0:T(8,128)(2,1)S(1)}, u32[]{:S(2)}, u32[]{:S(2)}) collective-permute-start(bf16[144,512]{1,0:T(8,128)(2,1)S(1)} %collective-permute-done.2.refs_14_.refs_2_), channel_id=1, source_target_pairs={{0,4},{1,5},{4,8},{5,9},{8,12},{9,13},{12,14},{13,15},{14,10},{15,... | collective-permute-start | bytes 442376 | tf_op jit(solution)/shard_map/ppermute | solution.py:460
  30.9 6.0 %collective-permute-start.17 = (bf16[144,512]{1,0:T(8,128)(2,1)S(1)}, bf16[144,512]{1,0:T(8,128)(2,1)S(1)}, u32[]{:S(2)}, u32[]{:S(2)}) collective-permute-start(bf16[144,512]{1,0:T(8,128)(2,1)S(1)} %collective-permute-done.12.refs_17_.refs_5_), channel_id=1, source_target_pairs={{4,0},{5,1},{8,4},{9,5},{12,8},{13,9},{14,12},{15,13},{10,14},{11,... | collective-permute-start | bytes 442376 | tf_op jit(solution)/shard_map/ppermute | solution.py:463
  32.2 20.6 %slice-start = ((s8[5767168]{0:T(1024)(128)(4,1)}), s8[4194304]{0:T(1024)(128)(4,1)S(1)}, s32[]{:S(2)}) async-start(s8[5767168]{0:T(1024)(128)(4,1)} %bitcast.12), calls=%async_computation | async-start | bytes 8388608
  33.9 18.9 %slice-start.1 = ((s8[5767168]{0:T(1024)(128)(4,1)}), s8[1572864]{0:T(1024)(128)(4,1)S(1)}, s32[]{:S(2)}) async-start(s8[5767168]{0:T(1024)(128)(4,1)} %bitcast.12), calls=%async_computation.1 | async-start | bytes 3145728
  37.7 1.4 collective-permute-start.18
  39.7 9.0 %collective-permute-start.19 = (bf16[128,1024]{1,0:T(8,128)(2,1)S(1)}, bf16[128,1024]{1,0:T(8,128)(2,1)S(1)}, u32[]{:S(2)}, u32[]{:S(2)}) collective-permute-start(bf16[128,1024]{1,0:T(8,128)(2,1)S(1)} %beside.2.refs_0_), channel_id=1, source_target_pairs={{0,4},{1,5},{4,8},{5,9},{8,12},{9,13},{12,14},{13,15},{14,10},{15,... | collective-permute-start | bytes 786440 | tf_op jit(solution)/shard_map/ppermute | solution.py:460
  41.3 8.1 %collective-permute-start.20 = (bf16[128,1024]{1,0:T(8,128)(2,1)S(1)}, bf16[128,1024]{1,0:T(8,128)(2,1)S(1)}, u32[]{:S(2)}, u32[]{:S(2)}) collective-permute-start(bf16[128,1024]{1,0:T(8,128)(2,1)S(1)} %beside.2.refs_0_), channel_id=1, source_target_pairs={{4,0},{5,1},{8,4},{9,5},{12,8},{13,9},{14,12},{15,13},{10,14},{11,... | collective-permute-start | bytes 786440 | tf_op jit(solution)/shard_map/ppermute | solution.py:463
  41.8 6.4 %collective-permute-start.21 = (bf16[128,512]{1,0:T(8,128)(2,1)S(1)}, bf16[128,512]{1,0:T(8,128)(2,1)S(1)}, u32[]{:S(2)}, u32[]{:S(2)}) collective-permute-start(bf16[128,512]{1,0:T(8,128)(2,1)S(1)} %get-tuple-element.116), channel_id=1, source_target_pairs={{0,16},{1,17},{2,18},{3,19},{4,20},{5,21},{6,22},{7,23},{8,24},{9,... | collective-permute-start | bytes 393224 | tf_op jit(solution)/shard_map/ppermute | solution.py:474
  42.3 5.9 %collective-permute-start.22 = (bf16[128,512]{1,0:T(8,128)(2,1)S(1)}, bf16[128,512]{1,0:T(8,128)(2,1)S(1)}, u32[]{:S(2)}, u32[]{:S(2)}) collective-permute-start(bf16[128,512]{1,0:T(8,128)(2,1)S(1)} %get-tuple-element.117), channel_id=1, source_target_pairs={{0,17},{1,16},{2,19},{3,18},{4,21},{5,20},{6,23},{7,22},{8,25},{9,... | collective-permute-start | bytes 393224 | tf_op jit(solution)/shard_map/ppermute | solution.py:474
  50.0 2.8 %collective-permute-start.25 = (bf16[128,2048]{1,0:T(8,128)(2,1)S(1)}, bf16[128,2048]{1,0:T(8,128)(2,1)S(1)}, u32[]{:S(2)}, u32[]{:S(2)}) collective-permute-start(bf16[128,2048]{1,0:T(8,128)(2,1)S(1)} %weave.3.refs_0_.refs_1_), channel_id=1, source_target_pairs={{0,1},{1,0},{2,3},{3,2},{4,5},{5,4},{6,7},{7,6},{8,9},{9,8},{10,11... | collective-permute-start | bytes 1572872 | tf_op jit(solution)/shard_map/ppermute | solution.py:466
  50.8 8.3 %collective-permute-start.23 = (bf16[128,1024]{1,0:T(8,128)(2,1)S(1)}, bf16[128,1024]{1,0:T(8,128)(2,1)S(1)}, u32[]{:S(2)}, u32[]{:S(2)}) collective-permute-start(bf16[128,1024]{1,0:T(8,128)(2,1)S(1)} %beside.3.refs_1_), channel_id=1, source_target_pairs={{0,4},{1,5},{4,8},{5,9},{8,12},{9,13},{12,14},{13,15},{14,10},{15,... | collective-permute-start | bytes 786440 | tf_op jit(solution)/shard_map/ppermute | solution.py:460
  52.3 8.0 %collective-permute-start.24 = (bf16[128,1024]{1,0:T(8,128)(2,1)S(1)}, bf16[128,1024]{1,0:T(8,128)(2,1)S(1)}, u32[]{:S(2)}, u32[]{:S(2)}) collective-permute-start(bf16[128,1024]{1,0:T(8,128)(2,1)S(1)} %beside.3.refs_1_), channel_id=1, source_target_pairs={{4,0},{5,1},{8,4},{9,5},{12,8},{13,9},{14,12},{15,13},{10,14},{11,... | collective-permute-start | bytes 786440 | tf_op jit(solution)/shard_map/ppermute | solution.py:463
  60.9 3.3 %collective-permute-start.29 = (bf16[128,2048]{1,0:T(8,128)(2,1)S(1)}, bf16[128,2048]{1,0:T(8,128)(2,1)S(1)}, u32[]{:S(2)}, u32[]{:S(2)}) collective-permute-start(bf16[128,2048]{1,0:T(8,128)(2,1)S(1)} %weave.5.refs_2_), channel_id=1, source_target_pairs={{0,1},{1,0},{2,3},{3,2},{4,5},{5,4},{6,7},{7,6},{8,9},{9,8},{10,11... | collective-permute-start | bytes 1572872 | tf_op jit(solution)/shard_map/ppermute | solution.py:466
  61.6 2.6 %collective-permute-start.28 = (bf16[128,2048]{1,0:T(8,128)(2,1)S(1)}, bf16[128,2048]{1,0:T(8,128)(2,1)S(1)}, u32[]{:S(2)}, u32[]{:S(2)}) collective-permute-start(bf16[128,2048]{1,0:T(8,128)(2,1)S(1)} %weave.4.refs_0_), channel_id=1, source_target_pairs={{0,1},{1,0},{2,3},{3,2},{4,5},{5,4},{6,7},{7,6},{8,9},{9,8},{10,11... | collective-permute-start | bytes 1572872 | tf_op jit(solution)/shard_map/ppermute | solution.py:466
  62.1 13.9 %collective-permute-start.27 = (bf16[128,2048]{1,0:T(8,128)(2,1)S(1)}, bf16[128,2048]{1,0:T(8,128)(2,1)S(1)}, u32[]{:S(2)}, u32[]{:S(2)}) collective-permute-start(bf16[128,2048]{1,0:T(8,128)(2,1)S(1)} %weave.5.refs_2_), channel_id=1, source_target_pairs={{4,0},{5,1},{8,4},{9,5},{12,8},{13,9},{14,12},{15,13},{10,14},{11,... | collective-permute-start | bytes 1572872 | tf_op jit(solution)/shard_map/ppermute | solution.py:463
  62.6 13.7 %collective-permute-start.26 = (bf16[128,2048]{1,0:T(8,128)(2,1)S(1)}, bf16[128,2048]{1,0:T(8,128)(2,1)S(1)}, u32[]{:S(2)}, u32[]{:S(2)}) collective-permute-start(bf16[128,2048]{1,0:T(8,128)(2,1)S(1)} %weave.4.refs_0_), channel_id=1, source_target_pairs={{0,4},{1,5},{4,8},{5,9},{8,12},{9,13},{12,14},{13,15},{14,10},{15,... | collective-permute-start | bytes 1572872 | tf_op jit(solution)/shard_map/ppermute | solution.py:460
  64.2 12.1 %collective-permute-start.30 = (bf16[128,2048]{1,0:T(8,128)(2,1)S(1)}, bf16[128,2048]{1,0:T(8,128)(2,1)S(1)}, u32[]{:S(2)}, u32[]{:S(2)}) collective-permute-start(bf16[128,2048]{1,0:T(8,128)(2,1)S(1)} %get-tuple-element.153), channel_id=1, source_target_pairs={{0,1},{1,0},{2,3},{3,2},{4,5},{5,4},{6,7},{7,6},{8,9},{9,8},{10,11... | collective-permute-start | bytes 1572872 | tf_op jit(solution)/shard_map/ppermute | solution.py:466
  76.3 3.1 %collective-permute-start.33 = (bf16[128,2048]{1,0:T(8,128)(2,1)S(1)}, bf16[128,2048]{1,0:T(8,128)(2,1)S(1)}, u32[]{:S(2)}, u32[]{:S(2)}) collective-permute-start(bf16[128,2048]{1,0:T(8,128)(2,1)S(1)} %collective-permute-done.26.refs_0_), channel_id=1, source_target_pairs={{0,1},{1,0},{2,3},{3,2},{4,5},{5,4},{6,7},{7,6},{8,9},{9,8},{10,11... | collective-permute-start | bytes 1572872 | tf_op jit(solution)/shard_map/ppermute | solution.py:466
  76.3 3.1 %collective-permute-start.34 = (bf16[128,2048]{1,0:T(8,128)(2,1)S(1)}, bf16[128,2048]{1,0:T(8,128)(2,1)S(1)}, u32[]{:S(2)}, u32[]{:S(2)}) collective-permute-start(bf16[128,2048]{1,0:T(8,128)(2,1)S(1)} %collective-permute-done.27.refs_2_), channel_id=1, source_target_pairs={{0,1},{1,0},{2,3},{3,2},{4,5},{5,4},{6,7},{7,6},{8,9},{9,8},{10,11... | collective-permute-start | bytes 1572872 | tf_op jit(solution)/shard_map/ppermute | solution.py:466
  76.8 13.8 %collective-permute-start.31 = (bf16[128,2048]{1,0:T(8,128)(2,1)S(1)}, bf16[128,2048]{1,0:T(8,128)(2,1)S(1)}, u32[]{:S(2)}, u32[]{:S(2)}) collective-permute-start(bf16[128,2048]{1,0:T(8,128)(2,1)S(1)} %collective-permute-done.26.refs_0_), channel_id=1, source_target_pairs={{0,4},{1,5},{4,8},{5,9},{8,12},{9,13},{12,14},{13,15},{14,10},{15,... | collective-permute-start | bytes 1572872 | tf_op jit(solution)/shard_map/ppermute | solution.py:460
  78.3 13.6 %collective-permute-start.32 = (bf16[128,2048]{1,0:T(8,128)(2,1)S(1)}, bf16[128,2048]{1,0:T(8,128)(2,1)S(1)}, u32[]{:S(2)}, u32[]{:S(2)}) collective-permute-start(bf16[128,2048]{1,0:T(8,128)(2,1)S(1)} %collective-permute-done.27.refs_2_), channel_id=1, source_target_pairs={{4,0},{5,1},{8,4},{9,5},{12,8},{13,9},{14,12},{15,13},{10,14},{11,... | collective-permute-start | bytes 1572872 | tf_op jit(solution)/shard_map/ppermute | solution.py:463
  78.8 13.3 %collective-permute-start.35 = (bf16[128,2048]{1,0:T(8,128)(2,1)S(1)}, bf16[128,2048]{1,0:T(8,128)(2,1)S(1)}, u32[]{:S(2)}, u32[]{:S(2)}) collective-permute-start(bf16[128,2048]{1,0:T(8,128)(2,1)S(1)} %weave.3.refs_0_.refs_1_), channel_id=1, source_target_pairs={{0,16},{1,17},{2,18},{3,19},{4,20},{5,21},{6,22},{7,23},{8,24},{9,... | collective-permute-start | bytes 1572872 | tf_op jit(solution)/shard_map/ppermute | solution.py:474
  92.1 1.9 %collective-permute-start.38 = (bf16[128,2048]{1,0:T(8,128)(2,1)S(1)}, bf16[128,2048]{1,0:T(8,128)(2,1)S(1)}, u32[]{:S(2)}, u32[]{:S(2)}) collective-permute-start(bf16[128,2048]{1,0:T(8,128)(2,1)S(1)} %collective-permute-done.31.refs_0_), channel_id=1, source_target_pairs={{0,1},{1,0},{2,3},{3,2},{4,5},{5,4},{6,7},{7,6},{8,9},{9,8},{10,11... | collective-permute-start | bytes 1572872 | tf_op jit(solution)/shard_map/ppermute | solution.py:466
  92.1 2.7 %collective-permute-start.39 = (bf16[128,2048]{1,0:T(8,128)(2,1)S(1)}, bf16[128,2048]{1,0:T(8,128)(2,1)S(1)}, u32[]{:S(2)}, u32[]{:S(2)}) collective-permute-start(bf16[128,2048]{1,0:T(8,128)(2,1)S(1)} %collective-permute-done.32.refs_2_), channel_id=1, source_target_pairs={{0,1},{1,0},{2,3},{3,2},{4,5},{5,4},{6,7},{7,6},{8,9},{9,8},{10,11... | collective-permute-start | bytes 1572872 | tf_op jit(solution)/shard_map/ppermute | solution.py:466
  92.6 12.2 %collective-permute-start.40 = (bf16[256,2048]{1,0:T(8,128)(2,1)S(1)}, bf16[256,2048]{1,0:T(8,128)(2,1)S(1)}, u32[]{:S(2)}, u32[]{:S(2)}) collective-permute-start(bf16[256,2048]{1,0:T(8,128)(2,1)S(1)} %get-tuple-element.174), channel_id=1, source_target_pairs={{0,1},{1,0},{2,3},{3,2},{4,5},{5,4},{6,7},{7,6},{8,9},{9,8},{10,11... | collective-permute-start | bytes 3145736 | tf_op jit(solution)/shard_map/ppermute | solution.py:466
  94.8 17.7 %collective-permute-start.42 = (bf16[256,2048]{1,0:T(8,128)(2,1)S(1)}, bf16[256,2048]{1,0:T(8,128)(2,1)S(1)}, u32[]{:S(2)}, u32[]{:S(2)}) collective-permute-start(bf16[256,2048]{1,0:T(8,128)(2,1)S(1)} %get-tuple-element.180), channel_id=1, source_target_pairs={{0,1},{1,0},{2,3},{3,2},{4,5},{5,4},{6,7},{7,6},{8,9},{9,8},{10,11... | collective-permute-start | bytes 3145736 | tf_op jit(solution)/shard_map/ppermute | solution.py:466
  94.9 9.3 %collective-permute-start.36 = (bf16[64,2048]{1,0:T(8,128)(2,1)S(1)}, bf16[64,2048]{1,0:T(8,128)(2,1)S(1)}, u32[]{:S(2)}, u32[]{:S(2)}) collective-permute-start(bf16[64,2048]{1,0:T(8,128)(2,1)S(1)} %slice.6), channel_id=1, source_target_pairs={{0,4},{1,5},{4,8},{5,9},{8,12},{9,13},{12,14},{13,15},{14,10},{15,... | collective-permute-start | bytes 786440 | tf_op jit(solution)/shard_map/ppermute | solution.py:460
  96.5 8.3 %collective-permute-start.37 = (bf16[64,2048]{1,0:T(8,128)(2,1)S(1)}, bf16[64,2048]{1,0:T(8,128)(2,1)S(1)}, u32[]{:S(2)}, u32[]{:S(2)}) collective-permute-start(bf16[64,2048]{1,0:T(8,128)(2,1)S(1)} %slice.7), channel_id=1, source_target_pairs={{4,0},{5,1},{8,4},{9,5},{12,8},{13,9},{14,12},{15,13},{10,14},{11,... | collective-permute-start | bytes 786440 | tf_op jit(solution)/shard_map/ppermute | solution.py:463
  104.8 11.9 %collective-permute-start.41 = (bf16[256,2048]{1,0:T(8,128)(2,1)S(1)}, bf16[256,2048]{1,0:T(8,128)(2,1)S(1)}, u32[]{:S(2)}, u32[]{:S(2)}) collective-permute-start(bf16[256,2048]{1,0:T(8,128)(2,1)S(1)} %get-tuple-element.176), channel_id=1, source_target_pairs={{0,1},{1,0},{2,3},{3,2},{4,5},{5,4},{6,7},{7,6},{8,9},{9,8},{10,11... | collective-permute-start | bytes 3145736 | tf_op jit(solution)/shard_map/ppermute | solution.py:466
  104.8 3.0 %collective-permute-start.43 = (bf16[64,2048]{1,0:T(8,128)(2,1)S(1)}, bf16[64,2048]{1,0:T(8,128)(2,1)S(1)}, u32[]{:S(2)}, u32[]{:S(2)}) collective-permute-start(bf16[64,2048]{1,0:T(8,128)(2,1)S(1)} %collective-permute-done.36.refs_0_), channel_id=1, source_target_pairs={{0,1},{1,0},{2,3},{3,2},{4,5},{5,4},{6,7},{7,6},{8,9},{9,8},{10,11... | collective-permute-start | bytes 786440 | tf_op jit(solution)/shard_map/ppermute | solution.py:466
  105.3 2.9 %collective-permute-start.44 = (bf16[64,2048]{1,0:T(8,128)(2,1)S(1)}, bf16[64,2048]{1,0:T(8,128)(2,1)S(1)}, u32[]{:S(2)}, u32[]{:S(2)}) collective-permute-start(bf16[64,2048]{1,0:T(8,128)(2,1)S(1)} %collective-permute-done.37.refs_1_), channel_id=1, source_target_pairs={{0,1},{1,0},{2,3},{3,2},{4,5},{5,4},{6,7},{7,6},{8,9},{9,8},{10,11... | collective-permute-start | bytes 786440 | tf_op jit(solution)/shard_map/ppermute | solution.py:466
  112.5 2.0 %collective-permute-start.45 = (bf16[128,2048]{1,0:T(8,128)(2,1)S(1)}, bf16[128,2048]{1,0:T(8,128)(2,1)S(1)}, u32[]{:S(2)}, u32[]{:S(2)}) collective-permute-start(bf16[128,2048]{1,0:T(8,128)(2,1)S(1)} %get-tuple-element.186), channel_id=1, source_target_pairs={{0,1},{1,0},{2,3},{3,2},{4,5},{5,4},{6,7},{7,6},{8,9},{9,8},{10,11... | collective-permute-start | bytes 1572872 | tf_op jit(solution)/shard_map/ppermute | solution.py:466
  114.5 9.9 %collective-permute-start.49 = (bf16[64,2048]{1,0:T(8,128)(2,1)S(1)}, bf16[64,2048]{1,0:T(8,128)(2,1)S(1)}, u32[]{:S(2)}, u32[]{:S(2)}) collective-permute-start(bf16[64,2048]{1,0:T(8,128)(2,1)S(1)} %add.23.refs_2_), channel_id=1, source_target_pairs={{4,0},{5,1},{8,4},{9,5},{12,8},{13,9},{14,12},{15,13},{10,14},{11,... | collective-permute-start | bytes 786440 | tf_op jit(solution)/shard_map/ppermute | solution.py:463
  115.1 9.9 %collective-permute-start.48 = (bf16[64,2048]{1,0:T(8,128)(2,1)S(1)}, bf16[64,2048]{1,0:T(8,128)(2,1)S(1)}, u32[]{:S(2)}, u32[]{:S(2)}) collective-permute-start(bf16[64,2048]{1,0:T(8,128)(2,1)S(1)} %add.24.refs_2_), channel_id=1, source_target_pairs={{0,4},{1,5},{4,8},{5,9},{8,12},{9,13},{12,14},{13,15},{14,10},{15,... | collective-permute-start | bytes 786440 | tf_op jit(solution)/shard_map/ppermute | solution.py:460
  116.8 12.6 %collective-permute-start.47 = (bf16[64,2048]{1,0:T(8,128)(2,1)S(1)}, bf16[64,2048]{1,0:T(8,128)(2,1)S(1)}, u32[]{:S(2)}, u32[]{:S(2)}) collective-permute-start(bf16[64,2048]{1,0:T(8,128)(2,1)S(1)} %add.25.refs_2_), channel_id=1, source_target_pairs={{4,0},{5,1},{8,4},{9,5},{12,8},{13,9},{14,12},{15,13},{10,14},{11,... | collective-permute-start | bytes 786440 | tf_op jit(solution)/shard_map/ppermute | solution.py:463
  122.2 17.2 %collective-permute-start.46 = (bf16[128,2048]{1,0:T(8,128)(2,1)S(1)}, bf16[128,2048]{1,0:T(8,128)(2,1)S(1)}, u32[]{:S(2)}, u32[]{:S(2)}) collective-permute-start(bf16[128,2048]{1,0:T(8,128)(2,1)S(1)} %get-tuple-element.190), channel_id=1, source_target_pairs={{0,16},{1,17},{2,18},{3,19},{4,20},{5,21},{6,22},{7,23},{8,24},{9,... | collective-permute-start | bytes 1572872 | tf_op jit(solution)/shard_map/ppermute | solution.py:474
  122.8 9.2 %collective-permute-start.53 = (bf16[64,2048]{1,0:T(8,128)(2,1)S(1)}, bf16[64,2048]{1,0:T(8,128)(2,1)S(1)}, u32[]{:S(2)}, u32[]{:S(2)}) collective-permute-start(bf16[64,2048]{1,0:T(8,128)(2,1)S(1)} %add.26.refs_2_), channel_id=1, source_target_pairs={{0,4},{1,5},{4,8},{5,9},{8,12},{9,13},{12,14},{13,15},{14,10},{15,... | collective-permute-start | bytes 786440 | tf_op jit(solution)/shard_map/ppermute | solution.py:460
  124.5 10.5 %collective-permute-start.52 = (bf16[64,2048]{1,0:T(8,128)(2,1)S(1)}, bf16[64,2048]{1,0:T(8,128)(2,1)S(1)}, u32[]{:S(2)}, u32[]{:S(2)}) collective-permute-start(bf16[64,2048]{1,0:T(8,128)(2,1)S(1)} %add.27.refs_3_), channel_id=1, source_target_pairs={{4,0},{5,1},{8,4},{9,5},{12,8},{13,9},{14,12},{15,13},{10,14},{11,... | collective-permute-start | bytes 786440 | tf_op jit(solution)/shard_map/ppermute | solution.py:463
  125.1 12.6 %collective-permute-start.51 = (bf16[64,2048]{1,0:T(8,128)(2,1)S(1)}, bf16[64,2048]{1,0:T(8,128)(2,1)S(1)}, u32[]{:S(2)}, u32[]{:S(2)}) collective-permute-start(bf16[64,2048]{1,0:T(8,128)(2,1)S(1)} %add.28.refs_3_), channel_id=1, source_target_pairs={{0,4},{1,5},{4,8},{5,9},{8,12},{9,13},{12,14},{13,15},{14,10},{15,... | collective-permute-start | bytes 786440 | tf_op jit(solution)/shard_map/ppermute | solution.py:460
  129.4 11.1 %collective-permute-start.50 = (bf16[64,2048]{1,0:T(8,128)(2,1)S(1)}, bf16[64,2048]{1,0:T(8,128)(2,1)S(1)}, u32[]{:S(2)}, u32[]{:S(2)}) collective-permute-start(bf16[64,2048]{1,0:T(8,128)(2,1)S(1)} %add.29.refs_3_), channel_id=1, source_target_pairs={{4,0},{5,1},{8,4},{9,5},{12,8},{13,9},{14,12},{15,13},{10,14},{11,... | collective-permute-start | bytes 786440 | tf_op jit(solution)/shard_map/ppermute | solution.py:463
  132.2 11.1 %collective-permute-start.55 = (bf16[64,2048]{1,0:T(8,128)(2,1)S(1)}, bf16[64,2048]{1,0:T(8,128)(2,1)S(1)}, u32[]{:S(2)}, u32[]{:S(2)}) collective-permute-start(bf16[64,2048]{1,0:T(8,128)(2,1)S(1)} %add.30.refs_3_), channel_id=1, source_target_pairs={{0,4},{1,5},{4,8},{5,9},{8,12},{9,13},{12,14},{13,15},{14,10},{15,... | collective-permute-start | bytes 786440 | tf_op jit(solution)/shard_map/ppermute | solution.py:460
  135.0 11.1 %collective-permute-start.58 = (bf16[64,2048]{1,0:T(8,128)(2,1)S(1)}, bf16[64,2048]{1,0:T(8,128)(2,1)S(1)}, u32[]{:S(2)}, u32[]{:S(2)}) collective-permute-start(bf16[64,2048]{1,0:T(8,128)(2,1)S(1)} %add.31.refs_3_), channel_id=1, source_target_pairs={{4,0},{5,1},{8,4},{9,5},{12,8},{13,9},{14,12},{15,13},{10,14},{11,... | collective-permute-start | bytes 786440 | tf_op jit(solution)/shard_map/ppermute | solution.py:463
  137.8 11.1 %collective-permute-start.57 = (bf16[64,2048]{1,0:T(8,128)(2,1)S(1)}, bf16[64,2048]{1,0:T(8,128)(2,1)S(1)}, u32[]{:S(2)}, u32[]{:S(2)}) collective-permute-start(bf16[64,2048]{1,0:T(8,128)(2,1)S(1)} %add.32.refs_3_), channel_id=1, source_target_pairs={{0,4},{1,5},{4,8},{5,9},{8,12},{9,13},{12,14},{13,15},{14,10},{15,... | collective-permute-start | bytes 786440 | tf_op jit(solution)/shard_map/ppermute | solution.py:460
  140.7 13.9 %collective-permute-start.54 = (bf16[64,2048]{1,0:T(8,128)(2,1)S(1)}, bf16[64,2048]{1,0:T(8,128)(2,1)S(1)}, u32[]{:S(2)}, u32[]{:S(2)}) collective-permute-start(bf16[64,2048]{1,0:T(8,128)(2,1)S(1)} %add.33.refs_3_), channel_id=1, source_target_pairs={{4,0},{5,1},{8,4},{9,5},{12,8},{13,9},{14,12},{15,13},{10,14},{11,... | collective-permute-start | bytes 786440 | tf_op jit(solution)/shard_map/ppermute | solution.py:463
  143.4 11.1 %collective-permute-start.56 = (bf16[64,2048]{1,0:T(8,128)(2,1)S(1)}, bf16[64,2048]{1,0:T(8,128)(2,1)S(1)}, u32[]{:S(2)}, u32[]{:S(2)}) collective-permute-start(bf16[64,2048]{1,0:T(8,128)(2,1)S(1)} %add.34.refs_3_), channel_id=1, source_target_pairs={{0,4},{1,5},{4,8},{5,9},{8,12},{9,13},{12,14},{13,15},{14,10},{15,... | collective-permute-start | bytes 786440 | tf_op jit(solution)/shard_map/ppermute | solution.py:460
  149.0 9.1 %collective-permute-start.59 = (bf16[64,2048]{1,0:T(8,128)(2,1)S(1)}, bf16[64,2048]{1,0:T(8,128)(2,1)S(1)}, u32[]{:S(2)}, u32[]{:S(2)}) collective-permute-start(bf16[64,2048]{1,0:T(8,128)(2,1)S(1)} %add.36), channel_id=1, source_target_pairs={{0,4},{1,5},{4,8},{5,9},{8,12},{9,13},{12,14},{13,15},{14,10},{15,... | collective-permute-start | bytes 786440 | tf_op jit(solution)/shard_map/ppermute | solution.py:460
  150.6 7.5 %collective-permute-start.60 = (bf16[64,2048]{1,0:T(8,128)(2,1)S(1)}, bf16[64,2048]{1,0:T(8,128)(2,1)S(1)}, u32[]{:S(2)}, u32[]{:S(2)}) collective-permute-start(bf16[64,2048]{1,0:T(8,128)(2,1)S(1)} %add.35.refs_3_), channel_id=1, source_target_pairs={{4,0},{5,1},{8,4},{9,5},{12,8},{13,9},{14,12},{15,13},{10,14},{11,... | collective-permute-start | bytes 786440 | tf_op jit(solution)/shard_map/ppermute | solution.py:463
  (3 other events, 38.4 us)

commit v3 on v2

--- a/solution.py
+++ b/solution.py
@@ -529,10 +529,14 @@
         if k > 1:
             low, high, results[k - 1] = lax.optimization_barrier((low, high, results[k - 1]))
             if k == 2:
-                low, high, came[0] = lax.optimization_barrier((low, high, came[0]))
+                low, high, shared_rows = lax.optimization_barrier((low, high, shared_rows))
             theirs = results[k - 1][1]
         if k == depth - 1:
-            low, high, shared_rows = lax.optimization_barrier((low, high, shared_rows))
+            shared = shared_expert(
+                gain, [shared_gate.T, shared_up.T, shared_down.T], shared_rows, results[k - 2][1]
+            )
+            backs = [to_request(shared[shift], req_size - shift) for shift in range(1, req_size)]
+            low, high, shared, came[0] = lax.optimization_barrier((low, high, shared, came[0]))
         others = to_core(low), to_core(high)
         if k == depth - 1:
             others, theirs = lax.optimization_barrier((others, theirs))
@@ -547,7 +551,7 @@
             low, high = to_ahead(low), to_behind(high)
         else:
             low, high = to_ahead(low[: rows // 2]), to_behind(high[rows // 2 :])
-    low, high, results[depth - 1], came[1] = lax.optimization_barrier((low, high, results[depth - 1], came[1]))
+    low, high, results[depth - 1] = lax.optimization_barrier((low, high, results[depth - 1]))
     results[depth] = expert(0, 1, tabs_late, gain, weights, [low, high, to_core(low), to_core(high)])
 
     cut = rows // 2
@@ -569,17 +573,13 @@
     second = [], []
     after = [high_sum]
     for k in range(depth - 1, 0, -1):
-        if k == 1:
-            (mine,), _ = results[0]
-            backs = [to_request(shared[shift], req_size - shift) for shift in range(1, req_size)]
-            terms = [shared[0], own_rows, mine, came[0]] + backs
-            base = plain_call(base_kernel, "base", jax.ShapeDtypeStruct((rows, width), F32), terms)
-            after = after + [base]
+        if k == depth - 2:
+            after, backs = lax.optimization_barrier((after, backs))
         after, *second = step(after, k, 0, *second)
-        if k == depth - 1:
-            shared = shared_expert(gain, [shared_gate.T, shared_up.T, shared_down.T], shared_rows, after[0])
-            after = [shared[0]]
         after, *first = step(after, k, 1, *first)
+    (mine,), _ = results[0]
+    terms = [shared[0], own_rows, mine, came[0]] + backs
+    base = plain_call(base_kernel, "base", jax.ShapeDtypeStruct((rows, width), F32), terms)
     shape = base.shape
     part_sum = plain_call(
         half_sum_kernel, "part_sum", jax.ShapeDtypeStruct(shape, F32), [base, second[0][0], second[1][0]]

time: 159 us -> 158 us (level)
    ppermute x19, waiting for transfers between devices: 26.8 us -> 15.3 us  [to_ahead(): return lax.ppermute(x, 'exp', ahead)]
    ppermute x19, waiting for transfers between devices: 24.1 us -> 34.7 us  [to_behind(): return lax.ppermute(x, 'exp', behind)]
    ppermute x18, waiting for transfers between devices: 8.43 us -> 6.28 us  [to_core(): return lax.ppermute(x, 'exp', [(d, d ^ 1) for d in range(exp_size)])]
    ppermute x5, waiting for transfers between devices: 3.08 us -> 4.92 us  [to_request(): return lax.ppermute(x, ('req', 'exp'), pairs)]
  transfers between devices with their start and end apart: 61 -> 61, of which waited for: 35 -> 34; matrix products, arithmetic and copies ran while one was open for 0% -> 0% of each run, Pallas kernels for 26% -> 27%
where the time goes in v3:
time: 158 us
  waiting for transfers between devices  61.2 us (39%)
  starting transfers between devices  47.8 us (30%)
  Pallas kernels  47.7 us (30%)
    ppermute x19, waiting for transfers between devices, to_behind(): return lax.ppermute(x, 'exp', behind)  34.7 us
    pallas_call x5, Pallas kernels, expert(): pl.pallas_call(functools.partial(expert_kernel, first, blocks, len(inputs...  30 us
    ppermute x19, starting transfers between devices, to_ahead(): return lax.ppermute(x, 'exp', ahead)  28.3 us
    ppermute x19, waiting for transfers between devices, to_ahead(): return lax.ppermute(x, 'exp', ahead)  15.3 us
    ppermute x19, starting transfers between devices, to_behind(): return lax.ppermute(x, 'exp', behind)  11 us
    ppermute x18, waiting for transfers between devices, to_core(): return lax.ppermute(x, 'exp', [(d, d ^ 1) for d in range(exp_size)])  6.28 us
    ppermute x5, starting transfers between devices, to_request(): return lax.ppermute(x, ('req', 'exp'), pairs)  5.13 us
    ppermute x5, waiting for transfers between devices, to_request(): return lax.ppermute(x, ('req', 'exp'), pairs)  4.92 us
  transfers between devices with their start and end apart: 61, of which 34 were waited for; matrix products, arithmetic and copies ran while one was open for 0% of the time, Pallas kernels for 27%

profile of v3, /device:TPU:0, one launch (start us, length us, event | category | flops | bytes accessed | tf_op | source)
XLA Modules:
  0.0 157.8 jit_solution(6158049442839462120)
XLA Ops:
  0.1 2.4 %prepare.1 = (bf16[144,512]{1,0:T(8,128)(2,1)S(1)}, bf16[144,512]{1,0:T(8,128)(2,1)S(1)}, bf16[128,3072]{1,0:T(8,128)(2,1)S(1)}, bf16[128,3072]{1,0:T(8,128)(2,1)S(1)}) custom-call(s32[3]{0:T(128)S(1)} %pad_add_fusion.where_ref, s32[6,128]{1,0:T(8,128)} %bitcast.35, f32[6,128]{1,0:T(8,128)} %bitcast.36, bf16[128,2048]{1,0:T(8,128)(2,1)} %weight_hbm.1, ...), custom_call_target="tpu_custom_call" | custom-call | bytes 2097152 | tf_op jit(solution)/shard_map/prepare/pallas_call | solution.py:90
  2.5 3.0 %collective-permute-start.13 = (bf16[128,3072]{1,0:T(8,128)(2,1)S(1)}, bf16[128,3072]{1,0:T(8,128)(2,1)S(1)}, u32[]{:S(2)}, u32[]{:S(2)}) collective-permute-start(bf16[128,3072]{1,0:T(8,128)(2,1)S(1)} %get-tuple-element.106), channel_id=1, source_target_pairs={{0,16},{1,17},{2,18},{3,19},{4,20},{5,21},{6,22},{7,23},{8,24},{9,... | collective-permute-start | bytes 2359304 | tf_op jit(solution)/shard_map/ppermute | solution.py:474
  5.5 1.6 collective-permute-start
  7.5 1.5 collective-permute-start.10
  9.5 2.6 %collective-permute-done.refs_6_.refs_2_ = bf16[144,512]{1,0:T(8,128)(2,1)S(1)} collective-permute-done((bf16[144,512]{1,0:T(8,128)(2,1)S(1)}, bf16[144,512]{1,0:T(8,128)(2,1)S(1)}, u32[]{:S(2)}, u32[]{:S(2)}) %collective-permute-start) | collective-permute-done | bytes 147488 | tf_op jit(solution)/shard_map/ppermute | solution.py:460
  12.1 1.6 collective-permute-start.1
  14.2 2.7 %collective-permute-done.10.refs_9_.refs_5_ = bf16[144,512]{1,0:T(8,128)(2,1)S(1)} collective-permute-done((bf16[144,512]{1,0:T(8,128)(2,1)S(1)}, bf16[144,512]{1,0:T(8,128)(2,1)S(1)}, u32[]{:S(2)}, u32[]{:S(2)}) %collective-permute-start.10) | collective-permute-done | bytes 147488 | tf_op jit(solution)/shard_map/ppermute | solution.py:463
  17.3 1.6 collective-permute-start.5
  18.9 1.6 collective-permute-start.2
  21.0 2.7 %collective-permute-done.11.refs_13_.refs_9_ = bf16[144,512]{1,0:T(8,128)(2,1)S(1)} collective-permute-done((bf16[144,512]{1,0:T(8,128)(2,1)S(1)}, bf16[144,512]{1,0:T(8,128)(2,1)S(1)}, u32[]{:S(2)}, u32[]{:S(2)}) %collective-permute-start.11) | collective-permute-done | bytes 147488 | tf_op jit(solution)/shard_map/ppermute | solution.py:463
  24.1 1.6 collective-permute-start.6
  25.7 1.5 collective-permute-done.9.refs_16_.refs_4_
  27.2 1.6 %collective-permute-done.12.refs_17_.refs_5_ = bf16[144,512]{1,0:T(8,128)(2,1)S(1)} collective-permute-done((bf16[144,512]{1,0:T(8,128)(2,1)S(1)}, bf16[144,512]{1,0:T(8,128)(2,1)S(1)}, u32[]{:S(2)}, u32[]{:S(2)}) %collective-permute-start.12) | collective-permute-done | bytes 147488 | tf_op jit(solution)/shard_map/ppermute | solution.py:463
  29.3 1.6 collective-permute-start.16
  31.6 0.7 copy-done.3
  32.2 1.7 %proj_part.1.refs_6_ = f32[512,512]{1,0:T(8,128)S(1)} custom-call(s32[3]{0:T(128)S(1)} %pad_add_fusion.where_ref, s32[16]{0:T(128)S(1)} %copy-done.3, bf16[128,3072]{1,0:T(8,128)(2,1)S(1)} %get-tuple-element.103.refs_0_, bf16[128,3072]{1,0:T(8,128)(2,1)S(1)} %collective-permute-done.13.refs_1_, bf16[128,3072]{1,0:T(8,128)(2,1)S(1)} %collective-permute-done.14.refs_2_, ...), custom_call_target="tpu_custom_call" | custom-call | flops 1879048192 | bytes 3932160 | tf_op jit(solution)/shard_map/proj_part/pallas_call | solution.py:189
  33.9 1.6 %collective-permute-done.16.refs_4_.refs_0_ = bf16[144,512]{1,0:T(8,128)(2,1)S(1)} collective-permute-done((bf16[144,512]{1,0:T(8,128)(2,1)S(1)}, bf16[144,512]{1,0:T(8,128)(2,1)S(1)}, u32[]{:S(2)}, u32[]{:S(2)}) %collective-permute-start.16) | collective-permute-done | bytes 147488 | tf_op jit(solution)/shard_map/ppermute | solution.py:460
  35.5 1.3 collective-permute-done.17.refs_5_.refs_1_
  36.8 0.9 proj_final.1
  37.8 1.3 collective-permute-done.18.refs_1_
  39.7 1.6 %collective-permute-start.19 = (bf16[128,1024]{1,0:T(8,128)(2,1)S(1)}, bf16[128,1024]{1,0:T(8,128)(2,1)S(1)}, u32[]{:S(2)}, u32[]{:S(2)}) collective-permute-start(bf16[128,1024]{1,0:T(8,128)(2,1)S(1)} %beside.2.refs_0_), channel_id=1, source_target_pairs={{0,4},{1,5},{4,8},{5,9},{8,12},{9,13},{12,14},{13,15},{14,10},{15,... | collective-permute-start | bytes 786440 | tf_op jit(solution)/shard_map/ppermute | solution.py:460
  42.7 1.1 tables.3
  43.8 1.5 tables.2
  45.3 2.8 %collective-permute-done.21.refs_0_ = bf16[128,512]{1,0:T(8,128)(2,1)S(1)} collective-permute-done((bf16[128,512]{1,0:T(8,128)(2,1)S(1)}, bf16[128,512]{1,0:T(8,128)(2,1)S(1)}, u32[]{:S(2)}, u32[]{:S(2)}) %collective-permute-start.21) | collective-permute-done | bytes 131104 | tf_op jit(solution)/shard_map/ppermute | solution.py:474
  48.7 0.7 collective-permute-done.20.refs_0_
  50.0 0.8 collective-permute-start.25
  50.8 1.6 collective-permute-start.23
  52.8 4.2 %expert.5 = (bf16[128,2048]{1,0:T(8,128)(2,1)S(1)}, bf16[128,2048]{1,0:T(8,128)(2,1)S(1)}) custom-call(f32[1,2048]{1,0:T(1,128)S(1)} %bitcast.29, bf16[5,144,256]{2,1,0:T(8,128)(2,1)S(1)} %get-tuple-element.141.pick_ref, bf16[5,256,144]{2,1,0:T(8,128)(2,1)S(1)} %get-tuple-element.142.put_ref, f32[5,144,1]{2,1,0:T(8,128)S(1)} %get-tuple-element.143.factor_ref, ...), custom_call_target="tpu_custom_call" | custom-call | flops 830472192 | bytes 4194304 | tf_op jit(solution)/shard_map/expert/pallas_call | solution.py:290
  57.0 2.0 %collective-permute-done.23.refs_1_ = bf16[128,1024]{1,0:T(8,128)(2,1)S(1)} collective-permute-done((bf16[128,1024]{1,0:T(8,128)(2,1)S(1)}, bf16[128,1024]{1,0:T(8,128)(2,1)S(1)}, u32[]{:S(2)}, u32[]{:S(2)}) %collective-permute-start.23) | collective-permute-done | bytes 262176 | tf_op jit(solution)/shard_map/ppermute | solution.py:460
  59.0 1.3 collective-permute-done.24.refs_1_
  62.6 1.6 collective-permute-start.26
  64.7 7.2 %expert.6 = (bf16[128,2048]{1,0:T(8,128)(2,1)S(1)}, bf16[128,2048]{1,0:T(8,128)(2,1)S(1)}, bf16[256,2048]{1,0:T(8,128)(2,1)S(1)}) custom-call(f32[1,2048]{1,0:T(1,128)S(1)} %bitcast.30, bf16[5,144,256]{2,1,0:T(8,128)(2,1)S(1)} %get-tuple-element.141.pick_ref, bf16[5,256,144]{2,1,0:T(8,128)(2,1)S(1)} %get-tuple-element.142.put_ref, ...), custom_call_target="tpu_custom_call" | custom-call | flops 1660944384 | bytes 8388608 | tf_op jit(solution)/shard_map/expert/pallas_call | solution.py:290
  71.9 4.1 %collective-permute-done.27.refs_2_ = bf16[128,2048]{1,0:T(8,128)(2,1)S(1)} collective-permute-done((bf16[128,2048]{1,0:T(8,128)(2,1)S(1)}, bf16[128,2048]{1,0:T(8,128)(2,1)S(1)}, u32[]{:S(2)}, u32[]{:S(2)}) %collective-permute-start.27) | collective-permute-done | bytes 524320 | tf_op jit(solution)/shard_map/ppermute | solution.py:463
  76.3 1.2 collective-permute-done.30.refs_1_
  78.0 1.5 collective-permute-start.31
  80.1 4.8 %shared.1 = (f32[128,2048]{1,0:T(8,128)S(1)}, bf16[128,2048]{1,0:T(8,128)(2,1)S(1)}) custom-call(f32[1,2048]{1,0:T(1,128)S(1)} %bitcast.31, bf16[704,2048]{1,0:T(8,128)(2,1)} %bitcast.37, bf16[704,2048]{1,0:T(8,128)(2,1)} %bitcast.38, bf16[704,2048]{1,0:T(8,128)(2,1)} %bitcast.39, bf16[128,2048]{1,0:T(8,128)(2,1)S(1)} %weave.3.refs_0_.refs_1_, ...), custom_call_target="tpu_custom_call" | custom-call | flops 4429185024 | bytes 10747904 | tf_op jit(solution)/shard_map/shared/pallas_call | solution.py:351
  84.9 7.2 %expert.7 = (bf16[128,2048]{1,0:T(8,128)(2,1)S(1)}, bf16[128,2048]{1,0:T(8,128)(2,1)S(1)}, bf16[256,2048]{1,0:T(8,128)(2,1)S(1)}) custom-call(f32[1,2048]{1,0:T(1,128)S(1)} %bitcast.32, bf16[5,144,256]{2,1,0:T(8,128)(2,1)S(1)} %get-tuple-element.141.pick_ref, bf16[5,256,144]{2,1,0:T(8,128)(2,1)S(1)} %get-tuple-element.142.put_ref, ...), custom_call_target="tpu_custom_call" | custom-call | flops 1660944384 | bytes 8388608 | tf_op jit(solution)/shard_map/expert/pallas_call | solution.py:290
  92.4 1.2 collective-permute-done.32.refs_2_
  94.1 1.4 collective-permute-done.37.refs_1_
  95.5 0.7 collective-permute-done.38.refs_3_
  96.5 1.5 collective-permute-start.40
  98.5 7.2 %expert.8 = (bf16[128,2048]{1,0:T(8,128)(2,1)S(1)}, bf16[128,2048]{1,0:T(8,128)(2,1)S(1)}, bf16[256,2048]{1,0:T(8,128)(2,1)S(1)}) custom-call(f32[1,2048]{1,0:T(1,128)S(1)} %bitcast.33, bf16[3,144,256]{2,1,0:T(8,128)(2,1)S(1)} %get-tuple-element.175.pick_ref, bf16[3,256,144]{2,1,0:T(8,128)(2,1)S(1)} %get-tuple-element.176.put_ref, ...), custom_call_target="tpu_custom_call" | custom-call | flops 1660944384 | bytes 8388608 | tf_op jit(solution)/shard_map/expert/pallas_call | solution.py:290
  106.8 1.0 collective-permute-done.42.refs_2_
  108.2 4.2 %expert.9 = (bf16[128,2048]{1,0:T(8,128)(2,1)S(1)}, bf16[128,2048]{1,0:T(8,128)(2,1)S(1)}) custom-call(f32[1,2048]{1,0:T(1,128)S(1)} %bitcast.34, bf16[3,144,256]{2,1,0:T(8,128)(2,1)S(1)} %get-tuple-element.175.pick_ref, bf16[3,256,144]{2,1,0:T(8,128)(2,1)S(1)} %get-tuple-element.176.put_ref, f32[3,144,1]{2,1,0:T(8,128)S(1)} %get-tuple-element.177.factor_ref, ...), custom_call_target="tpu_custom_call" | custom-call | flops 830472192 | bytes 4194304 | tf_op jit(solution)/shard_map/expert/pallas_call | solution.py:290
  112.6 0.7 collective-permute-start.48
  113.2 1.1 collective-permute-done.45.refs_1_
  115.1 1.5 collective-permute-start.46
  117.4 1.5 collective-permute-start.53
  118.9 4.7 %collective-permute-done.47.refs_2_ = bf16[64,2048]{1,0:T(8,128)(2,1)S(1)} collective-permute-done((bf16[64,2048]{1,0:T(8,128)(2,1)S(1)}, bf16[64,2048]{1,0:T(8,128)(2,1)S(1)}, u32[]{:S(2)}, u32[]{:S(2)}) %collective-permute-start.47) | collective-permute-done | bytes 262176 | tf_op jit(solution)/shard_map/ppermute | solution.py:463
  123.7 0.6 collective-permute-start.52
  124.5 1.5 collective-permute-start.51
  126.0 0.8 collective-permute-done.48.refs_4_
  126.8 2.5 %collective-permute-done.49.refs_2_ = bf16[64,2048]{1,0:T(8,128)(2,1)S(1)} collective-permute-done((bf16[64,2048]{1,0:T(8,128)(2,1)S(1)}, bf16[64,2048]{1,0:T(8,128)(2,1)S(1)}, u32[]{:S(2)}, u32[]{:S(2)}) %collective-permute-start.49) | collective-permute-done | bytes 262176 | tf_op jit(solution)/shard_map/ppermute | solution.py:463
  130.1 1.5 collective-permute-start.55
  131.6 3.3 %collective-permute-done.52.refs_2_ = bf16[64,2048]{1,0:T(8,128)(2,1)S(1)} collective-permute-done((bf16[64,2048]{1,0:T(8,128)(2,1)S(1)}, bf16[64,2048]{1,0:T(8,128)(2,1)S(1)}, u32[]{:S(2)}, u32[]{:S(2)}) %collective-permute-start.52) | collective-permute-done | bytes 262176 | tf_op jit(solution)/shard_map/ppermute | solution.py:463
  135.7 1.5 collective-permute-start.57
  137.2 3.3 %collective-permute-done.50.refs_2_ = bf16[64,2048]{1,0:T(8,128)(2,1)S(1)} collective-permute-done((bf16[64,2048]{1,0:T(8,128)(2,1)S(1)}, bf16[64,2048]{1,0:T(8,128)(2,1)S(1)}, u32[]{:S(2)}, u32[]{:S(2)}) %collective-permute-start.50) | collective-permute-done | bytes 262176 | tf_op jit(solution)/shard_map/ppermute | solution.py:463
  141.3 1.5 collective-permute-start.56
  142.8 3.3 %collective-permute-done.58.refs_2_ = bf16[64,2048]{1,0:T(8,128)(2,1)S(1)} collective-permute-done((bf16[64,2048]{1,0:T(8,128)(2,1)S(1)}, bf16[64,2048]{1,0:T(8,128)(2,1)S(1)}, u32[]{:S(2)}, u32[]{:S(2)}) %collective-permute-start.58) | collective-permute-done | bytes 262176 | tf_op jit(solution)/shard_map/ppermute | solution.py:463
  146.2 0.6 collective-permute-done.57.refs_2_
  146.9 1.5 collective-permute-start.59
  149.3 3.2 %collective-permute-done.56.bottom_ref = bf16[64,2048]{1,0:T(8,128)(2,1)S(1)} collective-permute-done((bf16[64,2048]{1,0:T(8,128)(2,1)S(1)}, bf16[64,2048]{1,0:T(8,128)(2,1)S(1)}, u32[]{:S(2)}, u32[]{:S(2)}) %collective-permute-start.56) | collective-permute-done | bytes 262176 | tf_op jit(solution)/shard_map/ppermute | solution.py:460
  152.5 4.4 %collective-permute-done.59.top_ref = bf16[64,2048]{1,0:T(8,128)(2,1)S(1)} collective-permute-done((bf16[64,2048]{1,0:T(8,128)(2,1)S(1)}, bf16[64,2048]{1,0:T(8,128)(2,1)S(1)}, u32[]{:S(2)}, u32[]{:S(2)}) %collective-permute-start.59) | collective-permute-done | bytes 262176 | tf_op jit(solution)/shard_map/ppermute | solution.py:460
  157.0 0.9 final.1
  (107 shorter events, 20.2 us)
Async XLA Ops:
  0.1 52.7 %copy-start.1 = (bf16[1,1408,2048]{2,1,0:T(8,128)(2,1)S(1)}, bf16[1,1408,2048]{2,1,0:T(8,128)(2,1)}, u32[]{:S(2)}) copy-start(bf16[1,1408,2048]{2,1,0:T(8,128)(2,1)} %param.21) | copy-start | bytes 17301508
  2.5 26.8 %collective-permute-start.13 = (bf16[128,3072]{1,0:T(8,128)(2,1)S(1)}, bf16[128,3072]{1,0:T(8,128)(2,1)S(1)}, u32[]{:S(2)}, u32[]{:S(2)}) collective-permute-start(bf16[128,3072]{1,0:T(8,128)(2,1)S(1)} %get-tuple-element.106), channel_id=1, source_target_pairs={{0,16},{1,17},{2,18},{3,19},{4,20},{5,21},{6,22},{7,23},{8,24},{9,... | collective-permute-start | bytes 2359304 | tf_op jit(solution)/shard_map/ppermute | solution.py:474
  5.5 2.0 %collective-permute-start.3 = (bf16[144,512]{1,0:T(8,128)(2,1)S(1)}, bf16[144,512]{1,0:T(8,128)(2,1)S(1)}, u32[]{:S(2)}, u32[]{:S(2)}) collective-permute-start(bf16[144,512]{1,0:T(8,128)(2,1)S(1)} %get-tuple-element.105), channel_id=1, source_target_pairs={{0,1},{1,0},{2,3},{3,2},{4,5},{5,4},{6,7},{7,6},{8,9},{9,8},{10,11... | collective-permute-start | bytes 442376 | tf_op jit(solution)/shard_map/ppermute | solution.py:466
  5.5 6.6 %collective-permute-start = (bf16[144,512]{1,0:T(8,128)(2,1)S(1)}, bf16[144,512]{1,0:T(8,128)(2,1)S(1)}, u32[]{:S(2)}, u32[]{:S(2)}) collective-permute-start(bf16[144,512]{1,0:T(8,128)(2,1)S(1)} %get-tuple-element.120.refs_4_.refs_0_), channel_id=1, source_target_pairs={{0,4},{1,5},{4,8},{5,9},{8,12},{9,13},{12,14},{13,15},{14,10},{15,... | collective-permute-start | bytes 442376 | tf_op jit(solution)/shard_map/ppermute | solution.py:460
  7.0 6.7 %collective-permute-start.7 = (bf16[144,512]{1,0:T(8,128)(2,1)S(1)}, bf16[144,512]{1,0:T(8,128)(2,1)S(1)}, u32[]{:S(2)}, u32[]{:S(2)}) collective-permute-start(bf16[144,512]{1,0:T(8,128)(2,1)S(1)} %get-tuple-element.120.refs_4_.refs_0_), channel_id=1, source_target_pairs={{4,0},{5,1},{8,4},{9,5},{12,8},{13,9},{14,12},{15,13},{10,14},{11,... | collective-permute-start | bytes 442376 | tf_op jit(solution)/shard_map/ppermute | solution.py:463
  7.5 9.4 %collective-permute-start.10 = (bf16[144,512]{1,0:T(8,128)(2,1)S(1)}, bf16[144,512]{1,0:T(8,128)(2,1)S(1)}, u32[]{:S(2)}, u32[]{:S(2)}) collective-permute-start(bf16[144,512]{1,0:T(8,128)(2,1)S(1)} %collective-permute-done.3.refs_5_.refs_1_), channel_id=1, source_target_pairs={{4,0},{5,1},{8,4},{9,5},{12,8},{13,9},{14,12},{15,13},{10,14},{11,... | collective-permute-start | bytes 442376 | tf_op jit(solution)/shard_map/ppermute | solution.py:463
  9.0 8.3 %collective-permute-start.4 = (bf16[144,512]{1,0:T(8,128)(2,1)S(1)}, bf16[144,512]{1,0:T(8,128)(2,1)S(1)}, u32[]{:S(2)}, u32[]{:S(2)}) collective-permute-start(bf16[144,512]{1,0:T(8,128)(2,1)S(1)} %collective-permute-done.3.refs_5_.refs_1_), channel_id=1, source_target_pairs={{0,4},{1,5},{4,8},{5,9},{8,12},{9,13},{12,14},{13,15},{14,10},{15,... | collective-permute-start | bytes 442376 | tf_op jit(solution)/shard_map/ppermute | solution.py:460
  12.1 6.8 %collective-permute-start.1 = (bf16[144,512]{1,0:T(8,128)(2,1)S(1)}, bf16[144,512]{1,0:T(8,128)(2,1)S(1)}, u32[]{:S(2)}, u32[]{:S(2)}) collective-permute-start(bf16[144,512]{1,0:T(8,128)(2,1)S(1)} %collective-permute-done.refs_6_.refs_2_), channel_id=1, source_target_pairs={{0,4},{1,5},{4,8},{5,9},{8,12},{9,13},{12,14},{13,15},{14,10},{15,... | collective-permute-start | bytes 442376 | tf_op jit(solution)/shard_map/ppermute | solution.py:460
  13.7 6.8 %collective-permute-start.8 = (bf16[144,512]{1,0:T(8,128)(2,1)S(1)}, bf16[144,512]{1,0:T(8,128)(2,1)S(1)}, u32[]{:S(2)}, u32[]{:S(2)}) collective-permute-start(bf16[144,512]{1,0:T(8,128)(2,1)S(1)} %collective-permute-done.7.refs_8_.refs_4_), channel_id=1, source_target_pairs={{4,0},{5,1},{8,4},{9,5},{12,8},{13,9},{14,12},{15,13},{10,14},{11,... | collective-permute-start | bytes 442376 | tf_op jit(solution)/shard_map/ppermute | solution.py:463
  16.9 6.8 %collective-permute-start.11 = (bf16[144,512]{1,0:T(8,128)(2,1)S(1)}, bf16[144,512]{1,0:T(8,128)(2,1)S(1)}, u32[]{:S(2)}, u32[]{:S(2)}) collective-permute-start(bf16[144,512]{1,0:T(8,128)(2,1)S(1)} %collective-permute-done.10.refs_9_.refs_5_), channel_id=1, source_target_pairs={{4,0},{5,1},{8,4},{9,5},{12,8},{13,9},{14,12},{15,13},{10,14},{11,... | collective-permute-start | bytes 442376 | tf_op jit(solution)/shard_map/ppermute | solution.py:463
  17.3 6.8 %collective-permute-start.5 = (bf16[144,512]{1,0:T(8,128)(2,1)S(1)}, bf16[144,512]{1,0:T(8,128)(2,1)S(1)}, u32[]{:S(2)}, u32[]{:S(2)}) collective-permute-start(bf16[144,512]{1,0:T(8,128)(2,1)S(1)} %collective-permute-done.4.refs_7_.refs_3_), channel_id=1, source_target_pairs={{0,4},{1,5},{4,8},{5,9},{8,12},{9,13},{12,14},{13,15},{14,10},{15,... | collective-permute-start | bytes 442376 | tf_op jit(solution)/shard_map/ppermute | solution.py:460
  18.9 6.8 %collective-permute-start.2 = (bf16[144,512]{1,0:T(8,128)(2,1)S(1)}, bf16[144,512]{1,0:T(8,128)(2,1)S(1)}, u32[]{:S(2)}, u32[]{:S(2)}) collective-permute-start(bf16[144,512]{1,0:T(8,128)(2,1)S(1)} %collective-permute-done.1.refs_10_.refs_6_), channel_id=1, source_target_pairs={{0,4},{1,5},{4,8},{5,9},{8,12},{9,13},{12,14},{13,15},{14,10},{15,... | collective-permute-start | bytes 442376 | tf_op jit(solution)/shard_map/ppermute | solution.py:460
  20.5 6.7 %collective-permute-start.9 = (bf16[144,512]{1,0:T(8,128)(2,1)S(1)}, bf16[144,512]{1,0:T(8,128)(2,1)S(1)}, u32[]{:S(2)}, u32[]{:S(2)}) collective-permute-start(bf16[144,512]{1,0:T(8,128)(2,1)S(1)} %collective-permute-done.8.refs_12_.refs_8_), channel_id=1, source_target_pairs={{4,0},{5,1},{8,4},{9,5},{12,8},{13,9},{14,12},{15,13},{10,14},{11,... | collective-permute-start | bytes 442376 | tf_op jit(solution)/shard_map/ppermute | solution.py:463
  23.7 5.1 %collective-permute-start.12 = (bf16[144,512]{1,0:T(8,128)(2,1)S(1)}, bf16[144,512]{1,0:T(8,128)(2,1)S(1)}, u32[]{:S(2)}, u32[]{:S(2)}) collective-permute-start(bf16[144,512]{1,0:T(8,128)(2,1)S(1)} %collective-permute-done.11.refs_13_.refs_9_), channel_id=1, source_target_pairs={{4,0},{5,1},{8,4},{9,5},{12,8},{13,9},{14,12},{15,13},{10,14},{11,... | collective-permute-start | bytes 442376 | tf_op jit(solution)/shard_map/ppermute | solution.py:463
  24.1 5.1 %collective-permute-start.6 = (bf16[144,512]{1,0:T(8,128)(2,1)S(1)}, bf16[144,512]{1,0:T(8,128)(2,1)S(1)}, u32[]{:S(2)}, u32[]{:S(2)}) collective-permute-start(bf16[144,512]{1,0:T(8,128)(2,1)S(1)} %collective-permute-done.5.refs_11_.refs_7_), channel_id=1, source_target_pairs={{0,4},{1,5},{4,8},{5,9},{8,12},{9,13},{12,14},{13,15},{14,10},{15,... | collective-permute-start | bytes 442376 | tf_op jit(solution)/shard_map/ppermute | solution.py:460
  25.7 5.6 %collective-permute-start.14 = (bf16[128,3072]{1,0:T(8,128)(2,1)S(1)}, bf16[128,3072]{1,0:T(8,128)(2,1)S(1)}, u32[]{:S(2)}, u32[]{:S(2)}) collective-permute-start(bf16[128,3072]{1,0:T(8,128)(2,1)S(1)} %get-tuple-element.103.refs_0_), channel_id=1, source_target_pairs={{0,1},{1,0},{2,3},{3,2},{4,5},{5,4},{6,7},{7,6},{8,9},{9,8},{10,11... | collective-permute-start | bytes 2359304 | tf_op jit(solution)/shard_map/ppermute | solution.py:466
  29.3 2.3 %collective-permute-start.15 = (bf16[128,3072]{1,0:T(8,128)(2,1)S(1)}, bf16[128,3072]{1,0:T(8,128)(2,1)S(1)}, u32[]{:S(2)}, u32[]{:S(2)}) collective-permute-start(bf16[128,3072]{1,0:T(8,128)(2,1)S(1)} %collective-permute-done.13.refs_1_), channel_id=1, source_target_pairs={{0,1},{1,0},{2,3},{3,2},{4,5},{5,4},{6,7},{7,6},{8,9},{9,8},{10,11... | collective-permute-start | bytes 2359304 | tf_op jit(solution)/shard_map/ppermute | solution.py:466
  29.3 6.3 %collective-permute-start.16 = (bf16[144,512]{1,0:T(8,128)(2,1)S(1)}, bf16[144,512]{1,0:T(8,128)(2,1)S(1)}, u32[]{:S(2)}, u32[]{:S(2)}) collective-permute-start(bf16[144,512]{1,0:T(8,128)(2,1)S(1)} %collective-permute-done.2.refs_14_.refs_2_), channel_id=1, source_target_pairs={{0,4},{1,5},{4,8},{5,9},{8,12},{9,13},{12,14},{13,15},{14,10},{15,... | collective-permute-start | bytes 442376 | tf_op jit(solution)/shard_map/ppermute | solution.py:460
  30.9 6.0 %collective-permute-start.17 = (bf16[144,512]{1,0:T(8,128)(2,1)S(1)}, bf16[144,512]{1,0:T(8,128)(2,1)S(1)}, u32[]{:S(2)}, u32[]{:S(2)}) collective-permute-start(bf16[144,512]{1,0:T(8,128)(2,1)S(1)} %collective-permute-done.12.refs_17_.refs_5_), channel_id=1, source_target_pairs={{4,0},{5,1},{8,4},{9,5},{12,8},{13,9},{14,12},{15,13},{10,14},{11,... | collective-permute-start | bytes 442376 | tf_op jit(solution)/shard_map/ppermute | solution.py:463
  32.2 20.6 %slice-start = ((s8[5767168]{0:T(1024)(128)(4,1)}), s8[4194304]{0:T(1024)(128)(4,1)S(1)}, s32[]{:S(2)}) async-start(s8[5767168]{0:T(1024)(128)(4,1)} %bitcast.12), calls=%async_computation | async-start | bytes 8388608
  33.9 18.9 %slice-start.1 = ((s8[5767168]{0:T(1024)(128)(4,1)}), s8[1572864]{0:T(1024)(128)(4,1)S(1)}, s32[]{:S(2)}) async-start(s8[5767168]{0:T(1024)(128)(4,1)} %bitcast.12), calls=%async_computation.1 | async-start | bytes 3145728
  37.7 1.4 collective-permute-start.18
  39.7 9.0 %collective-permute-start.19 = (bf16[128,1024]{1,0:T(8,128)(2,1)S(1)}, bf16[128,1024]{1,0:T(8,128)(2,1)S(1)}, u32[]{:S(2)}, u32[]{:S(2)}) collective-permute-start(bf16[128,1024]{1,0:T(8,128)(2,1)S(1)} %beside.2.refs_0_), channel_id=1, source_target_pairs={{0,4},{1,5},{4,8},{5,9},{8,12},{9,13},{12,14},{13,15},{14,10},{15,... | collective-permute-start | bytes 786440 | tf_op jit(solution)/shard_map/ppermute | solution.py:460
  41.3 8.1 %collective-permute-start.20 = (bf16[128,1024]{1,0:T(8,128)(2,1)S(1)}, bf16[128,1024]{1,0:T(8,128)(2,1)S(1)}, u32[]{:S(2)}, u32[]{:S(2)}) collective-permute-start(bf16[128,1024]{1,0:T(8,128)(2,1)S(1)} %beside.2.refs_0_), channel_id=1, source_target_pairs={{4,0},{5,1},{8,4},{9,5},{12,8},{13,9},{14,12},{15,13},{10,14},{11,... | collective-permute-start | bytes 786440 | tf_op jit(solution)/shard_map/ppermute | solution.py:463
  41.8 6.4 %collective-permute-start.21 = (bf16[128,512]{1,0:T(8,128)(2,1)S(1)}, bf16[128,512]{1,0:T(8,128)(2,1)S(1)}, u32[]{:S(2)}, u32[]{:S(2)}) collective-permute-start(bf16[128,512]{1,0:T(8,128)(2,1)S(1)} %get-tuple-element.118), channel_id=1, source_target_pairs={{0,16},{1,17},{2,18},{3,19},{4,20},{5,21},{6,22},{7,23},{8,24},{9,... | collective-permute-start | bytes 393224 | tf_op jit(solution)/shard_map/ppermute | solution.py:474
  42.3 5.9 %collective-permute-start.22 = (bf16[128,512]{1,0:T(8,128)(2,1)S(1)}, bf16[128,512]{1,0:T(8,128)(2,1)S(1)}, u32[]{:S(2)}, u32[]{:S(2)}) collective-permute-start(bf16[128,512]{1,0:T(8,128)(2,1)S(1)} %get-tuple-element.119), channel_id=1, source_target_pairs={{0,17},{1,16},{2,19},{3,18},{4,21},{5,20},{6,23},{7,22},{8,25},{9,... | collective-permute-start | bytes 393224 | tf_op jit(solution)/shard_map/ppermute | solution.py:474
  50.0 2.8 %collective-permute-start.25 = (bf16[128,2048]{1,0:T(8,128)(2,1)S(1)}, bf16[128,2048]{1,0:T(8,128)(2,1)S(1)}, u32[]{:S(2)}, u32[]{:S(2)}) collective-permute-start(bf16[128,2048]{1,0:T(8,128)(2,1)S(1)} %weave.3.refs_0_.refs_1_), channel_id=1, source_target_pairs={{0,1},{1,0},{2,3},{3,2},{4,5},{5,4},{6,7},{7,6},{8,9},{9,8},{10,11... | collective-permute-start | bytes 1572872 | tf_op jit(solution)/shard_map/ppermute | solution.py:466
  50.8 8.3 %collective-permute-start.23 = (bf16[128,1024]{1,0:T(8,128)(2,1)S(1)}, bf16[128,1024]{1,0:T(8,128)(2,1)S(1)}, u32[]{:S(2)}, u32[]{:S(2)}) collective-permute-start(bf16[128,1024]{1,0:T(8,128)(2,1)S(1)} %beside.3.refs_1_), channel_id=1, source_target_pairs={{0,4},{1,5},{4,8},{5,9},{8,12},{9,13},{12,14},{13,15},{14,10},{15,... | collective-permute-start | bytes 786440 | tf_op jit(solution)/shard_map/ppermute | solution.py:460
  52.3 8.0 %collective-permute-start.24 = (bf16[128,1024]{1,0:T(8,128)(2,1)S(1)}, bf16[128,1024]{1,0:T(8,128)(2,1)S(1)}, u32[]{:S(2)}, u32[]{:S(2)}) collective-permute-start(bf16[128,1024]{1,0:T(8,128)(2,1)S(1)} %beside.3.refs_1_), channel_id=1, source_target_pairs={{4,0},{5,1},{8,4},{9,5},{12,8},{13,9},{14,12},{15,13},{10,14},{11,... | collective-permute-start | bytes 786440 | tf_op jit(solution)/shard_map/ppermute | solution.py:463
  60.9 3.8 %collective-permute-start.29 = (bf16[128,2048]{1,0:T(8,128)(2,1)S(1)}, bf16[128,2048]{1,0:T(8,128)(2,1)S(1)}, u32[]{:S(2)}, u32[]{:S(2)}) collective-permute-start(bf16[128,2048]{1,0:T(8,128)(2,1)S(1)} %weave.5.refs_2_), channel_id=1, source_target_pairs={{0,1},{1,0},{2,3},{3,2},{4,5},{5,4},{6,7},{7,6},{8,9},{9,8},{10,11... | collective-permute-start | bytes 1572872 | tf_op jit(solution)/shard_map/ppermute | solution.py:466
  61.6 3.1 %collective-permute-start.28 = (bf16[128,2048]{1,0:T(8,128)(2,1)S(1)}, bf16[128,2048]{1,0:T(8,128)(2,1)S(1)}, u32[]{:S(2)}, u32[]{:S(2)}) collective-permute-start(bf16[128,2048]{1,0:T(8,128)(2,1)S(1)} %weave.4.refs_0_), channel_id=1, source_target_pairs={{0,1},{1,0},{2,3},{3,2},{4,5},{5,4},{6,7},{7,6},{8,9},{9,8},{10,11... | collective-permute-start | bytes 1572872 | tf_op jit(solution)/shard_map/ppermute | solution.py:466
  62.1 13.9 %collective-permute-start.27 = (bf16[128,2048]{1,0:T(8,128)(2,1)S(1)}, bf16[128,2048]{1,0:T(8,128)(2,1)S(1)}, u32[]{:S(2)}, u32[]{:S(2)}) collective-permute-start(bf16[128,2048]{1,0:T(8,128)(2,1)S(1)} %weave.5.refs_2_), channel_id=1, source_target_pairs={{4,0},{5,1},{8,4},{9,5},{12,8},{13,9},{14,12},{15,13},{10,14},{11,... | collective-permute-start | bytes 1572872 | tf_op jit(solution)/shard_map/ppermute | solution.py:463
  62.6 13.7 %collective-permute-start.26 = (bf16[128,2048]{1,0:T(8,128)(2,1)S(1)}, bf16[128,2048]{1,0:T(8,128)(2,1)S(1)}, u32[]{:S(2)}, u32[]{:S(2)}) collective-permute-start(bf16[128,2048]{1,0:T(8,128)(2,1)S(1)} %weave.4.refs_0_), channel_id=1, source_target_pairs={{0,4},{1,5},{4,8},{5,9},{8,12},{9,13},{12,14},{13,15},{14,10},{15,... | collective-permute-start | bytes 1572872 | tf_op jit(solution)/shard_map/ppermute | solution.py:460
  64.2 13.4 %collective-permute-start.30 = (bf16[128,2048]{1,0:T(8,128)(2,1)S(1)}, bf16[128,2048]{1,0:T(8,128)(2,1)S(1)}, u32[]{:S(2)}, u32[]{:S(2)}) collective-permute-start(bf16[128,2048]{1,0:T(8,128)(2,1)S(1)} %weave.3.refs_0_.refs_1_), channel_id=1, source_target_pairs={{0,16},{1,17},{2,18},{3,19},{4,20},{5,21},{6,22},{7,23},{8,24},{9,... | collective-permute-start | bytes 1572872 | tf_op jit(solution)/shard_map/ppermute | solution.py:474
  77.5 7.4 %collective-permute-start.33 = (bf16[128,2048]{1,0:T(8,128)(2,1)S(1)}, bf16[128,2048]{1,0:T(8,128)(2,1)S(1)}, u32[]{:S(2)}, u32[]{:S(2)}) collective-permute-start(bf16[128,2048]{1,0:T(8,128)(2,1)S(1)} %collective-permute-done.26.refs_0_), channel_id=1, source_target_pairs={{0,1},{1,0},{2,3},{3,2},{4,5},{5,4},{6,7},{7,6},{8,9},{9,8},{10,11... | collective-permute-start | bytes 1572872 | tf_op jit(solution)/shard_map/ppermute | solution.py:466
  77.5 7.4 %collective-permute-start.34 = (bf16[128,2048]{1,0:T(8,128)(2,1)S(1)}, bf16[128,2048]{1,0:T(8,128)(2,1)S(1)}, u32[]{:S(2)}, u32[]{:S(2)}) collective-permute-start(bf16[128,2048]{1,0:T(8,128)(2,1)S(1)} %collective-permute-done.27.refs_2_), channel_id=1, source_target_pairs={{0,1},{1,0},{2,3},{3,2},{4,5},{5,4},{6,7},{7,6},{8,9},{9,8},{10,11... | collective-permute-start | bytes 1572872 | tf_op jit(solution)/shard_map/ppermute | solution.py:466
  78.0 15.6 %collective-permute-start.35 = (bf16[128,2048]{1,0:T(8,128)(2,1)S(1)}, bf16[128,2048]{1,0:T(8,128)(2,1)S(1)}, u32[]{:S(2)}, u32[]{:S(2)}) collective-permute-start(bf16[128,2048]{1,0:T(8,128)(2,1)S(1)} %get-tuple-element.167), channel_id=1, source_target_pairs={{0,1},{1,0},{2,3},{3,2},{4,5},{5,4},{6,7},{7,6},{8,9},{9,8},{10,11... | collective-permute-start | bytes 1572872 | tf_op jit(solution)/shard_map/ppermute | solution.py:466
  78.0 14.3 %collective-permute-start.31 = (bf16[128,2048]{1,0:T(8,128)(2,1)S(1)}, bf16[128,2048]{1,0:T(8,128)(2,1)S(1)}, u32[]{:S(2)}, u32[]{:S(2)}) collective-permute-start(bf16[128,2048]{1,0:T(8,128)(2,1)S(1)} %collective-permute-done.26.refs_0_), channel_id=1, source_target_pairs={{0,4},{1,5},{4,8},{5,9},{8,12},{9,13},{12,14},{13,15},{14,10},{15,... | collective-permute-start | bytes 1572872 | tf_op jit(solution)/shard_map/ppermute | solution.py:460
  79.5 14.1 %collective-permute-start.32 = (bf16[128,2048]{1,0:T(8,128)(2,1)S(1)}, bf16[128,2048]{1,0:T(8,128)(2,1)S(1)}, u32[]{:S(2)}, u32[]{:S(2)}) collective-permute-start(bf16[128,2048]{1,0:T(8,128)(2,1)S(1)} %collective-permute-done.27.refs_2_), channel_id=1, source_target_pairs={{4,0},{5,1},{8,4},{9,5},{12,8},{13,9},{14,12},{15,13},{10,14},{11,... | collective-permute-start | bytes 1572872 | tf_op jit(solution)/shard_map/ppermute | solution.py:463
  93.6 1.9 %collective-permute-start.37 = (bf16[128,2048]{1,0:T(8,128)(2,1)S(1)}, bf16[128,2048]{1,0:T(8,128)(2,1)S(1)}, u32[]{:S(2)}, u32[]{:S(2)}) collective-permute-start(bf16[128,2048]{1,0:T(8,128)(2,1)S(1)} %collective-permute-done.31.refs_0_), channel_id=1, source_target_pairs={{0,1},{1,0},{2,3},{3,2},{4,5},{5,4},{6,7},{7,6},{8,9},{9,8},{10,11... | collective-permute-start | bytes 1572872 | tf_op jit(solution)/shard_map/ppermute | solution.py:466
  93.6 2.7 %collective-permute-start.38 = (bf16[128,2048]{1,0:T(8,128)(2,1)S(1)}, bf16[128,2048]{1,0:T(8,128)(2,1)S(1)}, u32[]{:S(2)}, u32[]{:S(2)}) collective-permute-start(bf16[128,2048]{1,0:T(8,128)(2,1)S(1)} %collective-permute-done.32.refs_2_), channel_id=1, source_target_pairs={{0,1},{1,0},{2,3},{3,2},{4,5},{5,4},{6,7},{7,6},{8,9},{9,8},{10,11... | collective-permute-start | bytes 1572872 | tf_op jit(solution)/shard_map/ppermute | solution.py:466
  94.1 18.3 %collective-permute-start.36 = (bf16[256,2048]{1,0:T(8,128)(2,1)S(1)}, bf16[256,2048]{1,0:T(8,128)(2,1)S(1)}, u32[]{:S(2)}, u32[]{:S(2)}) collective-permute-start(bf16[256,2048]{1,0:T(8,128)(2,1)S(1)} %get-tuple-element.164.refs_2_), channel_id=1, source_target_pairs={{0,1},{1,0},{2,3},{3,2},{4,5},{5,4},{6,7},{7,6},{8,9},{9,8},{10,11... | collective-permute-start | bytes 3145736 | tf_op jit(solution)/shard_map/ppermute | solution.py:466
  96.3 16.1 %collective-permute-start.39 = (bf16[256,2048]{1,0:T(8,128)(2,1)S(1)}, bf16[256,2048]{1,0:T(8,128)(2,1)S(1)}, u32[]{:S(2)}, u32[]{:S(2)}) collective-permute-start(bf16[256,2048]{1,0:T(8,128)(2,1)S(1)} %get-tuple-element.174), channel_id=1, source_target_pairs={{0,1},{1,0},{2,3},{3,2},{4,5},{5,4},{6,7},{7,6},{8,9},{9,8},{10,11... | collective-permute-start | bytes 3145736 | tf_op jit(solution)/shard_map/ppermute | solution.py:466
  96.5 9.3 %collective-permute-start.40 = (bf16[64,2048]{1,0:T(8,128)(2,1)S(1)}, bf16[64,2048]{1,0:T(8,128)(2,1)S(1)}, u32[]{:S(2)}, u32[]{:S(2)}) collective-permute-start(bf16[64,2048]{1,0:T(8,128)(2,1)S(1)} %slice.6), channel_id=1, source_target_pairs={{0,4},{1,5},{4,8},{5,9},{8,12},{9,13},{12,14},{13,15},{14,10},{15,... | collective-permute-start | bytes 786440 | tf_op jit(solution)/shard_map/ppermute | solution.py:460
  98.0 8.3 %collective-permute-start.41 = (bf16[64,2048]{1,0:T(8,128)(2,1)S(1)}, bf16[64,2048]{1,0:T(8,128)(2,1)S(1)}, u32[]{:S(2)}, u32[]{:S(2)}) collective-permute-start(bf16[64,2048]{1,0:T(8,128)(2,1)S(1)} %slice.7), channel_id=1, source_target_pairs={{4,0},{5,1},{8,4},{9,5},{12,8},{13,9},{14,12},{15,13},{10,14},{11,... | collective-permute-start | bytes 786440 | tf_op jit(solution)/shard_map/ppermute | solution.py:463
  106.3 1.5 collective-permute-start.42
  106.3 1.9 %collective-permute-start.43 = (bf16[64,2048]{1,0:T(8,128)(2,1)S(1)}, bf16[64,2048]{1,0:T(8,128)(2,1)S(1)}, u32[]{:S(2)}, u32[]{:S(2)}) collective-permute-start(bf16[64,2048]{1,0:T(8,128)(2,1)S(1)} %collective-permute-done.41.refs_1_), channel_id=1, source_target_pairs={{0,1},{1,0},{2,3},{3,2},{4,5},{5,4},{6,7},{7,6},{8,9},{9,8},{10,11... | collective-permute-start | bytes 786440 | tf_op jit(solution)/shard_map/ppermute | solution.py:466
  106.8 9.9 %collective-permute-start.44 = (bf16[256,2048]{1,0:T(8,128)(2,1)S(1)}, bf16[256,2048]{1,0:T(8,128)(2,1)S(1)}, u32[]{:S(2)}, u32[]{:S(2)}) collective-permute-start(bf16[256,2048]{1,0:T(8,128)(2,1)S(1)} %get-tuple-element.189), channel_id=1, source_target_pairs={{0,1},{1,0},{2,3},{3,2},{4,5},{5,4},{6,7},{7,6},{8,9},{9,8},{10,11... | collective-permute-start | bytes 3145736 | tf_op jit(solution)/shard_map/ppermute | solution.py:466
  112.4 2.0 %collective-permute-start.45 = (bf16[128,2048]{1,0:T(8,128)(2,1)S(1)}, bf16[128,2048]{1,0:T(8,128)(2,1)S(1)}, u32[]{:S(2)}, u32[]{:S(2)}) collective-permute-start(bf16[128,2048]{1,0:T(8,128)(2,1)S(1)} %get-tuple-element.191), channel_id=1, source_target_pairs={{0,1},{1,0},{2,3},{3,2},{4,5},{5,4},{6,7},{7,6},{8,9},{9,8},{10,11... | collective-permute-start | bytes 1572872 | tf_op jit(solution)/shard_map/ppermute | solution.py:466
  112.6 14.2 %collective-permute-start.48 = (bf16[128,2048]{1,0:T(8,128)(2,1)S(1)}, bf16[128,2048]{1,0:T(8,128)(2,1)S(1)}, u32[]{:S(2)}, u32[]{:S(2)}) collective-permute-start(bf16[128,2048]{1,0:T(8,128)(2,1)S(1)} %get-tuple-element.166), channel_id=1, source_target_pairs={{0,16},{1,17},{2,18},{3,19},{4,20},{5,21},{6,22},{7,23},{8,24},{9,... | collective-permute-start | bytes 1572872 | tf_op jit(solution)/shard_map/ppermute | solution.py:474
  114.4 9.2 %collective-permute-start.47 = (bf16[64,2048]{1,0:T(8,128)(2,1)S(1)}, bf16[64,2048]{1,0:T(8,128)(2,1)S(1)}, u32[]{:S(2)}, u32[]{:S(2)}) collective-permute-start(bf16[64,2048]{1,0:T(8,128)(2,1)S(1)} %add.23.refs_2_), channel_id=1, source_target_pairs={{4,0},{5,1},{8,4},{9,5},{12,8},{13,9},{14,12},{15,13},{10,14},{11,... | collective-permute-start | bytes 786440 | tf_op jit(solution)/shard_map/ppermute | solution.py:463
  115.1 9.2 %collective-permute-start.46 = (bf16[64,2048]{1,0:T(8,128)(2,1)S(1)}, bf16[64,2048]{1,0:T(8,128)(2,1)S(1)}, u32[]{:S(2)}, u32[]{:S(2)}) collective-permute-start(bf16[64,2048]{1,0:T(8,128)(2,1)S(1)} %add.24.refs_2_), channel_id=1, source_target_pairs={{0,4},{1,5},{4,8},{5,9},{8,12},{9,13},{12,14},{13,15},{14,10},{15,... | collective-permute-start | bytes 786440 | tf_op jit(solution)/shard_map/ppermute | solution.py:460
  116.7 12.6 %collective-permute-start.49 = (bf16[64,2048]{1,0:T(8,128)(2,1)S(1)}, bf16[64,2048]{1,0:T(8,128)(2,1)S(1)}, u32[]{:S(2)}, u32[]{:S(2)}) collective-permute-start(bf16[64,2048]{1,0:T(8,128)(2,1)S(1)} %add.25.refs_2_), channel_id=1, source_target_pairs={{4,0},{5,1},{8,4},{9,5},{12,8},{13,9},{14,12},{15,13},{10,14},{11,... | collective-permute-start | bytes 786440 | tf_op jit(solution)/shard_map/ppermute | solution.py:463
  117.4 12.6 %collective-permute-start.53 = (bf16[64,2048]{1,0:T(8,128)(2,1)S(1)}, bf16[64,2048]{1,0:T(8,128)(2,1)S(1)}, u32[]{:S(2)}, u32[]{:S(2)}) collective-permute-start(bf16[64,2048]{1,0:T(8,128)(2,1)S(1)} %add.26.refs_3_), channel_id=1, source_target_pairs={{0,4},{1,5},{4,8},{5,9},{8,12},{9,13},{12,14},{13,15},{14,10},{15,... | collective-permute-start | bytes 786440 | tf_op jit(solution)/shard_map/ppermute | solution.py:460
  123.7 11.1 %collective-permute-start.52 = (bf16[64,2048]{1,0:T(8,128)(2,1)S(1)}, bf16[64,2048]{1,0:T(8,128)(2,1)S(1)}, u32[]{:S(2)}, u32[]{:S(2)}) collective-permute-start(bf16[64,2048]{1,0:T(8,128)(2,1)S(1)} %add.27.refs_3_), channel_id=1, source_target_pairs={{4,0},{5,1},{8,4},{9,5},{12,8},{13,9},{14,12},{15,13},{10,14},{11,... | collective-permute-start | bytes 786440 | tf_op jit(solution)/shard_map/ppermute | solution.py:463
  124.5 11.1 %collective-permute-start.51 = (bf16[64,2048]{1,0:T(8,128)(2,1)S(1)}, bf16[64,2048]{1,0:T(8,128)(2,1)S(1)}, u32[]{:S(2)}, u32[]{:S(2)}) collective-permute-start(bf16[64,2048]{1,0:T(8,128)(2,1)S(1)} %add.28.refs_3_), channel_id=1, source_target_pairs={{0,4},{1,5},{4,8},{5,9},{8,12},{9,13},{12,14},{13,15},{14,10},{15,... | collective-permute-start | bytes 786440 | tf_op jit(solution)/shard_map/ppermute | solution.py:460
  129.3 11.1 %collective-permute-start.50 = (bf16[64,2048]{1,0:T(8,128)(2,1)S(1)}, bf16[64,2048]{1,0:T(8,128)(2,1)S(1)}, u32[]{:S(2)}, u32[]{:S(2)}) collective-permute-start(bf16[64,2048]{1,0:T(8,128)(2,1)S(1)} %add.29.refs_3_), channel_id=1, source_target_pairs={{4,0},{5,1},{8,4},{9,5},{12,8},{13,9},{14,12},{15,13},{10,14},{11,... | collective-permute-start | bytes 786440 | tf_op jit(solution)/shard_map/ppermute | solution.py:463
  130.1 11.1 %collective-permute-start.55 = (bf16[64,2048]{1,0:T(8,128)(2,1)S(1)}, bf16[64,2048]{1,0:T(8,128)(2,1)S(1)}, u32[]{:S(2)}, u32[]{:S(2)}) collective-permute-start(bf16[64,2048]{1,0:T(8,128)(2,1)S(1)} %add.30.refs_3_), channel_id=1, source_target_pairs={{0,4},{1,5},{4,8},{5,9},{8,12},{9,13},{12,14},{13,15},{14,10},{15,... | collective-permute-start | bytes 786440 | tf_op jit(solution)/shard_map/ppermute | solution.py:460
  135.0 11.1 %collective-permute-start.58 = (bf16[64,2048]{1,0:T(8,128)(2,1)S(1)}, bf16[64,2048]{1,0:T(8,128)(2,1)S(1)}, u32[]{:S(2)}, u32[]{:S(2)}) collective-permute-start(bf16[64,2048]{1,0:T(8,128)(2,1)S(1)} %add.31.refs_3_), channel_id=1, source_target_pairs={{4,0},{5,1},{8,4},{9,5},{12,8},{13,9},{14,12},{15,13},{10,14},{11,... | collective-permute-start | bytes 786440 | tf_op jit(solution)/shard_map/ppermute | solution.py:463
  135.7 11.1 %collective-permute-start.57 = (bf16[64,2048]{1,0:T(8,128)(2,1)S(1)}, bf16[64,2048]{1,0:T(8,128)(2,1)S(1)}, u32[]{:S(2)}, u32[]{:S(2)}) collective-permute-start(bf16[64,2048]{1,0:T(8,128)(2,1)S(1)} %add.32.refs_3_), channel_id=1, source_target_pairs={{0,4},{1,5},{4,8},{5,9},{8,12},{9,13},{12,14},{13,15},{14,10},{15,... | collective-permute-start | bytes 786440 | tf_op jit(solution)/shard_map/ppermute | solution.py:460
  140.6 11.9 %collective-permute-start.54 = (bf16[64,2048]{1,0:T(8,128)(2,1)S(1)}, bf16[64,2048]{1,0:T(8,128)(2,1)S(1)}, u32[]{:S(2)}, u32[]{:S(2)}) collective-permute-start(bf16[64,2048]{1,0:T(8,128)(2,1)S(1)} %add.33.refs_3_), channel_id=1, source_target_pairs={{4,0},{5,1},{8,4},{9,5},{12,8},{13,9},{14,12},{15,13},{10,14},{11,... | collective-permute-start | bytes 786440 | tf_op jit(solution)/shard_map/ppermute | solution.py:463
  141.3 11.1 %collective-permute-start.56 = (bf16[64,2048]{1,0:T(8,128)(2,1)S(1)}, bf16[64,2048]{1,0:T(8,128)(2,1)S(1)}, u32[]{:S(2)}, u32[]{:S(2)}) collective-permute-start(bf16[64,2048]{1,0:T(8,128)(2,1)S(1)} %add.34.refs_3_), channel_id=1, source_target_pairs={{0,4},{1,5},{4,8},{5,9},{8,12},{9,13},{12,14},{13,15},{14,10},{15,... | collective-permute-start | bytes 786440 | tf_op jit(solution)/shard_map/ppermute | solution.py:460
  146.9 10.0 %collective-permute-start.59 = (bf16[64,2048]{1,0:T(8,128)(2,1)S(1)}, bf16[64,2048]{1,0:T(8,128)(2,1)S(1)}, u32[]{:S(2)}, u32[]{:S(2)}) collective-permute-start(bf16[64,2048]{1,0:T(8,128)(2,1)S(1)} %add.36), channel_id=1, source_target_pairs={{0,4},{1,5},{4,8},{5,9},{8,12},{9,13},{12,14},{13,15},{14,10},{15,... | collective-permute-start | bytes 786440 | tf_op jit(solution)/shard_map/ppermute | solution.py:460
  148.4 8.5 %collective-permute-start.60 = (bf16[64,2048]{1,0:T(8,128)(2,1)S(1)}, bf16[64,2048]{1,0:T(8,128)(2,1)S(1)}, u32[]{:S(2)}, u32[]{:S(2)}) collective-permute-start(bf16[64,2048]{1,0:T(8,128)(2,1)S(1)} %add.35.refs_3_), channel_id=1, source_target_pairs={{4,0},{5,1},{8,4},{9,5},{12,8},{13,9},{14,12},{15,13},{10,14},{11,... | collective-permute-start | bytes 786440 | tf_op jit(solution)/shard_map/ppermute | solution.py:463
  (3 other events, 38.4 us)

commit v4 on v3

--- a/solution.py
+++ b/solution.py
@@ -11,6 +11,8 @@
 BF16 = jnp.bfloat16
 VMEM_BYTES = 12 * 1024 * 1024
 TILE = 512
+HIDDEN_TILE = 768
+DOWN_TILE = 1024
 TABLE_ROWS = 16
 
 
@@ -265,14 +267,14 @@
         scale = lax.rsqrt(jnp.sum(taken * taken, axis=1, keepdims=True) * (1.0 / width) + 1e-06)
         normed[b * slots : (b + 1) * slots, :] = (taken * scale * gain_ref[...]).astype(BF16)
 
-    for start in range(0, hidden_units, TILE):
-        columns = slice(start, min(start + TILE, hidden_units))
+    for start in range(0, hidden_units, HIDDEN_TILE):
+        columns = slice(start, min(start + HIDDEN_TILE, hidden_units))
         gate_part = mm(normed[...], gate_ref[:, columns])
         up_part = mm(normed[...], up_ref[:, columns])
         hidden[:, columns] = (jax.nn.silu(gate_part) * up_part).astype(BF16)
 
-    for start in range(0, width, TILE):
-        columns = slice(start, start + TILE)
+    for start in range(0, width, DOWN_TILE):
+        columns = slice(start, start + DOWN_TILE)
         result = mm(hidden[...], down_ref[:, columns])
         for b in range(blocks):
             weighted = (result[b * slots : (b + 1) * slots] * factor_ref[first + b]).astype(BF16)

time: 158 us -> 158 us (level)
  Pallas kernels: 47.7 us -> 46 us
    pallas_call x5, Pallas kernels: 30 us -> 28.3 us  [expert(): pl.pallas_call(functools.partial(expert_kernel, first, blocks, len(inputs...]
  transfers between devices with their start and end apart: 61 -> 61, of which waited for: 34 -> 34; matrix products, arithmetic and copies ran while one was open for 0% -> 0% of each run, Pallas kernels for 27% -> 25%
where the time goes in v4:
time: 158 us; the launch traced here: 157 us
  waiting for transfers between devices  62.6 us (40%)
  starting transfers between devices  47.8 us (30%)
  Pallas kernels  46 us (29%)
    ppermute x19, waiting for transfers between devices, to_behind(): return lax.ppermute(x, 'exp', behind)  35.3 us
    ppermute x19, starting transfers between devices, to_ahead(): return lax.ppermute(x, 'exp', ahead)  28.3 us
    pallas_call x5, Pallas kernels, expert(): pl.pallas_call(functools.partial(expert_kernel, first, blocks, len(inputs...  28.3 us
    ppermute x19, waiting for transfers between devices, to_ahead(): return lax.ppermute(x, 'exp', ahead)  16 us
    ppermute x19, starting transfers between devices, to_behind(): return lax.ppermute(x, 'exp', behind)  11 us
    ppermute x18, waiting for transfers between devices, to_core(): return lax.ppermute(x, 'exp', [(d, d ^ 1) for d in range(exp_size)])  6.28 us
    ppermute x5, starting transfers between devices, to_request(): return lax.ppermute(x, ('req', 'exp'), pairs)  5.11 us
    ppermute x5, waiting for transfers between devices, to_request(): return lax.ppermute(x, ('req', 'exp'), pairs)  4.92 us
  transfers between devices with their start and end apart: 61, of which 34 were waited for; matrix products, arithmetic and copies ran while one was open for 0% of the time, Pallas kernels for 25%

profile of v4, /device:TPU:0, one launch (start us, length us, event | category | flops | bytes accessed | tf_op | source)
XLA Modules:
  0.0 157.5 jit_solution(3177456123888165099)
XLA Ops:
  0.1 2.4 %prepare.1 = (bf16[144,512]{1,0:T(8,128)(2,1)S(1)}, bf16[144,512]{1,0:T(8,128)(2,1)S(1)}, bf16[128,3072]{1,0:T(8,128)(2,1)S(1)}, bf16[128,3072]{1,0:T(8,128)(2,1)S(1)}) custom-call(s32[3]{0:T(128)S(1)} %pad_add_fusion.where_ref, s32[6,128]{1,0:T(8,128)} %bitcast.35, f32[6,128]{1,0:T(8,128)} %bitcast.36, bf16[128,2048]{1,0:T(8,128)(2,1)} %weight_hbm.1, ...), custom_call_target="tpu_custom_call" | custom-call | bytes 2097152 | tf_op jit(solution)/shard_map/prepare/pallas_call | solution.py:92
  2.5 3.0 %collective-permute-start.13 = (bf16[128,3072]{1,0:T(8,128)(2,1)S(1)}, bf16[128,3072]{1,0:T(8,128)(2,1)S(1)}, u32[]{:S(2)}, u32[]{:S(2)}) collective-permute-start(bf16[128,3072]{1,0:T(8,128)(2,1)S(1)} %get-tuple-element.106), channel_id=1, source_target_pairs={{0,16},{1,17},{2,18},{3,19},{4,20},{5,21},{6,22},{7,23},{8,24},{9,... | collective-permute-start | bytes 2359304 | tf_op jit(solution)/shard_map/ppermute | solution.py:476
  5.5 1.6 %collective-permute-start = (bf16[144,512]{1,0:T(8,128)(2,1)S(1)}, bf16[144,512]{1,0:T(8,128)(2,1)S(1)}, u32[]{:S(2)}, u32[]{:S(2)}) collective-permute-start(bf16[144,512]{1,0:T(8,128)(2,1)S(1)} %get-tuple-element.120.refs_4_.refs_0_), channel_id=1, source_target_pairs={{0,4},{1,5},{4,8},{5,9},{8,12},{9,13},{12,14},{13,15},{14,10},{15,... | collective-permute-start | bytes 442376 | tf_op jit(solution)/shard_map/ppermute | solution.py:462
  7.5 1.5 collective-permute-start.10
  9.5 2.6 %collective-permute-done.refs_6_.refs_2_ = bf16[144,512]{1,0:T(8,128)(2,1)S(1)} collective-permute-done((bf16[144,512]{1,0:T(8,128)(2,1)S(1)}, bf16[144,512]{1,0:T(8,128)(2,1)S(1)}, u32[]{:S(2)}, u32[]{:S(2)}) %collective-permute-start) | collective-permute-done | bytes 147488 | tf_op jit(solution)/shard_map/ppermute | solution.py:462
  12.1 1.6 %collective-permute-start.1 = (bf16[144,512]{1,0:T(8,128)(2,1)S(1)}, bf16[144,512]{1,0:T(8,128)(2,1)S(1)}, u32[]{:S(2)}, u32[]{:S(2)}) collective-permute-start(bf16[144,512]{1,0:T(8,128)(2,1)S(1)} %collective-permute-done.refs_6_.refs_2_), channel_id=1, source_target_pairs={{0,4},{1,5},{4,8},{5,9},{8,12},{9,13},{12,14},{13,15},{14,10},{15,... | collective-permute-start | bytes 442376 | tf_op jit(solution)/shard_map/ppermute | solution.py:462
  14.2 2.7 %collective-permute-done.10.refs_9_.refs_5_ = bf16[144,512]{1,0:T(8,128)(2,1)S(1)} collective-permute-done((bf16[144,512]{1,0:T(8,128)(2,1)S(1)}, bf16[144,512]{1,0:T(8,128)(2,1)S(1)}, u32[]{:S(2)}, u32[]{:S(2)}) %collective-permute-start.10) | collective-permute-done | bytes 147488 | tf_op jit(solution)/shard_map/ppermute | solution.py:465
  17.3 1.6 %collective-permute-start.5 = (bf16[144,512]{1,0:T(8,128)(2,1)S(1)}, bf16[144,512]{1,0:T(8,128)(2,1)S(1)}, u32[]{:S(2)}, u32[]{:S(2)}) collective-permute-start(bf16[144,512]{1,0:T(8,128)(2,1)S(1)} %collective-permute-done.4.refs_7_.refs_3_), channel_id=1, source_target_pairs={{0,4},{1,5},{4,8},{5,9},{8,12},{9,13},{12,14},{13,15},{14,10},{15,... | collective-permute-start | bytes 442376 | tf_op jit(solution)/shard_map/ppermute | solution.py:462
  18.9 1.6 %collective-permute-start.2 = (bf16[144,512]{1,0:T(8,128)(2,1)S(1)}, bf16[144,512]{1,0:T(8,128)(2,1)S(1)}, u32[]{:S(2)}, u32[]{:S(2)}) collective-permute-start(bf16[144,512]{1,0:T(8,128)(2,1)S(1)} %collective-permute-done.1.refs_10_.refs_6_), channel_id=1, source_target_pairs={{0,4},{1,5},{4,8},{5,9},{8,12},{9,13},{12,14},{13,15},{14,10},{15,... | collective-permute-start | bytes 442376 | tf_op jit(solution)/shard_map/ppermute | solution.py:462
  21.0 2.7 %collective-permute-done.11.refs_13_.refs_9_ = bf16[144,512]{1,0:T(8,128)(2,1)S(1)} collective-permute-done((bf16[144,512]{1,0:T(8,128)(2,1)S(1)}, bf16[144,512]{1,0:T(8,128)(2,1)S(1)}, u32[]{:S(2)}, u32[]{:S(2)}) %collective-permute-start.11) | collective-permute-done | bytes 147488 | tf_op jit(solution)/shard_map/ppermute | solution.py:465
  24.1 1.6 %collective-permute-start.6 = (bf16[144,512]{1,0:T(8,128)(2,1)S(1)}, bf16[144,512]{1,0:T(8,128)(2,1)S(1)}, u32[]{:S(2)}, u32[]{:S(2)}) collective-permute-start(bf16[144,512]{1,0:T(8,128)(2,1)S(1)} %collective-permute-done.5.refs_11_.refs_7_), channel_id=1, source_target_pairs={{0,4},{1,5},{4,8},{5,9},{8,12},{9,13},{12,14},{13,15},{14,10},{15,... | collective-permute-start | bytes 442376 | tf_op jit(solution)/shard_map/ppermute | solution.py:462
  25.7 1.5 collective-permute-done.9.refs_16_.refs_4_
  27.2 1.6 %collective-permute-done.12.refs_17_.refs_5_ = bf16[144,512]{1,0:T(8,128)(2,1)S(1)} collective-permute-done((bf16[144,512]{1,0:T(8,128)(2,1)S(1)}, bf16[144,512]{1,0:T(8,128)(2,1)S(1)}, u32[]{:S(2)}, u32[]{:S(2)}) %collective-permute-start.12) | collective-permute-done | bytes 147488 | tf_op jit(solution)/shard_map/ppermute | solution.py:465
  29.3 1.6 %collective-permute-start.16 = (bf16[144,512]{1,0:T(8,128)(2,1)S(1)}, bf16[144,512]{1,0:T(8,128)(2,1)S(1)}, u32[]{:S(2)}, u32[]{:S(2)}) collective-permute-start(bf16[144,512]{1,0:T(8,128)(2,1)S(1)} %collective-permute-done.2.refs_14_.refs_2_), channel_id=1, source_target_pairs={{0,4},{1,5},{4,8},{5,9},{8,12},{9,13},{12,14},{13,15},{14,10},{15,... | collective-permute-start | bytes 442376 | tf_op jit(solution)/shard_map/ppermute | solution.py:462
  31.6 0.7 copy-done.3
  32.2 1.7 %proj_part.1.refs_6_ = f32[512,512]{1,0:T(8,128)S(1)} custom-call(s32[3]{0:T(128)S(1)} %pad_add_fusion.where_ref, s32[16]{0:T(128)S(1)} %copy-done.3, bf16[128,3072]{1,0:T(8,128)(2,1)S(1)} %get-tuple-element.103.refs_0_, bf16[128,3072]{1,0:T(8,128)(2,1)S(1)} %collective-permute-done.13.refs_1_, bf16[128,3072]{1,0:T(8,128)(2,1)S(1)} %collective-permute-done.14.refs_2_, ...), custom_call_target="tpu_custom_call" | custom-call | flops 1879048192 | bytes 3932160 | tf_op jit(solution)/shard_map/proj_part/pallas_call | solution.py:191
  33.9 1.6 %collective-permute-done.16.refs_4_.refs_0_ = bf16[144,512]{1,0:T(8,128)(2,1)S(1)} collective-permute-done((bf16[144,512]{1,0:T(8,128)(2,1)S(1)}, bf16[144,512]{1,0:T(8,128)(2,1)S(1)}, u32[]{:S(2)}, u32[]{:S(2)}) %collective-permute-start.16) | collective-permute-done | bytes 147488 | tf_op jit(solution)/shard_map/ppermute | solution.py:462
  35.5 1.3 collective-permute-done.17.refs_5_.refs_1_
  36.8 0.9 proj_final.1
  37.8 1.3 collective-permute-done.18.refs_1_
  39.7 1.6 %collective-permute-start.19 = (bf16[128,1024]{1,0:T(8,128)(2,1)S(1)}, bf16[128,1024]{1,0:T(8,128)(2,1)S(1)}, u32[]{:S(2)}, u32[]{:S(2)}) collective-permute-start(bf16[128,1024]{1,0:T(8,128)(2,1)S(1)} %beside.2.refs_0_), channel_id=1, source_target_pairs={{0,4},{1,5},{4,8},{5,9},{8,12},{9,13},{12,14},{13,15},{14,10},{15,... | collective-permute-start | bytes 786440 | tf_op jit(solution)/shard_map/ppermute | solution.py:462
  42.7 1.1 tables.3
  43.8 1.5 tables.2
  45.3 2.8 %collective-permute-done.21.refs_0_ = bf16[128,512]{1,0:T(8,128)(2,1)S(1)} collective-permute-done((bf16[128,512]{1,0:T(8,128)(2,1)S(1)}, bf16[128,512]{1,0:T(8,128)(2,1)S(1)}, u32[]{:S(2)}, u32[]{:S(2)}) %collective-permute-start.21) | collective-permute-done | bytes 131104 | tf_op jit(solution)/shard_map/ppermute | solution.py:476
  48.7 0.7 collective-permute-done.20.refs_0_
  50.0 0.8 collective-permute-start.25
  50.8 1.6 %collective-permute-start.23 = (bf16[128,1024]{1,0:T(8,128)(2,1)S(1)}, bf16[128,1024]{1,0:T(8,128)(2,1)S(1)}, u32[]{:S(2)}, u32[]{:S(2)}) collective-permute-start(bf16[128,1024]{1,0:T(8,128)(2,1)S(1)} %beside.3.refs_1_), channel_id=1, source_target_pairs={{0,4},{1,5},{4,8},{5,9},{8,12},{9,13},{12,14},{13,15},{14,10},{15,... | collective-permute-start | bytes 786440 | tf_op jit(solution)/shard_map/ppermute | solution.py:462
  52.8 3.8 %expert.5 = (bf16[128,2048]{1,0:T(8,128)(2,1)S(1)}, bf16[128,2048]{1,0:T(8,128)(2,1)S(1)}) custom-call(f32[1,2048]{1,0:T(1,128)S(1)} %bitcast.29, bf16[5,144,256]{2,1,0:T(8,128)(2,1)S(1)} %get-tuple-element.141.pick_ref, bf16[5,256,144]{2,1,0:T(8,128)(2,1)S(1)} %get-tuple-element.142.put_ref, f32[5,144,1]{2,1,0:T(8,128)S(1)} %get-tuple-element.143.factor_ref, ...), custom_call_target="tpu_custom_call" | custom-call | flops 830472192 | bytes 4194304 | tf_op jit(solution)/shard_map/expert/pallas_call | solution.py:292
  56.7 2.4 %collective-permute-done.23.refs_1_ = bf16[128,1024]{1,0:T(8,128)(2,1)S(1)} collective-permute-done((bf16[128,1024]{1,0:T(8,128)(2,1)S(1)}, bf16[128,1024]{1,0:T(8,128)(2,1)S(1)}, u32[]{:S(2)}, u32[]{:S(2)}) %collective-permute-start.23) | collective-permute-done | bytes 262176 | tf_op jit(solution)/shard_map/ppermute | solution.py:462
  59.0 1.3 collective-permute-done.24.refs_1_
  62.6 1.6 %collective-permute-start.26 = (bf16[128,2048]{1,0:T(8,128)(2,1)S(1)}, bf16[128,2048]{1,0:T(8,128)(2,1)S(1)}, u32[]{:S(2)}, u32[]{:S(2)}) collective-permute-start(bf16[128,2048]{1,0:T(8,128)(2,1)S(1)} %weave.4.refs_0_), channel_id=1, source_target_pairs={{0,4},{1,5},{4,8},{5,9},{8,12},{9,13},{12,14},{13,15},{14,10},{15,... | collective-permute-start | bytes 1572872 | tf_op jit(solution)/shard_map/ppermute | solution.py:462
  64.7 6.9 %expert.6 = (bf16[128,2048]{1,0:T(8,128)(2,1)S(1)}, bf16[128,2048]{1,0:T(8,128)(2,1)S(1)}, bf16[256,2048]{1,0:T(8,128)(2,1)S(1)}) custom-call(f32[1,2048]{1,0:T(1,128)S(1)} %bitcast.30, bf16[5,144,256]{2,1,0:T(8,128)(2,1)S(1)} %get-tuple-element.141.pick_ref, bf16[5,256,144]{2,1,0:T(8,128)(2,1)S(1)} %get-tuple-element.142.put_ref, ...), custom_call_target="tpu_custom_call" | custom-call | flops 1660944384 | bytes 8388608 | tf_op jit(solution)/shard_map/expert/pallas_call | solution.py:292
  71.6 4.4 %collective-permute-done.27.refs_2_ = bf16[128,2048]{1,0:T(8,128)(2,1)S(1)} collective-permute-done((bf16[128,2048]{1,0:T(8,128)(2,1)S(1)}, bf16[128,2048]{1,0:T(8,128)(2,1)S(1)}, u32[]{:S(2)}, u32[]{:S(2)}) %collective-permute-start.27) | collective-permute-done | bytes 524320 | tf_op jit(solution)/shard_map/ppermute | solution.py:465
  76.3 1.2 collective-permute-done.30.refs_1_
  78.0 1.5 collective-permute-start.31
  80.1 4.8 %shared.1 = (f32[128,2048]{1,0:T(8,128)S(1)}, bf16[128,2048]{1,0:T(8,128)(2,1)S(1)}) custom-call(f32[1,2048]{1,0:T(1,128)S(1)} %bitcast.31, bf16[704,2048]{1,0:T(8,128)(2,1)} %bitcast.37, bf16[704,2048]{1,0:T(8,128)(2,1)} %bitcast.38, bf16[704,2048]{1,0:T(8,128)(2,1)} %bitcast.39, bf16[128,2048]{1,0:T(8,128)(2,1)S(1)} %weave.3.refs_0_.refs_1_, ...), custom_call_target="tpu_custom_call" | custom-call | flops 4429185024 | bytes 10747904 | tf_op jit(solution)/shard_map/shared/pallas_call | solution.py:353
  84.9 6.9 %expert.7 = (bf16[128,2048]{1,0:T(8,128)(2,1)S(1)}, bf16[128,2048]{1,0:T(8,128)(2,1)S(1)}, bf16[256,2048]{1,0:T(8,128)(2,1)S(1)}) custom-call(f32[1,2048]{1,0:T(1,128)S(1)} %bitcast.32, bf16[5,144,256]{2,1,0:T(8,128)(2,1)S(1)} %get-tuple-element.141.pick_ref, bf16[5,256,144]{2,1,0:T(8,128)(2,1)S(1)} %get-tuple-element.142.put_ref, ...), custom_call_target="tpu_custom_call" | custom-call | flops 1660944384 | bytes 8388608 | tf_op jit(solution)/shard_map/expert/pallas_call | solution.py:292
  92.4 1.2 collective-permute-done.32.refs_2_
  94.1 1.4 collective-permute-done.37.refs_1_
  95.5 0.7 collective-permute-done.38.refs_3_
  96.5 1.5 collective-permute-start.40
  98.5 6.9 %expert.8 = (bf16[128,2048]{1,0:T(8,128)(2,1)S(1)}, bf16[128,2048]{1,0:T(8,128)(2,1)S(1)}, bf16[256,2048]{1,0:T(8,128)(2,1)S(1)}) custom-call(f32[1,2048]{1,0:T(1,128)S(1)} %bitcast.33, bf16[3,144,256]{2,1,0:T(8,128)(2,1)S(1)} %get-tuple-element.175.pick_ref, bf16[3,256,144]{2,1,0:T(8,128)(2,1)S(1)} %get-tuple-element.176.put_ref, ...), custom_call_target="tpu_custom_call" | custom-call | flops 1660944384 | bytes 8388608 | tf_op jit(solution)/shard_map/expert/pallas_call | solution.py:292
  105.4 0.8 collective-permute-done.41.refs_1_
  106.8 1.0 collective-permute-done.42.refs_2_
  108.2 3.8 %expert.9 = (bf16[128,2048]{1,0:T(8,128)(2,1)S(1)}, bf16[128,2048]{1,0:T(8,128)(2,1)S(1)}) custom-call(f32[1,2048]{1,0:T(1,128)S(1)} %bitcast.34, bf16[3,144,256]{2,1,0:T(8,128)(2,1)S(1)} %get-tuple-element.175.pick_ref, bf16[3,256,144]{2,1,0:T(8,128)(2,1)S(1)} %get-tuple-element.176.put_ref, f32[3,144,1]{2,1,0:T(8,128)S(1)} %get-tuple-element.177.factor_ref, ...), custom_call_target="tpu_custom_call" | custom-call | flops 830472192 | bytes 4194304 | tf_op jit(solution)/shard_map/expert/pallas_call | solution.py:292
  112.2 0.6 collective-permute-start.48
  112.9 1.1 collective-permute-done.45.refs_1_
  114.7 1.5 collective-permute-start.46
  117.0 1.5 collective-permute-start.53
  118.5 4.7 %collective-permute-done.47.refs_2_ = bf16[64,2048]{1,0:T(8,128)(2,1)S(1)} collective-permute-done((bf16[64,2048]{1,0:T(8,128)(2,1)S(1)}, bf16[64,2048]{1,0:T(8,128)(2,1)S(1)}, u32[]{:S(2)}, u32[]{:S(2)}) %collective-permute-start.47) | collective-permute-done | bytes 262176 | tf_op jit(solution)/shard_map/ppermute | solution.py:465
  124.1 1.5 collective-permute-start.51
  125.6 0.8 collective-permute-done.48.refs_4_
  126.4 2.5 %collective-permute-done.49.refs_2_ = bf16[64,2048]{1,0:T(8,128)(2,1)S(1)} collective-permute-done((bf16[64,2048]{1,0:T(8,128)(2,1)S(1)}, bf16[64,2048]{1,0:T(8,128)(2,1)S(1)}, u32[]{:S(2)}, u32[]{:S(2)}) %collective-permute-start.49) | collective-permute-done | bytes 262176 | tf_op jit(solution)/shard_map/ppermute | solution.py:465
  129.7 1.5 collective-permute-start.55
  131.2 3.3 %collective-permute-done.52.refs_2_ = bf16[64,2048]{1,0:T(8,128)(2,1)S(1)} collective-permute-done((bf16[64,2048]{1,0:T(8,128)(2,1)S(1)}, bf16[64,2048]{1,0:T(8,128)(2,1)S(1)}, u32[]{:S(2)}, u32[]{:S(2)}) %collective-permute-start.52) | collective-permute-done | bytes 262176 | tf_op jit(solution)/shard_map/ppermute | solution.py:465
  135.3 1.5 collective-permute-start.57
  136.8 3.3 %collective-permute-done.50.refs_2_ = bf16[64,2048]{1,0:T(8,128)(2,1)S(1)} collective-permute-done((bf16[64,2048]{1,0:T(8,128)(2,1)S(1)}, bf16[64,2048]{1,0:T(8,128)(2,1)S(1)}, u32[]{:S(2)}, u32[]{:S(2)}) %collective-permute-start.50) | collective-permute-done | bytes 262176 | tf_op jit(solution)/shard_map/ppermute | solution.py:465
  140.9 1.5 collective-permute-start.56
  142.4 3.3 %collective-permute-done.58.refs_2_ = bf16[64,2048]{1,0:T(8,128)(2,1)S(1)} collective-permute-done((bf16[64,2048]{1,0:T(8,128)(2,1)S(1)}, bf16[64,2048]{1,0:T(8,128)(2,1)S(1)}, u32[]{:S(2)}, u32[]{:S(2)}) %collective-permute-start.58) | collective-permute-done | bytes 262176 | tf_op jit(solution)/shard_map/ppermute | solution.py:465
  145.8 0.6 collective-permute-done.57.refs_2_
  146.6 1.5 collective-permute-start.59
  148.9 3.2 %collective-permute-done.56.bottom_ref = bf16[64,2048]{1,0:T(8,128)(2,1)S(1)} collective-permute-done((bf16[64,2048]{1,0:T(8,128)(2,1)S(1)}, bf16[64,2048]{1,0:T(8,128)(2,1)S(1)}, u32[]{:S(2)}, u32[]{:S(2)}) %collective-permute-start.56) | collective-permute-done | bytes 262176 | tf_op jit(solution)/shard_map/ppermute | solution.py:462
  152.2 4.4 %collective-permute-done.59.top_ref = bf16[64,2048]{1,0:T(8,128)(2,1)S(1)} collective-permute-done((bf16[64,2048]{1,0:T(8,128)(2,1)S(1)}, bf16[64,2048]{1,0:T(8,128)(2,1)S(1)}, u32[]{:S(2)}, u32[]{:S(2)}) %collective-permute-start.59) | collective-permute-done | bytes 262176 | tf_op jit(solution)/shard_map/ppermute | solution.py:462
  156.6 0.9 final.1
  (107 shorter events, 20.6 us)
Async XLA Ops:
  0.1 52.7 %copy-start.1 = (bf16[1,1408,2048]{2,1,0:T(8,128)(2,1)S(1)}, bf16[1,1408,2048]{2,1,0:T(8,128)(2,1)}, u32[]{:S(2)}) copy-start(bf16[1,1408,2048]{2,1,0:T(8,128)(2,1)} %param.21) | copy-start | bytes 17301508
  2.5 26.8 %collective-permute-start.13 = (bf16[128,3072]{1,0:T(8,128)(2,1)S(1)}, bf16[128,3072]{1,0:T(8,128)(2,1)S(1)}, u32[]{:S(2)}, u32[]{:S(2)}) collective-permute-start(bf16[128,3072]{1,0:T(8,128)(2,1)S(1)} %get-tuple-element.106), channel_id=1, source_target_pairs={{0,16},{1,17},{2,18},{3,19},{4,20},{5,21},{6,22},{7,23},{8,24},{9,... | collective-permute-start | bytes 2359304 | tf_op jit(solution)/shard_map/ppermute | solution.py:476
  5.5 2.0 %collective-permute-start.3 = (bf16[144,512]{1,0:T(8,128)(2,1)S(1)}, bf16[144,512]{1,0:T(8,128)(2,1)S(1)}, u32[]{:S(2)}, u32[]{:S(2)}) collective-permute-start(bf16[144,512]{1,0:T(8,128)(2,1)S(1)} %get-tuple-element.105), channel_id=1, source_target_pairs={{0,1},{1,0},{2,3},{3,2},{4,5},{5,4},{6,7},{7,6},{8,9},{9,8},{10,11... | collective-permute-start | bytes 442376 | tf_op jit(solution)/shard_map/ppermute | solution.py:468
  5.5 6.6 %collective-permute-start = (bf16[144,512]{1,0:T(8,128)(2,1)S(1)}, bf16[144,512]{1,0:T(8,128)(2,1)S(1)}, u32[]{:S(2)}, u32[]{:S(2)}) collective-permute-start(bf16[144,512]{1,0:T(8,128)(2,1)S(1)} %get-tuple-element.120.refs_4_.refs_0_), channel_id=1, source_target_pairs={{0,4},{1,5},{4,8},{5,9},{8,12},{9,13},{12,14},{13,15},{14,10},{15,... | collective-permute-start | bytes 442376 | tf_op jit(solution)/shard_map/ppermute | solution.py:462
  7.0 6.7 %collective-permute-start.7 = (bf16[144,512]{1,0:T(8,128)(2,1)S(1)}, bf16[144,512]{1,0:T(8,128)(2,1)S(1)}, u32[]{:S(2)}, u32[]{:S(2)}) collective-permute-start(bf16[144,512]{1,0:T(8,128)(2,1)S(1)} %get-tuple-element.120.refs_4_.refs_0_), channel_id=1, source_target_pairs={{4,0},{5,1},{8,4},{9,5},{12,8},{13,9},{14,12},{15,13},{10,14},{11,... | collective-permute-start | bytes 442376 | tf_op jit(solution)/shard_map/ppermute | solution.py:465
  7.5 9.4 %collective-permute-start.10 = (bf16[144,512]{1,0:T(8,128)(2,1)S(1)}, bf16[144,512]{1,0:T(8,128)(2,1)S(1)}, u32[]{:S(2)}, u32[]{:S(2)}) collective-permute-start(bf16[144,512]{1,0:T(8,128)(2,1)S(1)} %collective-permute-done.3.refs_5_.refs_1_), channel_id=1, source_target_pairs={{4,0},{5,1},{8,4},{9,5},{12,8},{13,9},{14,12},{15,13},{10,14},{11,... | collective-permute-start | bytes 442376 | tf_op jit(solution)/shard_map/ppermute | solution.py:465
  9.0 8.3 %collective-permute-start.4 = (bf16[144,512]{1,0:T(8,128)(2,1)S(1)}, bf16[144,512]{1,0:T(8,128)(2,1)S(1)}, u32[]{:S(2)}, u32[]{:S(2)}) collective-permute-start(bf16[144,512]{1,0:T(8,128)(2,1)S(1)} %collective-permute-done.3.refs_5_.refs_1_), channel_id=1, source_target_pairs={{0,4},{1,5},{4,8},{5,9},{8,12},{9,13},{12,14},{13,15},{14,10},{15,... | collective-permute-start | bytes 442376 | tf_op jit(solution)/shard_map/ppermute | solution.py:462
  12.1 6.8 %collective-permute-start.1 = (bf16[144,512]{1,0:T(8,128)(2,1)S(1)}, bf16[144,512]{1,0:T(8,128)(2,1)S(1)}, u32[]{:S(2)}, u32[]{:S(2)}) collective-permute-start(bf16[144,512]{1,0:T(8,128)(2,1)S(1)} %collective-permute-done.refs_6_.refs_2_), channel_id=1, source_target_pairs={{0,4},{1,5},{4,8},{5,9},{8,12},{9,13},{12,14},{13,15},{14,10},{15,... | collective-permute-start | bytes 442376 | tf_op jit(solution)/shard_map/ppermute | solution.py:462
  13.7 6.8 %collective-permute-start.8 = (bf16[144,512]{1,0:T(8,128)(2,1)S(1)}, bf16[144,512]{1,0:T(8,128)(2,1)S(1)}, u32[]{:S(2)}, u32[]{:S(2)}) collective-permute-start(bf16[144,512]{1,0:T(8,128)(2,1)S(1)} %collective-permute-done.7.refs_8_.refs_4_), channel_id=1, source_target_pairs={{4,0},{5,1},{8,4},{9,5},{12,8},{13,9},{14,12},{15,13},{10,14},{11,... | collective-permute-start | bytes 442376 | tf_op jit(solution)/shard_map/ppermute | solution.py:465
  16.9 6.8 %collective-permute-start.11 = (bf16[144,512]{1,0:T(8,128)(2,1)S(1)}, bf16[144,512]{1,0:T(8,128)(2,1)S(1)}, u32[]{:S(2)}, u32[]{:S(2)}) collective-permute-start(bf16[144,512]{1,0:T(8,128)(2,1)S(1)} %collective-permute-done.10.refs_9_.refs_5_), channel_id=1, source_target_pairs={{4,0},{5,1},{8,4},{9,5},{12,8},{13,9},{14,12},{15,13},{10,14},{11,... | collective-permute-start | bytes 442376 | tf_op jit(solution)/shard_map/ppermute | solution.py:465
  17.3 6.8 %collective-permute-start.5 = (bf16[144,512]{1,0:T(8,128)(2,1)S(1)}, bf16[144,512]{1,0:T(8,128)(2,1)S(1)}, u32[]{:S(2)}, u32[]{:S(2)}) collective-permute-start(bf16[144,512]{1,0:T(8,128)(2,1)S(1)} %collective-permute-done.4.refs_7_.refs_3_), channel_id=1, source_target_pairs={{0,4},{1,5},{4,8},{5,9},{8,12},{9,13},{12,14},{13,15},{14,10},{15,... | collective-permute-start | bytes 442376 | tf_op jit(solution)/shard_map/ppermute | solution.py:462
  18.9 6.8 %collective-permute-start.2 = (bf16[144,512]{1,0:T(8,128)(2,1)S(1)}, bf16[144,512]{1,0:T(8,128)(2,1)S(1)}, u32[]{:S(2)}, u32[]{:S(2)}) collective-permute-start(bf16[144,512]{1,0:T(8,128)(2,1)S(1)} %collective-permute-done.1.refs_10_.refs_6_), channel_id=1, source_target_pairs={{0,4},{1,5},{4,8},{5,9},{8,12},{9,13},{12,14},{13,15},{14,10},{15,... | collective-permute-start | bytes 442376 | tf_op jit(solution)/shard_map/ppermute | solution.py:462
  20.5 6.7 %collective-permute-start.9 = (bf16[144,512]{1,0:T(8,128)(2,1)S(1)}, bf16[144,512]{1,0:T(8,128)(2,1)S(1)}, u32[]{:S(2)}, u32[]{:S(2)}) collective-permute-start(bf16[144,512]{1,0:T(8,128)(2,1)S(1)} %collective-permute-done.8.refs_12_.refs_8_), channel_id=1, source_target_pairs={{4,0},{5,1},{8,4},{9,5},{12,8},{13,9},{14,12},{15,13},{10,14},{11,... | collective-permute-start | bytes 442376 | tf_op jit(solution)/shard_map/ppermute | solution.py:465
  23.7 5.1 %collective-permute-start.12 = (bf16[144,512]{1,0:T(8,128)(2,1)S(1)}, bf16[144,512]{1,0:T(8,128)(2,1)S(1)}, u32[]{:S(2)}, u32[]{:S(2)}) collective-permute-start(bf16[144,512]{1,0:T(8,128)(2,1)S(1)} %collective-permute-done.11.refs_13_.refs_9_), channel_id=1, source_target_pairs={{4,0},{5,1},{8,4},{9,5},{12,8},{13,9},{14,12},{15,13},{10,14},{11,... | collective-permute-start | bytes 442376 | tf_op jit(solution)/shard_map/ppermute | solution.py:465
  24.1 5.1 %collective-permute-start.6 = (bf16[144,512]{1,0:T(8,128)(2,1)S(1)}, bf16[144,512]{1,0:T(8,128)(2,1)S(1)}, u32[]{:S(2)}, u32[]{:S(2)}) collective-permute-start(bf16[144,512]{1,0:T(8,128)(2,1)S(1)} %collective-permute-done.5.refs_11_.refs_7_), channel_id=1, source_target_pairs={{0,4},{1,5},{4,8},{5,9},{8,12},{9,13},{12,14},{13,15},{14,10},{15,... | collective-permute-start | bytes 442376 | tf_op jit(solution)/shard_map/ppermute | solution.py:462
  25.7 5.6 %collective-permute-start.14 = (bf16[128,3072]{1,0:T(8,128)(2,1)S(1)}, bf16[128,3072]{1,0:T(8,128)(2,1)S(1)}, u32[]{:S(2)}, u32[]{:S(2)}) collective-permute-start(bf16[128,3072]{1,0:T(8,128)(2,1)S(1)} %get-tuple-element.103.refs_0_), channel_id=1, source_target_pairs={{0,1},{1,0},{2,3},{3,2},{4,5},{5,4},{6,7},{7,6},{8,9},{9,8},{10,11... | collective-permute-start | bytes 2359304 | tf_op jit(solution)/shard_map/ppermute | solution.py:468
  29.3 2.3 %collective-permute-start.15 = (bf16[128,3072]{1,0:T(8,128)(2,1)S(1)}, bf16[128,3072]{1,0:T(8,128)(2,1)S(1)}, u32[]{:S(2)}, u32[]{:S(2)}) collective-permute-start(bf16[128,3072]{1,0:T(8,128)(2,1)S(1)} %collective-permute-done.13.refs_1_), channel_id=1, source_target_pairs={{0,1},{1,0},{2,3},{3,2},{4,5},{5,4},{6,7},{7,6},{8,9},{9,8},{10,11... | collective-permute-start | bytes 2359304 | tf_op jit(solution)/shard_map/ppermute | solution.py:468
  29.3 6.3 %collective-permute-start.16 = (bf16[144,512]{1,0:T(8,128)(2,1)S(1)}, bf16[144,512]{1,0:T(8,128)(2,1)S(1)}, u32[]{:S(2)}, u32[]{:S(2)}) collective-permute-start(bf16[144,512]{1,0:T(8,128)(2,1)S(1)} %collective-permute-done.2.refs_14_.refs_2_), channel_id=1, source_target_pairs={{0,4},{1,5},{4,8},{5,9},{8,12},{9,13},{12,14},{13,15},{14,10},{15,... | collective-permute-start | bytes 442376 | tf_op jit(solution)/shard_map/ppermute | solution.py:462
  30.9 6.0 %collective-permute-start.17 = (bf16[144,512]{1,0:T(8,128)(2,1)S(1)}, bf16[144,512]{1,0:T(8,128)(2,1)S(1)}, u32[]{:S(2)}, u32[]{:S(2)}) collective-permute-start(bf16[144,512]{1,0:T(8,128)(2,1)S(1)} %collective-permute-done.12.refs_17_.refs_5_), channel_id=1, source_target_pairs={{4,0},{5,1},{8,4},{9,5},{12,8},{13,9},{14,12},{15,13},{10,14},{11,... | collective-permute-start | bytes 442376 | tf_op jit(solution)/shard_map/ppermute | solution.py:465
  32.2 20.6 %slice-start = ((s8[5767168]{0:T(1024)(128)(4,1)}), s8[4194304]{0:T(1024)(128)(4,1)S(1)}, s32[]{:S(2)}) async-start(s8[5767168]{0:T(1024)(128)(4,1)} %bitcast.12), calls=%async_computation | async-start | bytes 8388608
  33.9 18.9 %slice-start.1 = ((s8[5767168]{0:T(1024)(128)(4,1)}), s8[1572864]{0:T(1024)(128)(4,1)S(1)}, s32[]{:S(2)}) async-start(s8[5767168]{0:T(1024)(128)(4,1)} %bitcast.12), calls=%async_computation.1 | async-start | bytes 3145728
  37.7 1.4 collective-permute-start.18
  39.7 9.0 %collective-permute-start.19 = (bf16[128,1024]{1,0:T(8,128)(2,1)S(1)}, bf16[128,1024]{1,0:T(8,128)(2,1)S(1)}, u32[]{:S(2)}, u32[]{:S(2)}) collective-permute-start(bf16[128,1024]{1,0:T(8,128)(2,1)S(1)} %beside.2.refs_0_), channel_id=1, source_target_pairs={{0,4},{1,5},{4,8},{5,9},{8,12},{9,13},{12,14},{13,15},{14,10},{15,... | collective-permute-start | bytes 786440 | tf_op jit(solution)/shard_map/ppermute | solution.py:462
  41.3 8.1 %collective-permute-start.20 = (bf16[128,1024]{1,0:T(8,128)(2,1)S(1)}, bf16[128,1024]{1,0:T(8,128)(2,1)S(1)}, u32[]{:S(2)}, u32[]{:S(2)}) collective-permute-start(bf16[128,1024]{1,0:T(8,128)(2,1)S(1)} %beside.2.refs_0_), channel_id=1, source_target_pairs={{4,0},{5,1},{8,4},{9,5},{12,8},{13,9},{14,12},{15,13},{10,14},{11,... | collective-permute-start | bytes 786440 | tf_op jit(solution)/shard_map/ppermute | solution.py:465
  41.8 6.4 %collective-permute-start.21 = (bf16[128,512]{1,0:T(8,128)(2,1)S(1)}, bf16[128,512]{1,0:T(8,128)(2,1)S(1)}, u32[]{:S(2)}, u32[]{:S(2)}) collective-permute-start(bf16[128,512]{1,0:T(8,128)(2,1)S(1)} %get-tuple-element.118), channel_id=1, source_target_pairs={{0,16},{1,17},{2,18},{3,19},{4,20},{5,21},{6,22},{7,23},{8,24},{9,... | collective-permute-start | bytes 393224 | tf_op jit(solution)/shard_map/ppermute | solution.py:476
  42.3 5.9 %collective-permute-start.22 = (bf16[128,512]{1,0:T(8,128)(2,1)S(1)}, bf16[128,512]{1,0:T(8,128)(2,1)S(1)}, u32[]{:S(2)}, u32[]{:S(2)}) collective-permute-start(bf16[128,512]{1,0:T(8,128)(2,1)S(1)} %get-tuple-element.119), channel_id=1, source_target_pairs={{0,17},{1,16},{2,19},{3,18},{4,21},{5,20},{6,23},{7,22},{8,25},{9,... | collective-permute-start | bytes 393224 | tf_op jit(solution)/shard_map/ppermute | solution.py:476
  50.0 2.8 %collective-permute-start.25 = (bf16[128,2048]{1,0:T(8,128)(2,1)S(1)}, bf16[128,2048]{1,0:T(8,128)(2,1)S(1)}, u32[]{:S(2)}, u32[]{:S(2)}) collective-permute-start(bf16[128,2048]{1,0:T(8,128)(2,1)S(1)} %weave.3.refs_0_.refs_1_), channel_id=1, source_target_pairs={{0,1},{1,0},{2,3},{3,2},{4,5},{5,4},{6,7},{7,6},{8,9},{9,8},{10,11... | collective-permute-start | bytes 1572872 | tf_op jit(solution)/shard_map/ppermute | solution.py:468
  50.8 8.3 %collective-permute-start.23 = (bf16[128,1024]{1,0:T(8,128)(2,1)S(1)}, bf16[128,1024]{1,0:T(8,128)(2,1)S(1)}, u32[]{:S(2)}, u32[]{:S(2)}) collective-permute-start(bf16[128,1024]{1,0:T(8,128)(2,1)S(1)} %beside.3.refs_1_), channel_id=1, source_target_pairs={{0,4},{1,5},{4,8},{5,9},{8,12},{9,13},{12,14},{13,15},{14,10},{15,... | collective-permute-start | bytes 786440 | tf_op jit(solution)/shard_map/ppermute | solution.py:462
  52.3 8.0 %collective-permute-start.24 = (bf16[128,1024]{1,0:T(8,128)(2,1)S(1)}, bf16[128,1024]{1,0:T(8,128)(2,1)S(1)}, u32[]{:S(2)}, u32[]{:S(2)}) collective-permute-start(bf16[128,1024]{1,0:T(8,128)(2,1)S(1)} %beside.3.refs_1_), channel_id=1, source_target_pairs={{4,0},{5,1},{8,4},{9,5},{12,8},{13,9},{14,12},{15,13},{10,14},{11,... | collective-permute-start | bytes 786440 | tf_op jit(solution)/shard_map/ppermute | solution.py:465
  60.9 3.8 %collective-permute-start.29 = (bf16[128,2048]{1,0:T(8,128)(2,1)S(1)}, bf16[128,2048]{1,0:T(8,128)(2,1)S(1)}, u32[]{:S(2)}, u32[]{:S(2)}) collective-permute-start(bf16[128,2048]{1,0:T(8,128)(2,1)S(1)} %weave.5.refs_2_), channel_id=1, source_target_pairs={{0,1},{1,0},{2,3},{3,2},{4,5},{5,4},{6,7},{7,6},{8,9},{9,8},{10,11... | collective-permute-start | bytes 1572872 | tf_op jit(solution)/shard_map/ppermute | solution.py:468
  61.6 3.1 %collective-permute-start.28 = (bf16[128,2048]{1,0:T(8,128)(2,1)S(1)}, bf16[128,2048]{1,0:T(8,128)(2,1)S(1)}, u32[]{:S(2)}, u32[]{:S(2)}) collective-permute-start(bf16[128,2048]{1,0:T(8,128)(2,1)S(1)} %weave.4.refs_0_), channel_id=1, source_target_pairs={{0,1},{1,0},{2,3},{3,2},{4,5},{5,4},{6,7},{7,6},{8,9},{9,8},{10,11... | collective-permute-start | bytes 1572872 | tf_op jit(solution)/shard_map/ppermute | solution.py:468
  62.1 13.9 %collective-permute-start.27 = (bf16[128,2048]{1,0:T(8,128)(2,1)S(1)}, bf16[128,2048]{1,0:T(8,128)(2,1)S(1)}, u32[]{:S(2)}, u32[]{:S(2)}) collective-permute-start(bf16[128,2048]{1,0:T(8,128)(2,1)S(1)} %weave.5.refs_2_), channel_id=1, source_target_pairs={{4,0},{5,1},{8,4},{9,5},{12,8},{13,9},{14,12},{15,13},{10,14},{11,... | collective-permute-start | bytes 1572872 | tf_op jit(solution)/shard_map/ppermute | solution.py:465
  62.6 13.7 %collective-permute-start.26 = (bf16[128,2048]{1,0:T(8,128)(2,1)S(1)}, bf16[128,2048]{1,0:T(8,128)(2,1)S(1)}, u32[]{:S(2)}, u32[]{:S(2)}) collective-permute-start(bf16[128,2048]{1,0:T(8,128)(2,1)S(1)} %weave.4.refs_0_), channel_id=1, source_target_pairs={{0,4},{1,5},{4,8},{5,9},{8,12},{9,13},{12,14},{13,15},{14,10},{15,... | collective-permute-start | bytes 1572872 | tf_op jit(solution)/shard_map/ppermute | solution.py:462
  64.2 13.4 %collective-permute-start.30 = (bf16[128,2048]{1,0:T(8,128)(2,1)S(1)}, bf16[128,2048]{1,0:T(8,128)(2,1)S(1)}, u32[]{:S(2)}, u32[]{:S(2)}) collective-permute-start(bf16[128,2048]{1,0:T(8,128)(2,1)S(1)} %weave.3.refs_0_.refs_1_), channel_id=1, source_target_pairs={{0,16},{1,17},{2,18},{3,19},{4,20},{5,21},{6,22},{7,23},{8,24},{9,... | collective-permute-start | bytes 1572872 | tf_op jit(solution)/shard_map/ppermute | solution.py:476
  77.5 7.4 %collective-permute-start.33 = (bf16[128,2048]{1,0:T(8,128)(2,1)S(1)}, bf16[128,2048]{1,0:T(8,128)(2,1)S(1)}, u32[]{:S(2)}, u32[]{:S(2)}) collective-permute-start(bf16[128,2048]{1,0:T(8,128)(2,1)S(1)} %collective-permute-done.26.refs_0_), channel_id=1, source_target_pairs={{0,1},{1,0},{2,3},{3,2},{4,5},{5,4},{6,7},{7,6},{8,9},{9,8},{10,11... | collective-permute-start | bytes 1572872 | tf_op jit(solution)/shard_map/ppermute | solution.py:468
  77.5 7.4 %collective-permute-start.34 = (bf16[128,2048]{1,0:T(8,128)(2,1)S(1)}, bf16[128,2048]{1,0:T(8,128)(2,1)S(1)}, u32[]{:S(2)}, u32[]{:S(2)}) collective-permute-start(bf16[128,2048]{1,0:T(8,128)(2,1)S(1)} %collective-permute-done.27.refs_2_), channel_id=1, source_target_pairs={{0,1},{1,0},{2,3},{3,2},{4,5},{5,4},{6,7},{7,6},{8,9},{9,8},{10,11... | collective-permute-start | bytes 1572872 | tf_op jit(solution)/shard_map/ppermute | solution.py:468
  78.0 15.6 %collective-permute-start.35 = (bf16[128,2048]{1,0:T(8,128)(2,1)S(1)}, bf16[128,2048]{1,0:T(8,128)(2,1)S(1)}, u32[]{:S(2)}, u32[]{:S(2)}) collective-permute-start(bf16[128,2048]{1,0:T(8,128)(2,1)S(1)} %get-tuple-element.167), channel_id=1, source_target_pairs={{0,1},{1,0},{2,3},{3,2},{4,5},{5,4},{6,7},{7,6},{8,9},{9,8},{10,11... | collective-permute-start | bytes 1572872 | tf_op jit(solution)/shard_map/ppermute | solution.py:468
  78.0 14.3 %collective-permute-start.31 = (bf16[128,2048]{1,0:T(8,128)(2,1)S(1)}, bf16[128,2048]{1,0:T(8,128)(2,1)S(1)}, u32[]{:S(2)}, u32[]{:S(2)}) collective-permute-start(bf16[128,2048]{1,0:T(8,128)(2,1)S(1)} %collective-permute-done.26.refs_0_), channel_id=1, source_target_pairs={{0,4},{1,5},{4,8},{5,9},{8,12},{9,13},{12,14},{13,15},{14,10},{15,... | collective-permute-start | bytes 1572872 | tf_op jit(solution)/shard_map/ppermute | solution.py:462
  79.5 14.1 %collective-permute-start.32 = (bf16[128,2048]{1,0:T(8,128)(2,1)S(1)}, bf16[128,2048]{1,0:T(8,128)(2,1)S(1)}, u32[]{:S(2)}, u32[]{:S(2)}) collective-permute-start(bf16[128,2048]{1,0:T(8,128)(2,1)S(1)} %collective-permute-done.27.refs_2_), channel_id=1, source_target_pairs={{4,0},{5,1},{8,4},{9,5},{12,8},{13,9},{14,12},{15,13},{10,14},{11,... | collective-permute-start | bytes 1572872 | tf_op jit(solution)/shard_map/ppermute | solution.py:465
  93.6 1.9 %collective-permute-start.37 = (bf16[128,2048]{1,0:T(8,128)(2,1)S(1)}, bf16[128,2048]{1,0:T(8,128)(2,1)S(1)}, u32[]{:S(2)}, u32[]{:S(2)}) collective-permute-start(bf16[128,2048]{1,0:T(8,128)(2,1)S(1)} %collective-permute-done.31.refs_0_), channel_id=1, source_target_pairs={{0,1},{1,0},{2,3},{3,2},{4,5},{5,4},{6,7},{7,6},{8,9},{9,8},{10,11... | collective-permute-start | bytes 1572872 | tf_op jit(solution)/shard_map/ppermute | solution.py:468
  93.6 2.7 %collective-permute-start.38 = (bf16[128,2048]{1,0:T(8,128)(2,1)S(1)}, bf16[128,2048]{1,0:T(8,128)(2,1)S(1)}, u32[]{:S(2)}, u32[]{:S(2)}) collective-permute-start(bf16[128,2048]{1,0:T(8,128)(2,1)S(1)} %collective-permute-done.32.refs_2_), channel_id=1, source_target_pairs={{0,1},{1,0},{2,3},{3,2},{4,5},{5,4},{6,7},{7,6},{8,9},{9,8},{10,11... | collective-permute-start | bytes 1572872 | tf_op jit(solution)/shard_map/ppermute | solution.py:468
  94.1 17.9 %collective-permute-start.36 = (bf16[256,2048]{1,0:T(8,128)(2,1)S(1)}, bf16[256,2048]{1,0:T(8,128)(2,1)S(1)}, u32[]{:S(2)}, u32[]{:S(2)}) collective-permute-start(bf16[256,2048]{1,0:T(8,128)(2,1)S(1)} %get-tuple-element.164.refs_2_), channel_id=1, source_target_pairs={{0,1},{1,0},{2,3},{3,2},{4,5},{5,4},{6,7},{7,6},{8,9},{9,8},{10,11... | collective-permute-start | bytes 3145736 | tf_op jit(solution)/shard_map/ppermute | solution.py:468
  96.3 15.7 %collective-permute-start.39 = (bf16[256,2048]{1,0:T(8,128)(2,1)S(1)}, bf16[256,2048]{1,0:T(8,128)(2,1)S(1)}, u32[]{:S(2)}, u32[]{:S(2)}) collective-permute-start(bf16[256,2048]{1,0:T(8,128)(2,1)S(1)} %get-tuple-element.174), channel_id=1, source_target_pairs={{0,1},{1,0},{2,3},{3,2},{4,5},{5,4},{6,7},{7,6},{8,9},{9,8},{10,11... | collective-permute-start | bytes 3145736 | tf_op jit(solution)/shard_map/ppermute | solution.py:468
  96.5 9.0 %collective-permute-start.40 = (bf16[64,2048]{1,0:T(8,128)(2,1)S(1)}, bf16[64,2048]{1,0:T(8,128)(2,1)S(1)}, u32[]{:S(2)}, u32[]{:S(2)}) collective-permute-start(bf16[64,2048]{1,0:T(8,128)(2,1)S(1)} %slice.6), channel_id=1, source_target_pairs={{0,4},{1,5},{4,8},{5,9},{8,12},{9,13},{12,14},{13,15},{14,10},{15,... | collective-permute-start | bytes 786440 | tf_op jit(solution)/shard_map/ppermute | solution.py:462
  98.0 8.3 %collective-permute-start.41 = (bf16[64,2048]{1,0:T(8,128)(2,1)S(1)}, bf16[64,2048]{1,0:T(8,128)(2,1)S(1)}, u32[]{:S(2)}, u32[]{:S(2)}) collective-permute-start(bf16[64,2048]{1,0:T(8,128)(2,1)S(1)} %slice.7), channel_id=1, source_target_pairs={{4,0},{5,1},{8,4},{9,5},{12,8},{13,9},{14,12},{15,13},{10,14},{11,... | collective-permute-start | bytes 786440 | tf_op jit(solution)/shard_map/ppermute | solution.py:465
  106.3 1.5 collective-permute-start.42
  106.3 1.9 %collective-permute-start.43 = (bf16[64,2048]{1,0:T(8,128)(2,1)S(1)}, bf16[64,2048]{1,0:T(8,128)(2,1)S(1)}, u32[]{:S(2)}, u32[]{:S(2)}) collective-permute-start(bf16[64,2048]{1,0:T(8,128)(2,1)S(1)} %collective-permute-done.41.refs_1_), channel_id=1, source_target_pairs={{0,1},{1,0},{2,3},{3,2},{4,5},{5,4},{6,7},{7,6},{8,9},{9,8},{10,11... | collective-permute-start | bytes 786440 | tf_op jit(solution)/shard_map/ppermute | solution.py:468
  106.8 9.5 %collective-permute-start.44 = (bf16[256,2048]{1,0:T(8,128)(2,1)S(1)}, bf16[256,2048]{1,0:T(8,128)(2,1)S(1)}, u32[]{:S(2)}, u32[]{:S(2)}) collective-permute-start(bf16[256,2048]{1,0:T(8,128)(2,1)S(1)} %get-tuple-element.189), channel_id=1, source_target_pairs={{0,1},{1,0},{2,3},{3,2},{4,5},{5,4},{6,7},{7,6},{8,9},{9,8},{10,11... | collective-permute-start | bytes 3145736 | tf_op jit(solution)/shard_map/ppermute | solution.py:468
  112.0 2.0 %collective-permute-start.45 = (bf16[128,2048]{1,0:T(8,128)(2,1)S(1)}, bf16[128,2048]{1,0:T(8,128)(2,1)S(1)}, u32[]{:S(2)}, u32[]{:S(2)}) collective-permute-start(bf16[128,2048]{1,0:T(8,128)(2,1)S(1)} %get-tuple-element.191), channel_id=1, source_target_pairs={{0,1},{1,0},{2,3},{3,2},{4,5},{5,4},{6,7},{7,6},{8,9},{9,8},{10,11... | collective-permute-start | bytes 1572872 | tf_op jit(solution)/shard_map/ppermute | solution.py:468
  112.2 14.2 %collective-permute-start.48 = (bf16[128,2048]{1,0:T(8,128)(2,1)S(1)}, bf16[128,2048]{1,0:T(8,128)(2,1)S(1)}, u32[]{:S(2)}, u32[]{:S(2)}) collective-permute-start(bf16[128,2048]{1,0:T(8,128)(2,1)S(1)} %get-tuple-element.166), channel_id=1, source_target_pairs={{0,16},{1,17},{2,18},{3,19},{4,20},{5,21},{6,22},{7,23},{8,24},{9,... | collective-permute-start | bytes 1572872 | tf_op jit(solution)/shard_map/ppermute | solution.py:476
  114.1 9.2 %collective-permute-start.47 = (bf16[64,2048]{1,0:T(8,128)(2,1)S(1)}, bf16[64,2048]{1,0:T(8,128)(2,1)S(1)}, u32[]{:S(2)}, u32[]{:S(2)}) collective-permute-start(bf16[64,2048]{1,0:T(8,128)(2,1)S(1)} %add.23.refs_2_), channel_id=1, source_target_pairs={{4,0},{5,1},{8,4},{9,5},{12,8},{13,9},{14,12},{15,13},{10,14},{11,... | collective-permute-start | bytes 786440 | tf_op jit(solution)/shard_map/ppermute | solution.py:465
  114.7 9.2 %collective-permute-start.46 = (bf16[64,2048]{1,0:T(8,128)(2,1)S(1)}, bf16[64,2048]{1,0:T(8,128)(2,1)S(1)}, u32[]{:S(2)}, u32[]{:S(2)}) collective-permute-start(bf16[64,2048]{1,0:T(8,128)(2,1)S(1)} %add.24.refs_2_), channel_id=1, source_target_pairs={{0,4},{1,5},{4,8},{5,9},{8,12},{9,13},{12,14},{13,15},{14,10},{15,... | collective-permute-start | bytes 786440 | tf_op jit(solution)/shard_map/ppermute | solution.py:462
  116.3 12.6 %collective-permute-start.49 = (bf16[64,2048]{1,0:T(8,128)(2,1)S(1)}, bf16[64,2048]{1,0:T(8,128)(2,1)S(1)}, u32[]{:S(2)}, u32[]{:S(2)}) collective-permute-start(bf16[64,2048]{1,0:T(8,128)(2,1)S(1)} %add.25.refs_2_), channel_id=1, source_target_pairs={{4,0},{5,1},{8,4},{9,5},{12,8},{13,9},{14,12},{15,13},{10,14},{11,... | collective-permute-start | bytes 786440 | tf_op jit(solution)/shard_map/ppermute | solution.py:465
  117.0 12.6 %collective-permute-start.53 = (bf16[64,2048]{1,0:T(8,128)(2,1)S(1)}, bf16[64,2048]{1,0:T(8,128)(2,1)S(1)}, u32[]{:S(2)}, u32[]{:S(2)}) collective-permute-start(bf16[64,2048]{1,0:T(8,128)(2,1)S(1)} %add.26.refs_3_), channel_id=1, source_target_pairs={{0,4},{1,5},{4,8},{5,9},{8,12},{9,13},{12,14},{13,15},{14,10},{15,... | collective-permute-start | bytes 786440 | tf_op jit(solution)/shard_map/ppermute | solution.py:462
  123.4 11.1 %collective-permute-start.52 = (bf16[64,2048]{1,0:T(8,128)(2,1)S(1)}, bf16[64,2048]{1,0:T(8,128)(2,1)S(1)}, u32[]{:S(2)}, u32[]{:S(2)}) collective-permute-start(bf16[64,2048]{1,0:T(8,128)(2,1)S(1)} %add.27.refs_3_), channel_id=1, source_target_pairs={{4,0},{5,1},{8,4},{9,5},{12,8},{13,9},{14,12},{15,13},{10,14},{11,... | collective-permute-start | bytes 786440 | tf_op jit(solution)/shard_map/ppermute | solution.py:465
  124.1 11.1 %collective-permute-start.51 = (bf16[64,2048]{1,0:T(8,128)(2,1)S(1)}, bf16[64,2048]{1,0:T(8,128)(2,1)S(1)}, u32[]{:S(2)}, u32[]{:S(2)}) collective-permute-start(bf16[64,2048]{1,0:T(8,128)(2,1)S(1)} %add.28.refs_3_), channel_id=1, source_target_pairs={{0,4},{1,5},{4,8},{5,9},{8,12},{9,13},{12,14},{13,15},{14,10},{15,... | collective-permute-start | bytes 786440 | tf_op jit(solution)/shard_map/ppermute | solution.py:462
  129.0 11.1 %collective-permute-start.50 = (bf16[64,2048]{1,0:T(8,128)(2,1)S(1)}, bf16[64,2048]{1,0:T(8,128)(2,1)S(1)}, u32[]{:S(2)}, u32[]{:S(2)}) collective-permute-start(bf16[64,2048]{1,0:T(8,128)(2,1)S(1)} %add.29.refs_3_), channel_id=1, source_target_pairs={{4,0},{5,1},{8,4},{9,5},{12,8},{13,9},{14,12},{15,13},{10,14},{11,... | collective-permute-start | bytes 786440 | tf_op jit(solution)/shard_map/ppermute | solution.py:465
  129.7 11.1 %collective-permute-start.55 = (bf16[64,2048]{1,0:T(8,128)(2,1)S(1)}, bf16[64,2048]{1,0:T(8,128)(2,1)S(1)}, u32[]{:S(2)}, u32[]{:S(2)}) collective-permute-start(bf16[64,2048]{1,0:T(8,128)(2,1)S(1)} %add.30.refs_3_), channel_id=1, source_target_pairs={{0,4},{1,5},{4,8},{5,9},{8,12},{9,13},{12,14},{13,15},{14,10},{15,... | collective-permute-start | bytes 786440 | tf_op jit(solution)/shard_map/ppermute | solution.py:462
  134.6 11.1 %collective-permute-start.58 = (bf16[64,2048]{1,0:T(8,128)(2,1)S(1)}, bf16[64,2048]{1,0:T(8,128)(2,1)S(1)}, u32[]{:S(2)}, u32[]{:S(2)}) collective-permute-start(bf16[64,2048]{1,0:T(8,128)(2,1)S(1)} %add.31.refs_3_), channel_id=1, source_target_pairs={{4,0},{5,1},{8,4},{9,5},{12,8},{13,9},{14,12},{15,13},{10,14},{11,... | collective-permute-start | bytes 786440 | tf_op jit(solution)/shard_map/ppermute | solution.py:465
  135.3 11.1 %collective-permute-start.57 = (bf16[64,2048]{1,0:T(8,128)(2,1)S(1)}, bf16[64,2048]{1,0:T(8,128)(2,1)S(1)}, u32[]{:S(2)}, u32[]{:S(2)}) collective-permute-start(bf16[64,2048]{1,0:T(8,128)(2,1)S(1)} %add.32.refs_3_), channel_id=1, source_target_pairs={{0,4},{1,5},{4,8},{5,9},{8,12},{9,13},{12,14},{13,15},{14,10},{15,... | collective-permute-start | bytes 786440 | tf_op jit(solution)/shard_map/ppermute | solution.py:462
  140.2 11.9 %collective-permute-start.54 = (bf16[64,2048]{1,0:T(8,128)(2,1)S(1)}, bf16[64,2048]{1,0:T(8,128)(2,1)S(1)}, u32[]{:S(2)}, u32[]{:S(2)}) collective-permute-start(bf16[64,2048]{1,0:T(8,128)(2,1)S(1)} %add.33.refs_3_), channel_id=1, source_target_pairs={{4,0},{5,1},{8,4},{9,5},{12,8},{13,9},{14,12},{15,13},{10,14},{11,... | collective-permute-start | bytes 786440 | tf_op jit(solution)/shard_map/ppermute | solution.py:465
  140.9 11.1 %collective-permute-start.56 = (bf16[64,2048]{1,0:T(8,128)(2,1)S(1)}, bf16[64,2048]{1,0:T(8,128)(2,1)S(1)}, u32[]{:S(2)}, u32[]{:S(2)}) collective-permute-start(bf16[64,2048]{1,0:T(8,128)(2,1)S(1)} %add.34.refs_3_), channel_id=1, source_target_pairs={{0,4},{1,5},{4,8},{5,9},{8,12},{9,13},{12,14},{13,15},{14,10},{15,... | collective-permute-start | bytes 786440 | tf_op jit(solution)/shard_map/ppermute | solution.py:462
  146.6 10.0 %collective-permute-start.59 = (bf16[64,2048]{1,0:T(8,128)(2,1)S(1)}, bf16[64,2048]{1,0:T(8,128)(2,1)S(1)}, u32[]{:S(2)}, u32[]{:S(2)}) collective-permute-start(bf16[64,2048]{1,0:T(8,128)(2,1)S(1)} %add.36), channel_id=1, source_target_pairs={{0,4},{1,5},{4,8},{5,9},{8,12},{9,13},{12,14},{13,15},{14,10},{15,... | collective-permute-start | bytes 786440 | tf_op jit(solution)/shard_map/ppermute | solution.py:462
  148.1 8.5 %collective-permute-start.60 = (bf16[64,2048]{1,0:T(8,128)(2,1)S(1)}, bf16[64,2048]{1,0:T(8,128)(2,1)S(1)}, u32[]{:S(2)}, u32[]{:S(2)}) collective-permute-start(bf16[64,2048]{1,0:T(8,128)(2,1)S(1)} %add.35.refs_3_), channel_id=1, source_target_pairs={{4,0},{5,1},{8,4},{9,5},{12,8},{13,9},{14,12},{15,13},{10,14},{11,... | collective-permute-start | bytes 786440 | tf_op jit(solution)/shard_map/ppermute | solution.py:465
  (3 other events, 38.4 us)
